TPU v7x, 256 devices: a whole 4x4x8 slice. The times are simulated.
256 devices in a mesh: mem: 8 (over z), reg: 32 (over y, x, core).
Axes of the slice: x: 4, y: 4, z: 8, core: 2. Of those that a mesh axis runs over, the one named last changes fastest.
Arguments:
- background: bfloat16 [32, 32, 256, 640], P('reg', None, 'mem'), may hold values from -6 to 6
- obs_ensemble: bfloat16 [32, 32, 2048, 256], P('reg', 'mem'), may hold values from -180 to 180
- innovation: bfloat16 [32, 32, 2048], P('reg', 'mem'), may hold values from -8 to 8
- obs_precision: bfloat16 [32, 32, 2048], P('reg', 'mem'), may hold values from 0.25 to 4
- taper_weight: bfloat16 [32, 32, 5, 2048], P('reg', 'mem'), may hold values from 0.049804688 to 1
- obs_count: int32 [32, 32], P('reg', 'mem'), may hold values from 256 to 2048, as said below
Outputs:
- analysis: bfloat16 [32, 32, 256, 640], P('reg', None, 'mem')
Inputs may be any that keep to these rules, and one draw needn't show every extreme that they name: Slots 0 to obs_count - 1 of a patch hold its observations; in every draw some patch has all 2048 slots filled.
All inputs are finite; a program needn't handle non-finite values. Where the computation divides by a largest or mean magnitude, that divisor is 1e-20 or more.
Results may differ from a plain program's by a relative error of at most 0.0063.
Values may be sent and summed in bfloat16 or wider, within the bound.
No kernel may reach another device: no remote copies, remote signals or barrier semaphores. Data moves between devices by JAX's collectives and lax.ppermute only.
A program may use at most 128 MiB of HBM per device.

v0:
```python
import jax
import jax.numpy as jnp
from jax import lax
from jax.sharding import PartitionSpec as P

ITERS = 12


def padded(value, sides, width):
    for axis, dim in sides:
        peers, length = (lax.axis_size(axis), value.shape[dim])
        up = [(i, (i + 1) % peers) for i in range(peers)]
        down = [(j, i) for i, j in up]
        last = lax.slice_in_dim(value, length - width, length, axis=dim)
        leading = lax.slice_in_dim(value, 0, width, axis=dim)
        before = lax.ppermute(last, axis, up)
        after = lax.ppermute(leading, axis, down)
        value = jnp.concatenate([before, value, after], axis=dim)
    return value


def square_root_weights(gram, drive, members):
    ident = jnp.eye(members, dtype=jnp.float32)
    system = gram + float(members - 1) * ident
    bound = jnp.max(jnp.sum(jnp.abs(system), axis=2), axis=1)
    root = system / bound[:, None, None]
    inverse = jnp.broadcast_to(ident, system.shape)

    def sweep(step_index, carry):
        root, inverse = carry
        step = 1.5 * ident - 0.5 * jnp.einsum(
            "pij,pjk->pik", inverse, root, precision=lax.Precision.HIGHEST
        )
        root = jnp.einsum("pij,pjk->pik", root, step, precision=lax.Precision.HIGHEST)
        inverse = jnp.einsum("pij,pjk->pik", step, inverse, precision=lax.Precision.HIGHEST)
        return (root, inverse)

    root, inverse = lax.fori_loop(0, ITERS, sweep, (root, inverse))
    half = inverse / jnp.sqrt(bound)[:, None, None]
    inner = jnp.einsum("pkl,pl->pk", half, drive, precision=lax.Precision.HIGHEST)
    mean_weight = jnp.einsum("pkl,pl->pk", half, inner, precision=lax.Precision.HIGHEST)
    transform = jnp.sqrt(float(members - 1)) * half + mean_weight[:, :, None]
    return transform.astype(jnp.bfloat16)


def weighted_gram(block, weights, innov):
    scaled = (weights[:, :, None] * block).astype(jnp.bfloat16)
    gram = jnp.einsum("pok,pol->pkl", scaled, block, preferred_element_type=jnp.float32)
    drive = jnp.einsum("pok,po->pk", scaled, innov, preferred_element_type=jnp.float32)
    return (gram, drive)


def body(background, obs_ensemble, innovation, obs_precision, taper_weight, obs_count):
    members = obs_ensemble.shape[3]
    slots = obs_ensemble.shape[2]
    patches = obs_ensemble.shape[1]
    valid = jnp.arange(slots, dtype=jnp.int32)[None, None, :] < obs_count[:, :, None]
    precision_live = jnp.where(valid, obs_precision, jnp.zeros_like(obs_precision))
    side_data = jnp.concatenate(
        [innovation[:, :, None, :], precision_live[:, :, None, :], taper_weight], axis=2
    )
    padded_ens, padded_side = (
        padded(obs_ensemble, (("reg", 0), ("mem", 1)), 1),
        padded(side_data, (("reg", 0), ("mem", 1)), 1),
    )
    sources = ((1, 1, 0), (0, 1, 1), (2, 1, 2), (1, 0, 3), (1, 2, 4))
    gram = jnp.zeros((patches, members, members), jnp.float32)
    drive = jnp.zeros((patches, members), jnp.float32)
    for row_index, start, side_index in sources:
        block = padded_ens[row_index, start : start + patches]
        extra = padded_side[row_index, start : start + patches]
        weights = extra[:, 1].astype(jnp.float32) * extra[:, 2 + side_index].astype(jnp.float32)
        part_gram, part_drive = weighted_gram(block, weights, extra[:, 0])
        gram = gram + part_gram
        drive = drive + part_drive
    transform = square_root_weights(gram, drive, members)
    states = lax.all_to_all(background, "mem", split_axis=1, concat_axis=2, tiled=True)[0].astype(
        jnp.float32
    )
    mean_state = jnp.mean(states, axis=1, keepdims=True)
    perturbation = (states - mean_state).astype(jnp.bfloat16)
    result = mean_state + jnp.einsum(
        "pki,pkr->pir", transform, perturbation, preferred_element_type=jnp.float32
    )
    return lax.all_to_all(
        result.astype(jnp.bfloat16)[None], "mem", split_axis=2, concat_axis=1, tiled=True
    )


def solution(mesh):
    in_specs = (
        P("reg", None, "mem", None),
        P("reg", "mem", None, None),
        P("reg", "mem", None),
        P("reg", "mem", None),
        P("reg", "mem", None, None),
        P("reg", "mem"),
    )
    out_specs = P("reg", None, "mem", None)
    return jax.shard_map(body, mesh=mesh, in_specs=in_specs, out_specs=out_specs, check_vma=False)
```

profile of v0, /device:TPU:26, one launch (start us, length us, event | category | flops | bytes accessed | tf_op | source)
XLA Modules:
  0.0 254.6 jit_solution(7870426346370491818)
XLA Ops:
  3.6 6.3 %copy.62 = bf16[1,4,2048,256]{2,3,1,0:T(8,128)(2,1)} copy(bf16[1,4,2048,256]{3,2,1,0:T(8,128)(2,1)} %param.9) | data formatting | bytes 8388608 | tf_op args[1]
  9.9 1.7 collective-permute-start.3
  11.7 8.5 %all-to-all-start = ((bf16[1,32,32,640]{3,2,0,1:T(8,128)(2,1)}), bf16[1,32,32,640]{3,2,0,1:T(8,128)(2,1)S(1)}, u32[]{:S(2)}, u32[]{:S(2)}) async-start(bf16[1,32,32,640]{3,2,0,1:T(8,128)(2,1)} %bitcast), calls=%async_computation | async-start | bytes 2621440 | tf_op jit(solution)/shard_map/all_to_all | solution.py:77
  20.5 3.2 %fusion.4 = f32[4,1,256]{2,1,0:T(1,128)S(1)} fusion(bf16[1,4,2048,256]{3,2,1,0:T(8,128)(2,1)} %param.9, f32[4,2048]{1,0:T(4,128)S(1)} %multiply_bitcast_fusion.4, bf16[4,2048,1]{1,0,2:T(4,128)(2,1)S(1)} %slice_bitcast_fusion.4), kind=kOutput, calls=%fused_computation.11 | convolution fusion | flops 10485760 | bytes 4247552 | tf_op jit(solution)/shard_map/pok,po->pk/dot_general | solution.py:49
  23.8 4.1 %fusion.5 = f32[4,256,256]{1,2,0:T(8,128)} fusion(bf16[1,4,2048,256]{3,2,1,0:T(8,128)(2,1)S(1)} %copy-done.2, f32[4,2048]{1,0:T(4,128)S(1)} %multiply_bitcast_fusion.4), kind=kOutput, calls=%fused_computation.12 | convolution fusion | flops 1080033280 | bytes 5275648 | tf_op jit(solution)/shard_map/pok,pol->pkl/dot_general | solution.py:48
  28.4 2.1 collective-permute-start.4
  31.9 26.3 %collective-permute-done.1 = bf16[1,4,2048,256]{2,3,1,0:T(8,128)(2,1)} collective-permute-done((bf16[1,4,2048,256]{2,3,1,0:T(8,128)(2,1)}, bf16[1,4,2048,256]{2,3,1,0:T(8,128)(2,1)}, u32[]{:S(2)}, u32[]{:S(2)}) %collective-permute-start.1) | collective-permute-done | bytes 4194336 | tf_op jit(solution)/shard_map/ppermute | solution.py:16
  58.2 4.5 %pad_maximum_fusion.8 = (bf16[3,1,2048,256]{2,3,1,0:T(8,128)(2,1)}, bf16[3,1,2048,256]{2,3,1,0:T(8,128)(2,1)}) fusion(bf16[1,4,2048,256]{2,3,1,0:T(8,128)(2,1)} %collective-permute-done.3, bf16[1,4,2048,256]{2,3,1,0:T(8,128)(2,1)S(1)} %copy-done, bf16[1,4,2048,256]{2,3,1,0:T(8,128)(2,1)} %collective-permute-done.1), kind=kLoop, calls=%fused_computation.47 | loop fusion | flops 6291456 | bytes 18874368 | tf_op jit(solution)/shard_map/slice | solution.py:14
  62.6 1.9 collective-permute-start.5
  64.6 4.2 %collective-permute-start.7 = (bf16[3,1,2048,256]{2,3,1,0:T(8,128)(2,1)}, bf16[3,1,2048,256]{2,3,1,0:T(8,128)(2,1)}, u32[]{:S(2)}, u32[]{:S(2)}) collective-permute-start(bf16[3,1,2048,256]{2,3,1,0:T(8,128)(2,1)} %get-tuple-element.45), channel_id=1, source_target_pairs={{32,0},{64,32},{96,64},{128,96},{160,128},{192,160},{224,192},{0,2... | collective-permute-start | bytes 9437192 | tf_op jit(solution)/shard_map/ppermute | solution.py:17
  69.1 1.9 copy.70
  71.4 3.4 %fusion.6 = f32[4,1,256]{2,1,0:T(1,128)S(1)} fusion(bf16[1,4,2048,256]{2,3,1,0:T(8,128)(2,1)} %collective-permute-done.1, f32[4,2048]{1,0:T(4,128)S(1)} %multiply_bitcast_fusion.3, bf16[4,2048,1]{1,0,2:T(4,128)(2,1)S(1)} %slice_bitcast_fusion.3), kind=kOutput, calls=%fused_computation.13 | convolution fusion | flops 10485760 | bytes 4247552 | tf_op jit(solution)/shard_map/pok,po->pk/dot_general | solution.py:49
  74.8 3.5 %fusion.8 = f32[4,1,256]{2,1,0:T(1,128)S(1)} fusion(bf16[1,4,2048,256]{2,3,1,0:T(8,128)(2,1)} %collective-permute-done.3, f32[4,2048]{1,0:T(4,128)S(1)} %multiply_bitcast_fusion.2, bf16[4,2048,1]{1,0,2:T(4,128)(2,1)S(1)} %slice_bitcast_fusion.2), kind=kOutput, calls=%fused_computation.15 | convolution fusion | flops 10485760 | bytes 4247552 | tf_op jit(solution)/shard_map/pok,po->pk/dot_general | solution.py:49
  78.2 4.9 %fusion.39 = f32[4,256,256]{1,2,0:T(8,128)S(1)} fusion(f32[4,256,256]{1,2,0:T(8,128)S(1)} %copy-done.9, bf16[1,4,2048,256]{2,3,1,0:T(8,128)(2,1)} %collective-permute-done.1, f32[4,2048]{1,0:T(4,128)S(1)} %multiply_bitcast_fusion.3), kind=kOutput, calls=%fused_computation.53 | convolution fusion | flops 1080295424 | bytes 6324224 | tf_op jit(solution)/shard_map/pok,pol->pkl/dot_general | solution.py:48
  83.2 53.7 %collective-permute-done.5 = bf16[3,1,2048,256]{2,3,1,0:T(8,128)(2,1)} collective-permute-done((bf16[3,1,2048,256]{2,3,1,0:T(8,128)(2,1)}, bf16[3,1,2048,256]{2,3,1,0:T(8,128)(2,1)}, u32[]{:S(2)}, u32[]{:S(2)}) %collective-permute-start.5) | collective-permute-done | bytes 3145760 | tf_op jit(solution)/shard_map/ppermute | solution.py:16
  137.0 2.4 fusion.15
  144.0 5.0 %abs_reduce_fusion = (f32[4,256]{1,0:T(4,128)S(1)}, f32[4,256,256]{1,2,0:T(8,128)S(1)}) fusion(f32[256,256]{0,1:T(8,128)S(1)} %fusion.52, f32[4,256,256]{1,2,0:T(8,128)S(1)} %fusion.13, f32[4,256,256]{1,2,0:T(8,128)S(1)} %fusion.11, f32[4,256,256]{1,2,0:T(8,128)S(1)} %fusion.39, bf16[1,4,2048,256]{2,3,1,0:T(8,128)(2,1)} %collective-permute-done.3, ...), kind=kOutput, calls=%fused_computation.58 | convolution fusion | flops 1081605120 | bytes 8687616 | tf_op jit(solution)/shard_map/pok,pol->pkl/dot_general | solution.py:48
  149.4 53.8 %while.13 = (s32[]{:T(128)}, f32[4,256,256]{1,2,0:T(8,128)S(1)}, f32[4,256,256]{2,1,0:T(8,128)S(1)}, s32[]{:T(128)}) while((s32[]{:T(128)}, f32[4,256,256]{1,2,0:T(8,128)S(1)}, f32[4,256,256]{2,1,0:T(8,128)S(1)}, s32[]{:T(128)}) %tuple.28), condition=%wide.region_5.6_spmd.clone, body=%wide.region_4.5_spmd.clone.sunk | while | flops 2416574464 | bytes 14155829 | solution.py:38
  152.0 1.9 convolution_bitcast_fusion.2
  156.5 1.9 convolution_bitcast_fusion.2
  160.9 1.9 convolution_bitcast_fusion.2
  165.4 1.9 convolution_bitcast_fusion.2
  169.9 1.9 convolution_bitcast_fusion.2
  174.3 1.9 convolution_bitcast_fusion.2
  178.8 1.9 convolution_bitcast_fusion.2
  183.3 1.9 convolution_bitcast_fusion.2
  187.7 1.9 convolution_bitcast_fusion.2
  192.2 1.9 convolution_bitcast_fusion.2
  196.7 1.9 convolution_bitcast_fusion.2
  201.1 1.9 convolution_bitcast_fusion.2
  203.3 3.5 %fusion.10 = f32[4,1,256]{2,1,0:T(1,128)S(1)} fusion(bf16[4,2048,256]{1,2,0:T(8,128)(2,1)} %copy-done.5, f32[4,2048]{1,0:T(4,128)S(1)} %get-tuple-element.53, bf16[4,2048,1]{1,0,2:T(4,128)(2,1)S(1)} %get-tuple-element.55), kind=kOutput, calls=%fused_computation.17 | convolution fusion | flops 10485760 | bytes 4247552 | tf_op jit(solution)/shard_map/pok,po->pk/dot_general | solution.py:49
  212.0 41.4 %all_to_all.27 = bf16[1,4,256,640]{3,1,0,2:T(4,128)(2,1)S(1)} all-to-all(bf16[1,4,256,640]{3,1,0,2:T(4,128)(2,1)S(1)} %copy.72), channel_id=1, replica_groups=mesh['mem'=8,'reg'=32] {'mem'}, dimensions={2} | all-to-all | bytes 2621440 | tf_op jit(solution)/shard_map/all_to_all | solution.py:85
  (127 shorter events, 48.1 us)
Async XLA Ops:
  1.8 18.5 %copy-start.7 = (bf16[1,4,5,2048]{3,1,2,0:T(4,128)(2,1)S(1)}, bf16[1,4,5,2048]{3,1,2,0:T(4,128)(2,1)}, u32[]{:S(2)}) copy-start(bf16[1,4,5,2048]{3,1,2,0:T(4,128)(2,1)} %param.12) | copy-start | bytes 245764
  1.8 18.5 %copy-start.8 = (bf16[1,4,2048]{2,1,0:T(4,128)(2,1)S(1)}, bf16[1,4,2048]{2,1,0:T(4,128)(2,1)}, u32[]{:S(2)}) copy-start(bf16[1,4,2048]{2,1,0:T(4,128)(2,1)} %param.10) | copy-start | bytes 49156
  1.8 26.1 %collective-permute-start = (bf16[1,4,7,2048]{3,1,2,0:T(4,128)(2,1)S(1)}, bf16[1,4,7,2048]{3,1,2,0:T(4,128)(2,1)S(1)}, u32[]{:S(2)}, u32[]{:S(2)}) collective-permute-start(bf16[1,4,7,2048]{3,1,2,0:T(4,128)(2,1)S(1)} %pad_maximum_fusion.20), channel_id=1, source_target_pairs={{0,1},{1,2},{2,3},{3,4},{4,5},{5,6},{6,7},{7,8},{8,9},{9,10},{10,1... | collective-permute-start | bytes 344072 | tf_op jit(solution)/shard_map/ppermute | solution.py:16
  1.9 26.0 %collective-permute-start.2 = (bf16[1,4,7,2048]{3,1,2,0:T(4,128)(2,1)S(1)}, bf16[1,4,7,2048]{3,1,2,0:T(4,128)(2,1)S(1)}, u32[]{:S(2)}, u32[]{:S(2)}) collective-permute-start(bf16[1,4,7,2048]{3,1,2,0:T(4,128)(2,1)S(1)} %pad_maximum_fusion.20), channel_id=1, source_target_pairs={{1,0},{2,1},{3,2},{4,3},{5,4},{6,5},{7,6},{8,7},{9,8},{10,9},{11,1... | collective-permute-start | bytes 344072 | tf_op jit(solution)/shard_map/ppermute | solution.py:17
  9.9 48.2 %collective-permute-start.1 = (bf16[1,4,2048,256]{2,3,1,0:T(8,128)(2,1)}, bf16[1,4,2048,256]{2,3,1,0:T(8,128)(2,1)}, u32[]{:S(2)}, u32[]{:S(2)}) collective-permute-start(bf16[1,4,2048,256]{2,3,1,0:T(8,128)(2,1)} %copy.62), channel_id=1, source_target_pairs={{0,1},{1,2},{2,3},{3,4},{4,5},{5,6},{6,7},{7,8},{8,9},{9,10},{10,1... | collective-permute-start | bytes 12582920 | tf_op jit(solution)/shard_map/ppermute | solution.py:16
  9.9 48.2 %collective-permute-start.3 = (bf16[1,4,2048,256]{2,3,1,0:T(8,128)(2,1)}, bf16[1,4,2048,256]{2,3,1,0:T(8,128)(2,1)}, u32[]{:S(2)}, u32[]{:S(2)}) collective-permute-start(bf16[1,4,2048,256]{2,3,1,0:T(8,128)(2,1)} %copy.62), channel_id=1, source_target_pairs={{1,0},{2,1},{3,2},{4,3},{5,4},{6,5},{7,6},{8,7},{9,8},{10,9},{11,1... | collective-permute-start | bytes 12582920 | tf_op jit(solution)/shard_map/ppermute | solution.py:17
  11.7 57.4 %all-to-all-start = ((bf16[1,32,32,640]{3,2,0,1:T(8,128)(2,1)}), bf16[1,32,32,640]{3,2,0,1:T(8,128)(2,1)S(1)}, u32[]{:S(2)}, u32[]{:S(2)}) async-start(bf16[1,32,32,640]{3,2,0,1:T(8,128)(2,1)} %bitcast), calls=%async_computation | async-start | bytes 2621440 | tf_op jit(solution)/shard_map/all_to_all | solution.py:77
  20.3 3.5 %copy-start.2 = (bf16[1,4,2048,256]{3,2,1,0:T(8,128)(2,1)S(1)}, bf16[1,4,2048,256]{3,2,1,0:T(8,128)(2,1)}, u32[]{:S(2)}) copy-start(bf16[1,4,2048,256]{3,2,1,0:T(8,128)(2,1)} %param.9) | copy-start | bytes 12582916
  23.8 34.4 %copy-start = (bf16[1,4,2048,256]{2,3,1,0:T(8,128)(2,1)S(1)}, bf16[1,4,2048,256]{2,3,1,0:T(8,128)(2,1)}, u32[]{:S(2)}) copy-start(bf16[1,4,2048,256]{2,3,1,0:T(8,128)(2,1)} %copy.62) | copy-start | bytes 12582916
  28.4 40.3 %collective-permute-start.4 = (bf16[3,1,7,2048]{3,1,2,0:T(2,128)(2,1)S(1)}, bf16[3,1,7,2048]{3,1,2,0:T(2,128)(2,1)S(1)}, u32[]{:S(2)}, u32[]{:S(2)}) collective-permute-start(bf16[3,1,7,2048]{3,1,2,0:T(2,128)(2,1)S(1)} %get-tuple-element.48), channel_id=1, source_target_pairs={{0,32},{32,64},{64,96},{96,128},{128,160},{160,192},{192,224},{224... | collective-permute-start | bytes 258056 | tf_op jit(solution)/shard_map/ppermute | solution.py:16
  30.5 38.3 %collective-permute-start.6 = (bf16[3,1,7,2048]{3,1,2,0:T(2,128)(2,1)S(1)}, bf16[3,1,7,2048]{3,1,2,0:T(2,128)(2,1)S(1)}, u32[]{:S(2)}, u32[]{:S(2)}) collective-permute-start(bf16[3,1,7,2048]{3,1,2,0:T(2,128)(2,1)S(1)} %get-tuple-element.49), channel_id=1, source_target_pairs={{32,0},{64,32},{96,64},{128,96},{160,128},{192,160},{224,192},{0,2... | collective-permute-start | bytes 258056 | tf_op jit(solution)/shard_map/ppermute | solution.py:17
  62.6 74.2 %collective-permute-start.5 = (bf16[3,1,2048,256]{2,3,1,0:T(8,128)(2,1)}, bf16[3,1,2048,256]{2,3,1,0:T(8,128)(2,1)}, u32[]{:S(2)}, u32[]{:S(2)}) collective-permute-start(bf16[3,1,2048,256]{2,3,1,0:T(8,128)(2,1)} %get-tuple-element.44), channel_id=1, source_target_pairs={{0,32},{32,64},{64,96},{96,128},{128,160},{160,192},{192,224},{224... | collective-permute-start | bytes 9437192 | tf_op jit(solution)/shard_map/ppermute | solution.py:16
  64.6 72.4 %collective-permute-start.7 = (bf16[3,1,2048,256]{2,3,1,0:T(8,128)(2,1)}, bf16[3,1,2048,256]{2,3,1,0:T(8,128)(2,1)}, u32[]{:S(2)}, u32[]{:S(2)}) collective-permute-start(bf16[3,1,2048,256]{2,3,1,0:T(8,128)(2,1)} %get-tuple-element.45), channel_id=1, source_target_pairs={{32,0},{64,32},{96,64},{128,96},{160,128},{192,160},{224,192},{0,2... | collective-permute-start | bytes 9437192 | tf_op jit(solution)/shard_map/ppermute | solution.py:17
  74.8 3.5 %copy-start.9 = (f32[4,256,256]{1,2,0:T(8,128)S(1)}, f32[4,256,256]{1,2,0:T(8,128)}, u32[]{:S(2)}) copy-start(f32[4,256,256]{1,2,0:T(8,128)} %fusion.5) | copy-start | bytes 3145732
  78.2 58.8 %copy-start.1 = (bf16[1,4,2048,256]{2,3,1,0:T(8,128)(2,1)S(1)}, bf16[1,4,2048,256]{2,3,1,0:T(8,128)(2,1)}, u32[]{:S(2)}) copy-start(bf16[1,4,2048,256]{2,3,1,0:T(8,128)(2,1)} %copy.62) | copy-start | bytes 12582916
  139.4 2.0 copy-start.5
  139.5 3.3 %copy-start.3 = (bf16[4,2048,256]{1,2,0:T(8,128)(2,1)}, bf16[4,2048,256]{1,2,0:T(8,128)(2,1)S(1)}, u32[]{:S(2)}) copy-start(bf16[4,2048,256]{1,2,0:T(8,128)(2,1)S(1)} %get-tuple-element.43) | copy-start | bytes 12582916
  203.3 3.5 %copy-start.4 = (bf16[4,2048,256]{1,2,0:T(8,128)(2,1)S(1)}, bf16[4,2048,256]{1,2,0:T(8,128)(2,1)}, u32[]{:S(2)}) copy-start(bf16[4,2048,256]{1,2,0:T(8,128)(2,1)} %copy-done.3) | copy-start | bytes 12582916
  208.0 2.2 copy-start.6
where the time goes:
time: 255 us
  matrix products  85.2 us (33%)
  waiting for transfers between devices  80.1 us (31%)
  blocking collectives  41.4 us (16%)
  starting transfers between devices  21.5 us (8%)
  local copies, waits for them, and re-layouts  14.9 us (6%)
  other arithmetic  10.3 us (4%)
    ppermute x4, waiting for transfers between devices, padded(): before = lax.ppermute(last, axis, up)  80 us
    all_to_all x1, blocking collectives, body(): lax.all_to_all(result.astype(jnp.bfloat16)[None], 'mem', split_axis=2, co...  41.4 us
    dot_general x12, matrix products, sweep(): jnp.einsum('pij,pjk->pik', root, step, precision=lax.Precision.HIGHEST)  22.8 us
    dot_general x5, matrix products, weighted_gram(): jnp.einsum('pok,pol->pkl', scaled, block, preferred_element_type=jnp.floa...  16.6 us
    dot_general x5, matrix products, weighted_gram(): jnp.einsum('pok,po->pk', scaled, innov, preferred_element_type=jnp.float32)  14.8 us
    dot_general x12, matrix products, sweep(): jnp.einsum('pij,pjk->pik', inverse, root, precision=lax.Precision.HIGHEST)  14.3 us
    dot_general x12, matrix products, sweep(): jnp.einsum('pij,pjk->pik', step, inverse, precision=lax.Precision.HIGHEST)  13.7 us
    ppermute x4, starting transfers between devices, padded(): after = lax.ppermute(leading, axis, down)  8.97 us
  transfers between devices with their start and end apart: 9, of which 3 were waited for; matrix products, arithmetic and copies ran while one was open for 13% of the time, Pallas kernels for 0%

commit v1 on v0

v1 whole, which is shorter than its diff:
```python
import jax
import jax.numpy as jnp
from jax import lax
from jax.experimental import pallas as pl
from jax.experimental.pallas import tpu as pltpu
from jax.sharding import PartitionSpec as P

F32 = jnp.float32
BF16 = jnp.bfloat16
ITERS = 12
PATCHES = 4
K = 256
SLOTS = 2048
CHUNK = 512
PEERS = 8
EXT = K + 8
VMEM = pl.BlockSpec(memory_space=pltpu.VMEM)
SMEM = pl.BlockSpec(memory_space=pltpu.SMEM)
PARAMS = pltpu.CompilerParams(vmem_limit_bytes=56 << 20)


def dot(a, b):
    return jnp.dot(a, b, preferred_element_type=F32)


def split(x):
    high = x.astype(BF16)
    return high, (x - high.astype(F32)).astype(BF16)


def dot_split(a, b):
    return dot(a[0], b[0]) + (dot(a[0], b[1]) + dot(a[1], b[0]))


def pick_row(ref, p):
    patch = lax.broadcasted_iota(jnp.int32, (PATCHES, SLOTS), 0)
    return jnp.sum(jnp.where(patch == p, ref[0].astype(F32), 0.0), axis=0, keepdims=True)


def slot_weights(p, count_ref, prec_ref, taper_ref):
    slot = lax.broadcasted_iota(jnp.int32, (1, SLOTS), 1)
    prec = jnp.where(slot < count_ref[p], pick_row(prec_ref, p), 0.0)
    return prec * taper_ref[0, p].astype(F32)


def weighted_grams(ens_ref, weights, innov, sides, add):
    rows = jnp.concatenate([weights[d : d + 1] for d in sides], axis=0)
    driven = split(rows * innov)
    for c in range(SLOTS // CHUNK):
        part = slice(c * CHUNK, (c + 1) * CHUNK)
        ens = ens_ref[0, 0, part, :]
        flipped = ens.T.astype(F32)
        drives = dot(driven[0][:, part], ens) + dot(driven[1][:, part], ens)
        for i, d in enumerate(sides):
            scaled = (flipped * weights[d : d + 1, part]).astype(BF16)
            add(c, d, dot(scaled, ens), drives[i : i + 1])


def sent_kernel(count_ref, ens_ref, innov_ref, prec_ref, taper_ref, above_ref, below_ref, next_ref, prev_ref):
    p = pl.program_id(0)
    weights = slot_weights(p, count_ref, prec_ref, taper_ref)
    innov = pick_row(innov_ref, p)

    def adder(targets):
        def add(c, d, gram, drive):
            ref = targets[d]
            if c == 0:
                ref[0, 0:K, :] = gram
                ref[0, K : K + 1, :] = drive
                ref[0, K + 1 : EXT, :] = jnp.zeros((EXT - K - 1, K), F32)
            else:
                ref[0, 0:K, :] += gram
                ref[0, K : K + 1, :] += drive

        return add

    @pl.when(p == 0)
    def _():
        weighted_grams(ens_ref, weights, innov, (1, 2, 4), adder({1: above_ref, 2: below_ref, 4: prev_ref}))

    @pl.when((p > 0) & (p < PATCHES - 1))
    def _():
        weighted_grams(ens_ref, weights, innov, (1, 2), adder({1: above_ref, 2: below_ref}))

    @pl.when(p == PATCHES - 1)
    def _():
        weighted_grams(ens_ref, weights, innov, (1, 2, 3), adder({1: above_ref, 2: below_ref, 3: next_ref}))


def kept_kernel(count_ref, ens_ref, innov_ref, prec_ref, taper_ref, own_ref):
    p = pl.program_id(0)
    weights = slot_weights(p, count_ref, prec_ref, taper_ref)
    innov = pick_row(innov_ref, p)

    @pl.when(p == 0)
    def _():
        own_ref[...] = jnp.zeros_like(own_ref)

    shift = {0: 0, 3: 1, 4: -1}

    def add(c, d, gram, drive):
        to = p + shift[d]
        own_ref[to, 0:K, :] += gram
        own_ref[to, K : K + 1, :] += drive

    @pl.when(p == 0)
    def _():
        weighted_grams(ens_ref, weights, innov, (0, 3), add)

    @pl.when((p > 0) & (p < PATCHES - 1))
    def _():
        weighted_grams(ens_ref, weights, innov, (0, 3, 4), add)

    @pl.when(p == PATCHES - 1)
    def _():
        weighted_grams(ens_ref, weights, innov, (0, 4), add)


def gram_specs():
    return [
        SMEM,
        pl.BlockSpec((1, 1, SLOTS, K), lambda p: (0, p, 0, 0)),
        pl.BlockSpec((1, PATCHES, SLOTS), lambda p: (0, 0, 0)),
        pl.BlockSpec((1, PATCHES, SLOTS), lambda p: (0, 0, 0)),
        pl.BlockSpec((1, PATCHES, 5, SLOTS), lambda p: (0, 0, 0, 0)),
    ]


def cost(grams):
    return pl.CostEstimate(flops=grams * 2 * K * K * SLOTS, bytes_accessed=PATCHES * SLOTS * K * 2, transcendentals=0)


def sent_grams(*args):
    full = jax.ShapeDtypeStruct((PATCHES, EXT, K), F32)
    one = jax.ShapeDtypeStruct((1, EXT, K), F32)
    return pl.pallas_call(
        sent_kernel,
        grid=(PATCHES,),
        in_specs=gram_specs(),
        out_specs=[pl.BlockSpec((1, EXT, K), lambda p: (p, 0, 0))] * 2 + [pl.BlockSpec((1, EXT, K), lambda p: (0, 0, 0))] * 2,
        out_shape=[full, full, one, one],
        compiler_params=PARAMS,
        cost_estimate=cost(10),
        name="sent_grams",
    )(*args)


def kept_grams(*args):
    return pl.pallas_call(
        kept_kernel,
        grid=(PATCHES,),
        in_specs=gram_specs(),
        out_specs=pl.BlockSpec((PATCHES, EXT, K), lambda p: (0, 0, 0)),
        out_shape=jax.ShapeDtypeStruct((PATCHES, EXT, K), F32),
        compiler_params=PARAMS,
        cost_estimate=cost(10),
        name="kept_grams",
    )(*args)


def root_kernel(own_ref, above_ref, below_ref, next_ref, prev_ref, out_ref, y_ref, z_ref, bound_ref):
    row = lax.broadcasted_iota(jnp.int32, (K, K), 0)
    col = lax.broadcasted_iota(jnp.int32, (K, K), 1)
    ident = jnp.where(row == col, 1.0, 0.0).astype(F32)

    def total(p, part):
        value = own_ref[p, part, :] + above_ref[p, part, :] + below_ref[p, part, :]
        if p == 0:
            value = value + next_ref[0, part, :]
        if p == PATCHES - 1:
            value = value + prev_ref[0, part, :]
        return value

    for p in range(PATCHES):
        system = total(p, slice(0, K)) + float(K - 1) * ident
        sums = jnp.sum(jnp.abs(system), axis=0, keepdims=True)
        bound = jnp.max(sums, axis=1, keepdims=True)
        bound_ref[p] = jnp.broadcast_to(bound, (8, 128))
        root = system / bound
        step = 1.5 * ident - 0.5 * root
        y_ref[p] = dot_split(split(root), split(step))
        z_ref[p] = step

    def sweep(index, carry):
        for p in range(PATCHES):
            y = split(y_ref[p])
            z = split(z_ref[p])
            step = split(1.5 * ident - 0.5 * dot_split(z, y))
            y_ref[p] = dot_split(y, step)
            z_ref[p] = dot_split(step, z)
        return carry

    lax.fori_loop(0, ITERS - 1, sweep, 0)
    for p in range(PATCHES):
        half = z_ref[p] / jnp.sqrt(bound_ref[p, 0:1, 0:1])
        drive = total(p, slice(K, K + 1))
        inner = jnp.sum(half * drive, axis=1, keepdims=True)
        mean_weight = jnp.sum(half * inner, axis=0, keepdims=True)
        out_ref[p] = (jnp.sqrt(float(K - 1)) * half + mean_weight).astype(BF16)


def root_weights(*args):
    return pl.pallas_call(
        root_kernel,
        in_specs=[VMEM] * 5,
        out_specs=VMEM,
        out_shape=jax.ShapeDtypeStruct((PATCHES, K, K), BF16),
        scratch_shapes=[
            pltpu.VMEM((PATCHES, K, K), F32),
            pltpu.VMEM((PATCHES, K, K), F32),
            pltpu.VMEM((PATCHES, 8, 128), F32),
        ],
        compiler_params=PARAMS,
        cost_estimate=pl.CostEstimate(flops=PATCHES * 99 * 2 * K**3, bytes_accessed=4 << 20, transcendentals=0),
        name="root_weights",
    )(*args)


def apply_kernel(flipped_ref, states_ref, out_ref):
    rows = states_ref.shape[3]
    states = states_ref[:, 0].reshape(K, rows).astype(F32)
    mean = jnp.sum(states, axis=0, keepdims=True) * (1.0 / K)
    pert = (states - mean).astype(BF16)
    result = mean + dot(flipped_ref[0], pert)
    out_ref[:, 0] = result.astype(BF16).reshape(PEERS, K // PEERS, rows)


def apply_weights(flipped, states):
    rows = states.shape[3]
    block = pl.BlockSpec((PEERS, 1, K // PEERS, rows), lambda p: (0, p, 0, 0))
    return pl.pallas_call(
        apply_kernel,
        grid=(PATCHES,),
        in_specs=[pl.BlockSpec((1, K, K), lambda p: (p, 0, 0)), block],
        out_specs=block,
        out_shape=jax.ShapeDtypeStruct(states.shape, BF16),
        compiler_params=PARAMS,
        cost_estimate=pl.CostEstimate(flops=PATCHES * 2 * K * K * rows, bytes_accessed=4 << 20, transcendentals=0),
        name="apply_weights",
    )(flipped, states)


def swap(value):
    return lax.all_to_all(value, "mem", split_axis=0, concat_axis=0, tiled=True)


def shift(value, axis, by):
    peers = lax.axis_size(axis)
    return lax.ppermute(value, axis, [(i, (i + by) % peers) for i in range(peers)])


def body(background, obs_ensemble, innovation, obs_precision, taper_weight, obs_count):
    rows = background.shape[3]
    states = swap(background.reshape(PEERS, PATCHES, K // PEERS, rows))
    obs = (obs_count.reshape(PATCHES), obs_ensemble, innovation, obs_precision, taper_weight)
    above, below, following, previous = sent_grams(*obs)
    above = shift(above, "reg", 1)
    below = shift(below, "reg", -1)
    following = shift(following, "mem", 1)
    previous = shift(previous, "mem", -1)
    own = kept_grams(*obs)
    flipped = root_weights(own, above, below, following, previous)
    analysis = swap(apply_weights(flipped, states))
    return analysis.reshape(1, PEERS * PATCHES, K // PEERS, rows)


def solution(mesh):
    in_specs = (
        P("reg", None, "mem", None),
        P("reg", "mem", None, None),
        P("reg", "mem", None),
        P("reg", "mem", None),
        P("reg", "mem", None, None),
        P("reg", "mem"),
    )
    out_specs = P("reg", None, "mem", None)
    return jax.shard_map(body, mesh=mesh, in_specs=in_specs, out_specs=out_specs, check_vma=False)
```

time: 255 us -> 135 us (0.53)
  matrix products: 85.2 us -> 0 us
  waiting for transfers between devices: 80.1 us -> 26.8 us
  Pallas kernels: 0 us -> 48.7 us
  other arithmetic: 10.3 us -> 0 us
  local copies, waits for them, and re-layouts: 14.9 us -> 5.85 us
  starting transfers between devices: 21.5 us -> 13.5 us
    dot_general x49 -> x0, matrix products: 85.2 us -> none  [the longest x12 22.8 us: sweep(): jnp.einsum('pij,pjk->pik', root, step, precision=lax.Precision.HIGHEST)]
    ppermute x8 -> x4, waiting for transfers between devices: 80.1 us -> 26.8 us  [shift(): lax.ppermute(value, axis, [(i, (i + by) % peers) for i in range(peers)])]
    pallas_call x0 -> x4, Pallas kernels: none -> 48.7 us  [the longest x1 29.3 us: root_weights(): pl.pallas_call(root_kernel, in_specs=[VMEM] * 5, out_specs=VMEM, out_shap...]
    ppermute x8 -> x4, starting transfers between devices: 13.1 us -> 5.08 us  [shift(): lax.ppermute(value, axis, [(i, (i + by) % peers) for i in range(peers)])]
    slice x1 -> x0, other arithmetic: 4.47 us -> none  [padded(): last = lax.slice_in_dim(value, length - width, length, axis=dim)]
    squeeze x3 -> x0, other arithmetic: 2.79 us -> none  [the longest x1 2.45 us: body(): block = padded_ens[row_index, start:start + patches]]
    unnamed x21 -> x12, local copies, waits for them, and re-layouts: 8.45 us -> 5.85 us
  transfers between devices with their start and end apart: 9 -> 5, of which waited for: 3 -> 1; matrix products, arithmetic and copies ran while one was open for 13% -> 0% of each run, Pallas kernels for 0% -> 27%
where the time goes in v1:
time: 135 us; the launch traced here: 134 us
  Pallas kernels  48.7 us (36%)
  blocking collectives  39.2 us (29%)
  waiting for transfers between devices  26.8 us (20%)
  starting transfers between devices  13.5 us (10%)
  local copies, waits for them, and re-layouts  5.85 us (4%)
    all_to_all x1, blocking collectives, swap(): return lax.all_to_all(value, 'mem', split_axis=0, concat_axis=0, tiled=True)  39.2 us
    pallas_call x1, Pallas kernels, root_weights(): pl.pallas_call(root_kernel, in_specs=[VMEM] * 5, out_specs=VMEM, out_shap...  29.3 us
    ppermute x4, waiting for transfers between devices, shift(): lax.ppermute(value, axis, [(i, (i + by) % peers) for i in range(peers)])  26.8 us
    all_to_all x1, starting transfers between devices, swap(): return lax.all_to_all(value, 'mem', split_axis=0, concat_axis=0, tiled=True)  8.46 us
    pallas_call x1, Pallas kernels, sent_grams(): pl.pallas_call(sent_kernel, grid=(PATCHES,), in_specs=gram_specs(), out_s...  7.67 us
    pallas_call x1, Pallas kernels, kept_grams(): pl.pallas_call(kept_kernel, grid=(PATCHES,), in_specs=gram_specs(), out_s...  7.45 us
    unnamed x12, local copies, waits for them, and re-layouts  5.85 us
    ppermute x4, starting transfers between devices, shift(): lax.ppermute(value, axis, [(i, (i + by) % peers) for i in range(peers)])  5.08 us
  transfers between devices with their start and end apart: 5, of which 1 were waited for; matrix products, arithmetic and copies ran while one was open for 0% of the time, Pallas kernels for 27%

profile of v1, /device:TPU:26, one launch (start us, length us, event | category | flops | bytes accessed | tf_op | source)
XLA Modules:
  0.0 134.2 jit_solution(16484535591446188383)
XLA Ops:
  0.0 1.6 %copy.7.taper_ref = bf16[1,4,5,2048]{3,2,1,0:T(8,128)(2,1)} copy(bf16[1,4,5,2048]{3,1,2,0:T(4,128)(2,1)} %param.10) | data formatting | bytes 163840 | tf_op args[4]
  1.6 7.7 %sent_grams.1 = (f32[4,264,256]{2,1,0:T(8,128)}, f32[4,264,256]{2,1,0:T(8,128)}, f32[1,264,256]{2,1,0:T(8,128)}, f32[1,264,256]{2,1,0:T(8,128)}) custom-call(s32[4]{0:T(128)} %bitcast.4, bf16[1,4,2048,256]{3,2,1,0:T(8,128)(2,1)} %ens_ref.3, bf16[1,4,2048]{2,1,0:T(4,128)(2,1)} %innov_ref.3, bf16[1,4,2048]{2,1,0:T(4,128)(2,1)} %prec_ref.3, ...), custom_call_target="tpu_custom_call" | custom-call | flops 2684354560 | bytes 4194304 | tf_op jit(solution)/shard_map/sent_grams/pallas_call | solution.py:136
  9.3 0.1 collective-permute-start
  9.4 1.7 %collective-permute-start.1 = (f32[4,264,256]{2,1,0:T(8,128)}, f32[4,264,256]{2,1,0:T(8,128)S(1)}, u32[]{:S(2)}, u32[]{:S(2)}) collective-permute-start(f32[4,264,256]{2,1,0:T(8,128)} %get-tuple-element.10), channel_id=1, source_target_pairs={{0,31},{1,0},{2,1},{3,2},{4,3},{5,4},{6,5},{7,6},{8,7},{9,8},{10,9... | collective-permute-start | bytes 3244040 | tf_op jit(solution)/shard_map/ppermute | solution.py:249
  11.1 8.5 %all-to-all-start = ((bf16[8,4,32,640]{3,2,1,0:T(8,128)(2,1)}), bf16[8,4,32,640]{3,2,1,0:T(8,128)(2,1)S(1)}, u32[]{:S(2)}, u32[]{:S(2)}) async-start(bf16[8,4,32,640]{3,2,1,0:T(8,128)(2,1)} %bitcast.1), calls=%async_computation | async-start | bytes 2621440 | tf_op jit(solution)/shard_map/all_to_all | solution.py:244
  19.5 2.0 %collective-permute-start.2 = (f32[1,264,256]{2,1,0:T(8,128)}, f32[1,264,256]{2,1,0:T(8,128)S(1)}, u32[]{:S(2)}, u32[]{:S(2)}) collective-permute-start(f32[1,264,256]{2,1,0:T(8,128)} %get-tuple-element.11), channel_id=1, source_target_pairs={{0,32},{32,64},{64,96},{96,128},{128,160},{160,192},{192,224},{224... | collective-permute-start | bytes 811016 | tf_op jit(solution)/shard_map/ppermute | solution.py:249
  21.6 1.2 collective-permute-start.3
  22.8 7.4 %kept_grams.1.own_ref = f32[4,264,256]{2,1,0:T(8,128)} custom-call(s32[4]{0:T(128)} %bitcast.5, bf16[1,4,2048,256]{3,2,1,0:T(8,128)(2,1)} %ens_ref.3, bf16[1,4,2048]{2,1,0:T(4,128)(2,1)} %innov_ref.3, bf16[1,4,2048]{2,1,0:T(4,128)(2,1)} %prec_ref.3, bf16[1,4,5,2048]{3,2,1,0:T(8,128)(2,1)} %copy.7.taper_ref), custom_call_target="tpu_custom_call" | custom-call | flops 2684354560 | bytes 4194304 | tf_op jit(solution)/shard_map/kept_grams/pallas_call | solution.py:149
  30.3 26.8 %collective-permute-done.2.next_ref = f32[1,264,256]{2,1,0:T(8,128)S(1)} collective-permute-done((f32[1,264,256]{2,1,0:T(8,128)}, f32[1,264,256]{2,1,0:T(8,128)S(1)}, u32[]{:S(2)}, u32[]{:S(2)}) %collective-permute-start.2) | collective-permute-done | bytes 270368 | tf_op jit(solution)/shard_map/ppermute | solution.py:249
  57.0 0.0 copy-start.3
  57.0 0.0 collective-permute-done.3.prev_ref
  57.0 0.0 copy-start.4
  57.0 0.0 collective-permute-done.above_ref
  57.1 0.0 copy-start.1
  57.1 0.0 collective-permute-done.1.below_ref
  57.1 0.7 copy-done.3
  57.8 0.1 copy-done.4
  57.9 0.4 copy-done.1
  58.2 0.0 copy-start.2
  58.2 1.0 copy-done.2
  59.2 29.3 %root_weights.1.flipped_ref = bf16[4,256,256]{2,1,0:T(8,128)(2,1)} custom-call(f32[4,264,256]{2,1,0:T(8,128)} %kept_grams.1.own_ref, f32[4,264,256]{2,1,0:T(8,128)} %copy-done.1, f32[4,264,256]{2,1,0:T(8,128)} %copy-done.2, f32[1,264,256]{2,1,0:T(8,128)} %copy-done.3, f32[1,264,256]{2,1,0:T(8,128)} %copy-done.4), custom_call_target="tpu_custom_call" | custom-call | flops 13287555072 | bytes 4194304 | tf_op jit(solution)/shard_map/root_weights/pallas_call | solution.py:203
  88.6 0.0 all-to-all-done.states_ref
  88.6 0.0 copy-start
  88.6 1.1 copy-done
  89.6 4.3 %apply_weights.1 = bf16[8,4,32,640]{3,2,1,0:T(8,128)(2,1)} custom-call(bf16[4,256,256]{2,1,0:T(8,128)(2,1)} %root_weights.1.flipped_ref, bf16[8,4,32,640]{3,2,1,0:T(8,128)(2,1)} %copy-done), custom_call_target="tpu_custom_call" | custom-call | flops 335544320 | bytes 4194304 | tf_op jit(solution)/shard_map/apply_weights/pallas_call | solution.py:231
  93.9 39.2 %all_to_all.10 = bf16[8,4,32,640]{3,2,1,0:T(8,128)(2,1)S(1)} all-to-all(bf16[8,4,32,640]{3,2,1,0:T(8,128)(2,1)} %apply_weights.1), channel_id=1, replica_groups=mesh['mem'=8,'reg'=32] {'mem'}, dimensions={0} | all-to-all | bytes 2621440 | tf_op jit(solution)/shard_map/all_to_all | solution.py:244
  133.1 1.1 copy.10
Async XLA Ops:
  9.3 47.8 %collective-permute-start = (f32[4,264,256]{2,1,0:T(8,128)}, f32[4,264,256]{2,1,0:T(8,128)S(1)}, u32[]{:S(2)}, u32[]{:S(2)}) collective-permute-start(f32[4,264,256]{2,1,0:T(8,128)} %get-tuple-element.9), channel_id=1, source_target_pairs={{0,1},{1,2},{2,3},{3,4},{4,5},{5,6},{6,7},{7,8},{8,9},{9,10},{10,1... | collective-permute-start | bytes 3244040 | tf_op jit(solution)/shard_map/ppermute | solution.py:249
  9.4 47.7 %collective-permute-start.1 = (f32[4,264,256]{2,1,0:T(8,128)}, f32[4,264,256]{2,1,0:T(8,128)S(1)}, u32[]{:S(2)}, u32[]{:S(2)}) collective-permute-start(f32[4,264,256]{2,1,0:T(8,128)} %get-tuple-element.10), channel_id=1, source_target_pairs={{0,31},{1,0},{2,1},{3,2},{4,3},{5,4},{6,5},{7,6},{8,7},{9,8},{10,9... | collective-permute-start | bytes 3244040 | tf_op jit(solution)/shard_map/ppermute | solution.py:249
  11.1 77.5 %all-to-all-start = ((bf16[8,4,32,640]{3,2,1,0:T(8,128)(2,1)}), bf16[8,4,32,640]{3,2,1,0:T(8,128)(2,1)S(1)}, u32[]{:S(2)}, u32[]{:S(2)}) async-start(bf16[8,4,32,640]{3,2,1,0:T(8,128)(2,1)} %bitcast.1), calls=%async_computation | async-start | bytes 2621440 | tf_op jit(solution)/shard_map/all_to_all | solution.py:244
  19.5 37.5 %collective-permute-start.2 = (f32[1,264,256]{2,1,0:T(8,128)}, f32[1,264,256]{2,1,0:T(8,128)S(1)}, u32[]{:S(2)}, u32[]{:S(2)}) collective-permute-start(f32[1,264,256]{2,1,0:T(8,128)} %get-tuple-element.11), channel_id=1, source_target_pairs={{0,32},{32,64},{64,96},{96,128},{128,160},{160,192},{192,224},{224... | collective-permute-start | bytes 811016 | tf_op jit(solution)/shard_map/ppermute | solution.py:249
  21.6 35.5 %collective-permute-start.3 = (f32[1,264,256]{2,1,0:T(8,128)}, f32[1,264,256]{2,1,0:T(8,128)S(1)}, u32[]{:S(2)}, u32[]{:S(2)}) collective-permute-start(f32[1,264,256]{2,1,0:T(8,128)} %get-tuple-element.12), channel_id=1, source_target_pairs={{0,224},{32,0},{64,32},{96,64},{128,96},{160,128},{192,160},{224,1... | collective-permute-start | bytes 811016 | tf_op jit(solution)/shard_map/ppermute | solution.py:249
  57.0 0.7 copy-start.3
  57.0 0.8 copy-start.4
  57.1 1.2 copy-start.1
  58.2 1.0 copy-start.2
  88.6 1.1 copy-start

commit v2 on v1

v2 whole, which is shorter than its diff:
```python
import functools
import jax
import jax.numpy as jnp
from jax import lax
from jax.experimental import pallas as pl
from jax.experimental.pallas import tpu as pltpu
from jax.sharding import PartitionSpec as P

F32 = jnp.float32
BF16 = jnp.bfloat16
ITERS = 12
ROOT_COST = 2 * 10**9
PATCHES = 4
SIDES = 5
K = 256
SLOTS = 2048
PEERS = 8
EXT = K + 8
VMEM = pl.BlockSpec(memory_space=pltpu.VMEM)
SMEM = pl.BlockSpec(memory_space=pltpu.SMEM)
ANY = pl.BlockSpec(memory_space=pl.ANY)
PARAMS = pltpu.CompilerParams(vmem_limit_bytes=24 << 20)
SMALL = pltpu.CompilerParams(vmem_limit_bytes=16 << 20)
COST = pl.CostEstimate(flops=1000, bytes_accessed=1000, transcendentals=0)


def dot(a, b):
    return jnp.dot(a, b, preferred_element_type=F32)


def split(x):
    high = x.astype(BF16)
    return high, (x - high.astype(F32)).astype(BF16)


def start_all(copies):
    for copy in copies:
        copy.start()


def pick_row(value, p):
    patch = lax.broadcasted_iota(jnp.int32, (PATCHES, SLOTS), 0)
    return jnp.sum(jnp.where(patch == p, value.astype(F32), 0.0), axis=0, keepdims=True)


def slot_weights(p, count_ref, prec_ref, taper_ref):
    slot = lax.broadcasted_iota(jnp.int32, (1, SLOTS), 1)
    prec = jnp.where(slot < count_ref[p], pick_row(prec_ref[0], p), 0.0)
    return [prec * pick_row(taper_ref[0, d], p) for d in range(SIDES)]


def weighted_grams(ens_ref, flipped_ref, rows, innov):
    flipped_ref[...] = ens_ref[0, 0].T
    driven = jnp.concatenate([row * innov for row in rows] + [jnp.zeros((8 - len(rows), SLOTS), F32)], axis=0)
    scaled = [(flipped_ref[...].astype(F32) * row).astype(BF16) for row in rows]
    both = dot(jnp.concatenate(scaled + list(split(driven)), axis=0), ens_ref[0, 0])
    n = len(rows) * K
    drives = both[n : n + 8] + both[n + 8 : n + 16]
    return [(both[i * K : (i + 1) * K], drives[i : i + 1]) for i in range(len(rows))]


def sent_kernel(count_ref, ens_ref, innov_ref, prec_ref, taper_ref, near_ref, far_ref, next_ref, prev_ref, flipped_ref):
    p = pl.program_id(0)
    even = lax.rem(lax.axis_index("reg"), 2) == 0
    weights = slot_weights(p, count_ref, prec_ref, taper_ref)
    sided = [jnp.where(even, weights[1], weights[2]), jnp.where(even, weights[2], weights[1])]
    innov = pick_row(innov_ref[0], p)

    def store(rows, refs):
        for (gram, drive), ref in zip(weighted_grams(ens_ref, flipped_ref, rows, innov), refs):
            ref[0, 0:K, :] = gram
            ref[0, K:EXT, :] = jnp.broadcast_to(drive, (EXT - K, K))

    @pl.when(p == 0)
    def _():
        store(sided + [weights[4]], (near_ref, far_ref, prev_ref))

    @pl.when((p > 0) & (p < PATCHES - 1))
    def _():
        store(sided, (near_ref, far_ref))

    @pl.when(p == PATCHES - 1)
    def _():
        store(sided + [weights[3]], (near_ref, far_ref, next_ref))


def kept_kernel(count_ref, ens_ref, innov_ref, prec_ref, taper_ref, own_ref, flipped_ref):
    p = pl.program_id(0)
    weights = slot_weights(p, count_ref, prec_ref, taper_ref)
    innov = pick_row(innov_ref[0], p)

    @pl.when(p == 0)
    def _():
        own_ref[...] = jnp.zeros_like(own_ref)

    def add(sides):
        pairs = weighted_grams(ens_ref, flipped_ref, [weights[d] for d in sides], innov)
        for d, (gram, drive) in zip(sides, pairs):
            to = p + {0: 0, 3: 1, 4: -1}[d]
            own_ref[to, 0:K, :] += gram
            own_ref[to, K : K + 1, :] += drive

    @pl.when(p == 0)
    def _():
        add((0, 3))

    @pl.when((p > 0) & (p < PATCHES - 1))
    def _():
        add((0, 3, 4))

    @pl.when(p == PATCHES - 1)
    def _():
        add((0, 4))


def gram_specs():
    return [
        SMEM,
        pl.BlockSpec((1, 1, SLOTS, K), lambda p: (0, p, 0, 0)),
        pl.BlockSpec((1, PATCHES, SLOTS), lambda p: (0, 0, 0)),
        pl.BlockSpec((1, PATCHES, SLOTS), lambda p: (0, 0, 0)),
        pl.BlockSpec((1, SIDES, PATCHES, SLOTS), lambda p: (0, 0, 0, 0)),
    ]


def sent_grams(*args):
    full = jax.ShapeDtypeStruct((PATCHES, EXT, K), F32)
    one = jax.ShapeDtypeStruct((1, EXT, K), F32)
    return pl.pallas_call(
        sent_kernel,
        grid=(PATCHES,),
        in_specs=gram_specs(),
        out_specs=[pl.BlockSpec((1, EXT, K), lambda p: (p, 0, 0))] * 2 + [pl.BlockSpec((1, EXT, K), lambda p: (0, 0, 0))] * 2,
        out_shape=[full, full, one, one],
        scratch_shapes=[pltpu.VMEM((K, SLOTS), BF16)],
        compiler_params=PARAMS,
        cost_estimate=COST,
        name="sent_grams",
    )(*args)


def kept_grams(*args):
    return pl.pallas_call(
        kept_kernel,
        grid=(PATCHES,),
        in_specs=gram_specs(),
        out_specs=pl.BlockSpec((PATCHES, EXT, K), lambda p: (0, 0, 0)),
        out_shape=jax.ShapeDtypeStruct((PATCHES, EXT, K), F32),
        scratch_shapes=[pltpu.VMEM((K, SLOTS), BF16)],
        compiler_params=PARAMS,
        cost_estimate=COST,
        name="kept_grams",
    )(*args)


def split_to(refs, p, x):
    refs[0][p], refs[1][p] = split(x)


def root_kernel(patches, *refs):
    edges = len(patches) > 0 and patches[0] == 0
    count = 5 if edges else 3
    sources, out_ref, held, rest = refs[:count], refs[count], refs[count + 1 : 2 * count + 1], refs[2 * count + 1 :]
    sems, yh, yl, zh, zl, sh, sl, diag_ref, scale_ref = rest
    y, z, s = (yh, yl), (zh, zl), (sh, sl)
    n = len(patches)
    copies = []
    for p in range(n):
        which = [0, 1, 2] + ([3 if p == 0 else 4] if edges else [])
        at = [patches[p]] * 3 + [0]
        copies.append(
            [pltpu.make_async_copy(sources[w].at[i], held[w].at[p if w < 3 else 0], sems.at[p, j]) for j, (w, i) in enumerate(zip(which, at))]
        )
        start_all(copies[p])
    row = lax.broadcasted_iota(jnp.int32, (K, K), 0)
    col = lax.broadcasted_iota(jnp.int32, (K, K), 1)
    diag_ref[...] = jnp.where(row == col, 1.5, 0.0).astype(F32)

    def total(p, part):
        value = held[0][p, part, :] + held[1][p, part, :] + held[2][p, part, :]
        return value + held[3 + p][0, part, :] if edges else value

    def product(a, b, p):
        ah, al, bh, bl = a[0][p], a[1][p], b[0][p], b[1][p]
        return dot(jnp.concatenate([ah, ah, al], axis=1), jnp.concatenate([bl, bh, bh], axis=0))

    def residual(p):
        split_to(s, p, diag_ref[...] - 0.5 * product(z, y, p))

    for p in range(n):
        for copy in copies[p]:
            copy.wait()
        system = total(p, slice(0, K)) + jnp.where(row == col, float(K - 1), 0.0)
        bound = jnp.max(jnp.sum(jnp.abs(system), axis=1, keepdims=True), axis=0, keepdims=True)
        scale_ref[p] = jnp.broadcast_to(1.0 / jnp.sqrt(bound), (8, K))
        root = system / bound
        split_to(y, p, root)
        split_to(z, p, diag_ref[...] - 0.5 * root)
    for p in range(n):
        split_to(y, p, product(y, z, p))

    def sweep(index, carry):
        for p in range(n):
            residual(p)
        for p in range(n):
            split_to(y, p, product(y, s, p))
            split_to(z, p, product(s, z, p))
        return carry

    lax.fori_loop(0, ITERS - 2, sweep, 0, unroll=2)
    for p in range(n):
        residual(p)
    for p in range(n):
        half = product(s, z, p) * scale_ref[p, 0:1, :]
        flipped = half.T
        inner = jnp.sum(half * total(p, slice(K, K + 1)), axis=1, keepdims=True)
        mean_weight = jnp.sum(flipped * inner, axis=0, keepdims=True)
        out_ref[p] = (jnp.sqrt(float(K - 1)) * flipped + mean_weight).astype(BF16)


def root_weights(patches, *args):
    n = len(patches)
    piece = pltpu.VMEM((n, K, K), BF16)
    full, one = pltpu.VMEM((n, EXT, K), F32), pltpu.VMEM((1, EXT, K), F32)
    return pl.pallas_call(
        functools.partial(root_kernel, patches),
        in_specs=[ANY] * len(args),
        out_specs=VMEM,
        out_shape=jax.ShapeDtypeStruct((n, K, K), BF16),
        scratch_shapes=([full] * 3 + [one] * 2)[: len(args)]
        + [pltpu.SemaphoreType.DMA((n, 4))]
        + [piece] * 6
        + [pltpu.VMEM((K, K), F32), pltpu.VMEM((n, 8, K), F32)],
        compiler_params=PARAMS,
        cost_estimate=pl.CostEstimate(flops=ROOT_COST, bytes_accessed=1000, transcendentals=0),
        name="root_weights",
    )(*args)


def apply_kernel(inner_ref, outer_ref, states, c0, c2, c6, c1, c7, c4, states_s, result_s, sems):
    rows = states_s.shape[3]
    me = lax.axis_index("mem")
    copies = [pltpu.make_async_copy(states.at[:, p], states_s.at[:, p], sems.at[p]) for p in range(PATCHES)]
    start_all(copies)
    flipped = (outer_ref[0], inner_ref[0], inner_ref[1], outer_ref[1])
    for p in range(PATCHES):
        copies[p].wait()
        value = states_s[:, p].reshape(K, rows).astype(F32)
        mean = jnp.sum(value, axis=0, keepdims=True) * (1.0 / K)
        result = mean + dot(flipped[p], (value - mean).astype(BF16))
        result_s[:, p] = result.astype(BF16).reshape(PEERS, K // PEERS, rows)

    def away(places):
        return result_s[lax.rem(me + places, PEERS)]

    c0[...] = away(0)
    c2[0:PATCHES] = away(2)
    c2[PATCHES:] = away(3)
    c6[0:PATCHES] = away(6)
    c6[PATCHES:] = away(5)
    c1[...] = away(1)
    c7[...] = away(7)
    c4[...] = away(4)


def apply_weights(inner, outer, states):
    block = states.shape[1:]
    twice = (2 * PATCHES,) + block[1:]
    return pl.pallas_call(
        apply_kernel,
        in_specs=[VMEM, VMEM, ANY],
        out_specs=[VMEM] * 6,
        out_shape=[jax.ShapeDtypeStruct(shape, BF16) for shape in (block, twice, twice, block, block, block)],
        scratch_shapes=[pltpu.VMEM(states.shape, BF16)] * 2 + [pltpu.SemaphoreType.DMA((PATCHES,))],
        compiler_params=SMALL,
        cost_estimate=COST,
        name="apply_weights",
    )(inner, outer, states)


def gather_kernel(c0, c2, c6, c1, c7, c4, c3, c5, out, sems):
    me = lax.axis_index("mem")
    parts = ((c0, 0), (c1, 1), (c2, 2), (c3, 3), (c4, 4), (c5, 5), (c6, 6), (c7, 7))
    copies = []
    for ref, places in parts:
        source = lax.rem(me + PEERS - places, PEERS)
        copies.append(pltpu.make_async_copy(ref.at[pl.ds(0, PATCHES)], out.at[source], sems.at[places]))
    start_all(copies)
    for copy in copies:
        copy.wait()


def gather(*parts):
    shape = (PEERS,) + parts[0].shape
    return pl.pallas_call(
        gather_kernel,
        in_specs=[VMEM] * PEERS,
        out_specs=ANY,
        out_shape=jax.ShapeDtypeStruct(shape, BF16),
        scratch_shapes=[pltpu.SemaphoreType.DMA((PEERS,))],
        compiler_params=SMALL,
        cost_estimate=COST,
        name="gather",
    )(*parts)


def swap(value):
    return lax.all_to_all(value, "mem", split_axis=0, concat_axis=0, tiled=True)


def shift(value, axis, by):
    peers = lax.axis_size(axis)
    return lax.ppermute(value, axis, [(i, (i + by) % peers) for i in range(peers)])


def pair(value, axis, first):
    peers = lax.axis_size(axis)
    pairs = [((i + first) % peers, (i + 1 + first) % peers) for i in range(0, peers, 2)]
    return lax.ppermute(value, axis, pairs + [(j, i) for i, j in pairs])


def spread(c0, c2, c6, c1, c7, c4):
    c2 = shift(c2, "mem", 2)
    c6 = shift(c6, "mem", -2)
    c1 = shift(c1, "mem", 1)
    c7 = shift(c7, "mem", -1)
    c4 = shift(c4, "mem", 4)
    c3 = shift(c2[PATCHES:], "mem", 1)
    c5 = shift(c6[PATCHES:], "mem", -1)
    return gather(c0, c2, c6, c1, c7, c4, c3, c5)


def body(background, obs_ensemble, innovation, obs_precision, taper_weight, obs_count):
    rows = background.shape[3]
    background = background.reshape(PEERS, PATCHES, K // PEERS, rows)
    obs = (obs_count.reshape(PATCHES), obs_ensemble, innovation, obs_precision, taper_weight.transpose(0, 2, 1, 3))
    states = swap(background)
    near, far, following, previous = sent_grams(*obs)
    near = pair(near, "reg", 0)
    far = pair(far, "reg", 1)
    following = shift(following, "mem", 1)
    previous = shift(previous, "mem", -1)
    own = kept_grams(*obs)
    inner = root_weights((1, 2), own, near, far)
    outer = root_weights((0, 3), own, near, far, following, previous)
    analysis = spread(*apply_weights(inner, outer, states))
    return analysis.reshape(1, PEERS * PATCHES, K // PEERS, rows)


def solution(mesh):
    in_specs = (
        P("reg", None, "mem", None),
        P("reg", "mem", None, None),
        P("reg", "mem", None),
        P("reg", "mem", None),
        P("reg", "mem", None, None),
        P("reg", "mem"),
    )
    out_specs = P("reg", None, "mem", None)
    return jax.shard_map(body, mesh=mesh, in_specs=in_specs, out_specs=out_specs, check_vma=False)
```

time: 135 us -> 94.5 us (0.70)
  blocking collectives: 39.2 us -> 0 us
  Pallas kernels: 48.7 us -> 33.4 us
  starting transfers between devices: 13.5 us -> 27.5 us
  local copies, waits for them, and re-layouts: 5.85 us -> 2.23 us
  waiting for transfers between devices: 26.8 us -> 29.4 us
    all_to_all x1 -> x0, blocking collectives: 39.2 us -> none  [swap(): return lax.all_to_all(value, 'mem', split_axis=0, concat_axis=0, tiled=True)]
    ppermute x4 -> x9, starting transfers between devices: 5.08 us -> 18.1 us  [shift(): lax.ppermute(value, axis, [(i, (i + by) % peers) for i in range(peers)])]
    pallas_call x2 -> x4, Pallas kernels: 33.6 us -> 23.7 us  [the longest x2 20.9 us: root_weights(): pl.pallas_call(functools.partial(root_kernel, patches), in_specs=[ANY] *...]
    ppermute x0 -> x2, waiting for transfers between devices: none -> 5.92 us  [pair(): return lax.ppermute(value, axis, pairs + [(j, i) for i, j in pairs])]
    unnamed x12 -> x10, local copies, waits for them, and re-layouts: 5.85 us -> 2.2 us
    ppermute x4 -> x9, waiting for transfers between devices: 26.8 us -> 23.5 us  [shift(): lax.ppermute(value, axis, [(i, (i + by) % peers) for i in range(peers)])]
    pallas_call x1, Pallas kernels: 7.67 us -> 4.85 us  [sent_grams(): pl.pallas_call(sent_kernel, grid=(PATCHES,), in_specs=gram_specs(), out_s...]
    pallas_call x1, Pallas kernels: 7.45 us -> 4.84 us  [kept_grams(): pl.pallas_call(kept_kernel, grid=(PATCHES,), in_specs=gram_specs(), out_s...]
  transfers between devices with their start and end apart: 5 -> 12, of which waited for: 1 -> 7; matrix products, arithmetic and copies ran while one was open for 0% -> 0% of each run, Pallas kernels for 27% -> 33%
where the time goes in v2:
time: 94.5 us; the launch traced here: 92.8 us
  Pallas kernels  33.4 us (35%)
  waiting for transfers between devices  29.4 us (31%)
  starting transfers between devices  27.5 us (29%)
  local copies, waits for them, and re-layouts  2.23 us (2%)
    ppermute x9, waiting for transfers between devices, shift(): lax.ppermute(value, axis, [(i, (i + by) % peers) for i in range(peers)])  23.5 us
    pallas_call x2, Pallas kernels, root_weights(): pl.pallas_call(functools.partial(root_kernel, patches), in_specs=[ANY] *...  20.9 us
    ppermute x9, starting transfers between devices, shift(): lax.ppermute(value, axis, [(i, (i + by) % peers) for i in range(peers)])  18.1 us
    all_to_all x1, starting transfers between devices, swap(): return lax.all_to_all(value, 'mem', split_axis=0, concat_axis=0, tiled=True)  8.61 us
    ppermute x2, waiting for transfers between devices, pair(): return lax.ppermute(value, axis, pairs + [(j, i) for i, j in pairs])  5.92 us
    pallas_call x1, Pallas kernels, sent_grams(): pl.pallas_call(sent_kernel, grid=(PATCHES,), in_specs=gram_specs(), out_s...  4.85 us
    pallas_call x1, Pallas kernels, kept_grams(): pl.pallas_call(kept_kernel, grid=(PATCHES,), in_specs=gram_specs(), out_s...  4.84 us
    unnamed x10, local copies, waits for them, and re-layouts  2.2 us
  transfers between devices with their start and end apart: 12, of which 7 were waited for; matrix products, arithmetic and copies ran while one was open for 0% of the time, Pallas kernels for 33%

profile of v2, /device:TPU:26, one launch (start us, length us, event | category | flops | bytes accessed | tf_op | source)
XLA Modules:
  0.0 92.8 jit_solution(16400120235143531391)
XLA Ops:
  0.0 8.6 %all-to-all-start = ((bf16[8,4,32,640]{3,2,1,0:T(8,128)(2,1)}), bf16[8,4,32,640]{3,2,1,0:T(8,128)(2,1)S(1)}, u32[]{:S(2)}, u32[]{:S(2)}) async-start(bf16[8,4,32,640]{3,2,1,0:T(8,128)(2,1)} %bitcast.8), calls=%async_computation | async-start | bytes 2621440 | tf_op jit(solution)/shard_map/all_to_all | solution.py:308
  8.7 0.0 copy-start
  8.7 2.2 %copy-done = bf16[1,4,2048,256]{3,2,1,0:T(8,128)(2,1)S(1)} copy-done((bf16[1,4,2048,256]{3,2,1,0:T(8,128)(2,1)S(1)}, bf16[1,4,2048,256]{3,2,1,0:T(8,128)(2,1)}, u32[]{:S(2)}) %copy-start) | copy-done | bytes 4194328
  10.9 4.8 %sent_grams.1 = (f32[4,264,256]{2,1,0:T(8,128)S(1)}, f32[4,264,256]{2,1,0:T(8,128)S(1)}, f32[1,264,256]{2,1,0:T(8,128)S(1)}, f32[1,264,256]{2,1,0:T(8,128)S(1)}) custom-call(s32[4]{0:T(128)S(1)} %bitcast.6, bf16[1,4,2048,256]{3,2,1,0:T(8,128)(2,1)S(1)} %copy-done, bf16[1,4,2048]{2,1,0:T(4,128)(2,1)S(1)} %copy-done.2, bf16[1,4,2048]{2,1,0:T(4,128)(2,1)S(1)} %copy-done.3, ...), custom_call_target="tpu_custom_call" | custom-call | flops 1000 | bytes 1000 | tf_op jit(solution)/shard_map/sent_grams/pallas_call | solution.py:129
  15.7 0.1 collective-permute-start
  15.8 0.6 collective-permute-start.1
  16.5 2.0 %collective-permute-start.2 = (f32[1,264,256]{2,1,0:T(8,128)S(1)}, f32[1,264,256]{2,1,0:T(8,128)S(1)}, u32[]{:S(2)}, u32[]{:S(2)}) collective-permute-start(f32[1,264,256]{2,1,0:T(8,128)S(1)} %get-tuple-element.17), channel_id=1, source_target_pairs={{0,32},{32,64},{64,96},{96,128},{128,160},{160,192},{192,224},{224... | collective-permute-start | bytes 811016 | tf_op jit(solution)/shard_map/ppermute | solution.py:313
  18.5 1.2 %collective-permute-start.3 = (f32[1,264,256]{2,1,0:T(8,128)S(1)}, f32[1,264,256]{2,1,0:T(8,128)S(1)}, u32[]{:S(2)}, u32[]{:S(2)}) collective-permute-start(f32[1,264,256]{2,1,0:T(8,128)S(1)} %get-tuple-element.18), channel_id=1, source_target_pairs={{0,224},{32,0},{64,32},{96,64},{128,96},{160,128},{192,160},{224,1... | collective-permute-start | bytes 811016 | tf_op jit(solution)/shard_map/ppermute | solution.py:313
  19.7 4.8 %kept_grams.1.refs_0_ = f32[4,264,256]{2,1,0:T(8,128)S(1)} custom-call(s32[4]{0:T(128)S(1)} %bitcast.7, bf16[1,4,2048,256]{3,2,1,0:T(8,128)(2,1)S(1)} %copy-done, bf16[1,4,2048]{2,1,0:T(4,128)(2,1)S(1)} %copy-done.2, bf16[1,4,2048]{2,1,0:T(4,128)(2,1)S(1)} %copy-done.3, bf16[1,5,4,2048]{3,2,1,0:T(4,128)(2,1)S(1)} %bitcast.5), custom_call_target="tpu_custom_call" | custom-call | flops 1000 | bytes 1000 | tf_op jit(solution)/shard_map/kept_grams/pallas_call | solution.py:143
  24.5 0.0 collective-permute-done.refs_1_
  24.6 5.9 %collective-permute-done.1.refs_2_ = f32[4,264,256]{2,1,0:T(8,128)S(1)} collective-permute-done((f32[4,264,256]{2,1,0:T(8,128)S(1)}, f32[4,264,256]{2,1,0:T(8,128)S(1)}, u32[]{:S(2)}, u32[]{:S(2)}) %collective-permute-start.1) | collective-permute-done | bytes 1081376 | tf_op jit(solution)/shard_map/ppermute | solution.py:319
  30.5 10.4 %root_weights.2.inner_ref = bf16[2,256,256]{2,1,0:T(8,128)(2,1)S(1)} custom-call(f32[4,264,256]{2,1,0:T(8,128)S(1)} %kept_grams.1.refs_0_, f32[4,264,256]{2,1,0:T(8,128)S(1)} %collective-permute-done.refs_1_, f32[4,264,256]{2,1,0:T(8,128)S(1)} %collective-permute-done.1.refs_2_), custom_call_target="tpu_custom_call" | custom-call | flops 2000000000 | bytes 1000 | tf_op jit(solution)/shard_map/root_weights/pallas_call | solution.py:225
  40.9 5.2 %collective-permute-done.2.refs_3_ = f32[1,264,256]{2,1,0:T(8,128)S(1)} collective-permute-done((f32[1,264,256]{2,1,0:T(8,128)S(1)}, f32[1,264,256]{2,1,0:T(8,128)S(1)}, u32[]{:S(2)}, u32[]{:S(2)}) %collective-permute-start.2) | collective-permute-done | bytes 270368 | tf_op jit(solution)/shard_map/ppermute | solution.py:313
  46.1 0.0 collective-permute-done.3.refs_4_
  46.1 10.5 %root_weights.3.outer_ref = bf16[2,256,256]{2,1,0:T(8,128)(2,1)S(1)} custom-call(f32[4,264,256]{2,1,0:T(8,128)S(1)} %kept_grams.1.refs_0_, f32[4,264,256]{2,1,0:T(8,128)S(1)} %collective-permute-done.refs_1_, f32[4,264,256]{2,1,0:T(8,128)S(1)} %collective-permute-done.1.refs_2_, f32[1,264,256]{2,1,0:T(8,128)S(1)} %collective-permute-done.2.refs_3_, ...), custom_call_target="tpu_custom_call" | custom-call | flops 2000000000 | bytes 1000 | tf_op jit(solution)/shard_map/root_weights/pallas_call | solution.py:225
  56.6 0.0 all-to-all-done.states
  56.6 1.7 %apply_weights.1 = (bf16[4,32,640]{2,1,0:T(8,128)(2,1)S(1)}, bf16[8,32,640]{2,1,0:T(8,128)(2,1)S(1)}, bf16[8,32,640]{2,1,0:T(8,128)(2,1)S(1)}, bf16[4,32,640]{2,...) custom-call(bf16[2,256,256]{2,1,0:T(8,128)(2,1)S(1)} %root_weights.2.inner_ref, ...), custom_call_target="tpu_custom_call" | custom-call | flops 1000 | bytes 1000 | tf_op jit(solution)/shard_map/apply_weights/pallas_call | solution.py:269
  58.3 2.4 %collective-permute-start.5 = (bf16[8,32,640]{2,1,0:T(8,128)(2,1)S(1)}, bf16[8,32,640]{2,1,0:T(8,128)(2,1)S(1)}, u32[]{:S(2)}, u32[]{:S(2)}) collective-permute-start(bf16[8,32,640]{2,1,0:T(8,128)(2,1)S(1)} %get-tuple-element.21), channel_id=1, source_target_pairs={{0,192},{32,224},{64,0},{96,32},{128,64},{160,96},{192,128},{224,1... | collective-permute-start | bytes 983048 | tf_op jit(solution)/shard_map/ppermute | solution.py:313
  60.7 0.6 collective-permute-start.4
  61.3 1.0 %collective-permute-start.6 = (bf16[4,32,640]{2,1,0:T(8,128)(2,1)S(1)}, bf16[4,32,640]{2,1,0:T(8,128)(2,1)S(1)}, u32[]{:S(2)}, u32[]{:S(2)}) collective-permute-start(bf16[4,32,640]{2,1,0:T(8,128)(2,1)S(1)} %get-tuple-element.22), channel_id=1, source_target_pairs={{0,32},{32,64},{64,96},{96,128},{128,160},{160,192},{192,224},{224... | collective-permute-start | bytes 491528 | tf_op jit(solution)/shard_map/ppermute | solution.py:313
  62.3 2.3 %collective-permute-start.7 = (bf16[4,32,640]{2,1,0:T(8,128)(2,1)S(1)}, bf16[4,32,640]{2,1,0:T(8,128)(2,1)S(1)}, u32[]{:S(2)}, u32[]{:S(2)}) collective-permute-start(bf16[4,32,640]{2,1,0:T(8,128)(2,1)S(1)} %get-tuple-element.23), channel_id=1, source_target_pairs={{0,224},{32,0},{64,32},{96,64},{128,96},{160,128},{192,160},{224,1... | collective-permute-start | bytes 491528 | tf_op jit(solution)/shard_map/ppermute | solution.py:313
  64.5 3.9 %collective-permute-start.8 = (bf16[4,32,640]{2,1,0:T(8,128)(2,1)S(1)}, bf16[4,32,640]{2,1,0:T(8,128)(2,1)S(1)}, u32[]{:S(2)}, u32[]{:S(2)}) collective-permute-start(bf16[4,32,640]{2,1,0:T(8,128)(2,1)S(1)} %get-tuple-element.24), channel_id=1, source_target_pairs={{0,128},{32,160},{64,192},{96,224},{128,0},{160,32},{192,64},{224,... | collective-permute-start | bytes 491528 | tf_op jit(solution)/shard_map/ppermute | solution.py:313
  68.4 6.5 %collective-permute-done.5.c6 = bf16[8,32,640]{2,1,0:T(8,128)(2,1)S(1)} collective-permute-done((bf16[8,32,640]{2,1,0:T(8,128)(2,1)S(1)}, bf16[8,32,640]{2,1,0:T(8,128)(2,1)S(1)}, u32[]{:S(2)}, u32[]{:S(2)}) %collective-permute-start.5) | collective-permute-done | bytes 327712 | tf_op jit(solution)/shard_map/ppermute | solution.py:313
  75.0 4.6 %collective-permute-start.10 = (bf16[4,32,640]{2,1,0:T(8,128)(2,1)S(1)}, bf16[4,32,640]{2,1,0:T(8,128)(2,1)S(1)}, u32[]{:S(2)}, u32[]{:S(2)}) collective-permute-start(bf16[4,32,640]{2,1,0:T(8,128)(2,1)S(1)} %slice.9), channel_id=1, source_target_pairs={{0,224},{32,0},{64,32},{96,64},{128,96},{160,128},{192,160},{224,1... | collective-permute-start | bytes 491528 | tf_op jit(solution)/shard_map/ppermute | solution.py:313
  79.6 1.7 %collective-permute-done.4.c2 = bf16[8,32,640]{2,1,0:T(8,128)(2,1)S(1)} collective-permute-done((bf16[8,32,640]{2,1,0:T(8,128)(2,1)S(1)}, bf16[8,32,640]{2,1,0:T(8,128)(2,1)S(1)}, u32[]{:S(2)}, u32[]{:S(2)}) %collective-permute-start.4) | collective-permute-done | bytes 327712 | tf_op jit(solution)/shard_map/ppermute | solution.py:313
  81.3 0.1 collective-permute-start.9
  81.4 4.2 %collective-permute-done.6.c1 = bf16[4,32,640]{2,1,0:T(8,128)(2,1)S(1)} collective-permute-done((bf16[4,32,640]{2,1,0:T(8,128)(2,1)S(1)}, bf16[4,32,640]{2,1,0:T(8,128)(2,1)S(1)}, u32[]{:S(2)}, u32[]{:S(2)}) %collective-permute-start.6) | collective-permute-done | bytes 163872 | tf_op jit(solution)/shard_map/ppermute | solution.py:313
  85.6 0.0 collective-permute-done.7.c7
  85.6 3.8 %collective-permute-done.8.c4 = bf16[4,32,640]{2,1,0:T(8,128)(2,1)S(1)} collective-permute-done((bf16[4,32,640]{2,1,0:T(8,128)(2,1)S(1)}, bf16[4,32,640]{2,1,0:T(8,128)(2,1)S(1)}, u32[]{:S(2)}, u32[]{:S(2)}) %collective-permute-start.8) | collective-permute-done | bytes 163872 | tf_op jit(solution)/shard_map/ppermute | solution.py:313
  89.4 0.0 collective-permute-done.10.c5
  89.4 2.1 %collective-permute-done.9.c3 = bf16[4,32,640]{2,1,0:T(8,128)(2,1)S(1)} collective-permute-done((bf16[4,32,640]{2,1,0:T(8,128)(2,1)S(1)}, bf16[4,32,640]{2,1,0:T(8,128)(2,1)S(1)}, u32[]{:S(2)}, u32[]{:S(2)}) %collective-permute-start.9) | collective-permute-done | bytes 163872 | tf_op jit(solution)/shard_map/ppermute | solution.py:313
  91.5 1.1 %gather.1 = bf16[8,4,32,640]{3,2,1,0:T(8,128)(2,1)} custom-call(bf16[4,32,640]{2,1,0:T(8,128)(2,1)S(1)} %get-tuple-element.19.c0, bf16[8,32,640]{2,1,0:T(8,128)(2,1)S(1)} %collective-permute-done.4.c2, bf16[8,32,640]{2,1,0:T(8,128)(2,1)S(1)} %collective-permute-done.5.c6, bf16[4,32,640]{2,1,0:T(8,128)(2,1)S(1)} %collective-permute-done.6.c1, ...), custom_call_target="tpu_custom_call" | custom-call | flops 1000 | bytes 1000 | tf_op jit(solution)/shard_map/gather/pallas_call | solution.py:295
  (10 shorter events, 0.0 us)
Async XLA Ops:
  0.0 8.6 %copy-start.1 = (bf16[1,4,5,2048]{3,1,2,0:T(4,128)(2,1)S(1)}, bf16[1,4,5,2048]{3,1,2,0:T(4,128)(2,1)}, u32[]{:S(2)}) copy-start(bf16[1,4,5,2048]{3,1,2,0:T(4,128)(2,1)} %param.10) | copy-start | bytes 245764
  0.0 8.6 %copy-start.2 = (bf16[1,4,2048]{2,1,0:T(4,128)(2,1)S(1)}, bf16[1,4,2048]{2,1,0:T(4,128)(2,1)}, u32[]{:S(2)}) copy-start(bf16[1,4,2048]{2,1,0:T(4,128)(2,1)} %innov_ref.3) | copy-start | bytes 49156
  0.0 8.6 %copy-start.3 = (bf16[1,4,2048]{2,1,0:T(4,128)(2,1)S(1)}, bf16[1,4,2048]{2,1,0:T(4,128)(2,1)}, u32[]{:S(2)}) copy-start(bf16[1,4,2048]{2,1,0:T(4,128)(2,1)} %prec_ref.3) | copy-start | bytes 49156
  0.0 8.6 %copy-start.4 = (s32[1,4]{1,0:T(1,128)S(1)}, s32[1,4]{1,0:T(1,128)}, u32[]{:S(2)}) copy-start(s32[1,4]{1,0:T(1,128)} %param.11) | copy-start | bytes 52
  0.0 56.6 %all-to-all-start = ((bf16[8,4,32,640]{3,2,1,0:T(8,128)(2,1)}), bf16[8,4,32,640]{3,2,1,0:T(8,128)(2,1)S(1)}, u32[]{:S(2)}, u32[]{:S(2)}) async-start(bf16[8,4,32,640]{3,2,1,0:T(8,128)(2,1)} %bitcast.8), calls=%async_computation | async-start | bytes 2621440 | tf_op jit(solution)/shard_map/all_to_all | solution.py:308
  8.7 2.2 %copy-start = (bf16[1,4,2048,256]{3,2,1,0:T(8,128)(2,1)S(1)}, bf16[1,4,2048,256]{3,2,1,0:T(8,128)(2,1)}, u32[]{:S(2)}) copy-start(bf16[1,4,2048,256]{3,2,1,0:T(8,128)(2,1)} %ens_ref.3) | copy-start | bytes 12582916
  15.7 8.8 %collective-permute-start = (f32[4,264,256]{2,1,0:T(8,128)S(1)}, f32[4,264,256]{2,1,0:T(8,128)S(1)}, u32[]{:S(2)}, u32[]{:S(2)}) collective-permute-start(f32[4,264,256]{2,1,0:T(8,128)S(1)} %get-tuple-element.15), channel_id=1, source_target_pairs={{0,1},{2,3},{4,5},{6,7},{8,9},{10,11},{12,13},{14,15},{16,17},{18,... | collective-permute-start | bytes 3244040 | tf_op jit(solution)/shard_map/ppermute | solution.py:319
  15.8 14.7 %collective-permute-start.1 = (f32[4,264,256]{2,1,0:T(8,128)S(1)}, f32[4,264,256]{2,1,0:T(8,128)S(1)}, u32[]{:S(2)}, u32[]{:S(2)}) collective-permute-start(f32[4,264,256]{2,1,0:T(8,128)S(1)} %get-tuple-element.16), channel_id=1, source_target_pairs={{1,2},{3,4},{5,6},{7,8},{9,10},{11,12},{13,14},{15,16},{17,18},{19... | collective-permute-start | bytes 3244040 | tf_op jit(solution)/shard_map/ppermute | solution.py:319
  16.5 29.6 %collective-permute-start.2 = (f32[1,264,256]{2,1,0:T(8,128)S(1)}, f32[1,264,256]{2,1,0:T(8,128)S(1)}, u32[]{:S(2)}, u32[]{:S(2)}) collective-permute-start(f32[1,264,256]{2,1,0:T(8,128)S(1)} %get-tuple-element.17), channel_id=1, source_target_pairs={{0,32},{32,64},{64,96},{96,128},{128,160},{160,192},{192,224},{224... | collective-permute-start | bytes 811016 | tf_op jit(solution)/shard_map/ppermute | solution.py:313
  18.5 27.6 %collective-permute-start.3 = (f32[1,264,256]{2,1,0:T(8,128)S(1)}, f32[1,264,256]{2,1,0:T(8,128)S(1)}, u32[]{:S(2)}, u32[]{:S(2)}) collective-permute-start(f32[1,264,256]{2,1,0:T(8,128)S(1)} %get-tuple-element.18), channel_id=1, source_target_pairs={{0,224},{32,0},{64,32},{96,64},{128,96},{160,128},{192,160},{224,1... | collective-permute-start | bytes 811016 | tf_op jit(solution)/shard_map/ppermute | solution.py:313
  58.3 16.7 %collective-permute-start.5 = (bf16[8,32,640]{2,1,0:T(8,128)(2,1)S(1)}, bf16[8,32,640]{2,1,0:T(8,128)(2,1)S(1)}, u32[]{:S(2)}, u32[]{:S(2)}) collective-permute-start(bf16[8,32,640]{2,1,0:T(8,128)(2,1)S(1)} %get-tuple-element.21), channel_id=1, source_target_pairs={{0,192},{32,224},{64,0},{96,32},{128,64},{160,96},{192,128},{224,1... | collective-permute-start | bytes 983048 | tf_op jit(solution)/shard_map/ppermute | solution.py:313
  60.7 20.6 %collective-permute-start.4 = (bf16[8,32,640]{2,1,0:T(8,128)(2,1)S(1)}, bf16[8,32,640]{2,1,0:T(8,128)(2,1)S(1)}, u32[]{:S(2)}, u32[]{:S(2)}) collective-permute-start(bf16[8,32,640]{2,1,0:T(8,128)(2,1)S(1)} %get-tuple-element.20), channel_id=1, source_target_pairs={{0,64},{32,96},{64,128},{96,160},{128,192},{160,224},{192,0},{224,... | collective-permute-start | bytes 983048 | tf_op jit(solution)/shard_map/ppermute | solution.py:313
  61.3 24.3 %collective-permute-start.6 = (bf16[4,32,640]{2,1,0:T(8,128)(2,1)S(1)}, bf16[4,32,640]{2,1,0:T(8,128)(2,1)S(1)}, u32[]{:S(2)}, u32[]{:S(2)}) collective-permute-start(bf16[4,32,640]{2,1,0:T(8,128)(2,1)S(1)} %get-tuple-element.22), channel_id=1, source_target_pairs={{0,32},{32,64},{64,96},{96,128},{128,160},{160,192},{192,224},{224... | collective-permute-start | bytes 491528 | tf_op jit(solution)/shard_map/ppermute | solution.py:313
  62.3 23.3 %collective-permute-start.7 = (bf16[4,32,640]{2,1,0:T(8,128)(2,1)S(1)}, bf16[4,32,640]{2,1,0:T(8,128)(2,1)S(1)}, u32[]{:S(2)}, u32[]{:S(2)}) collective-permute-start(bf16[4,32,640]{2,1,0:T(8,128)(2,1)S(1)} %get-tuple-element.23), channel_id=1, source_target_pairs={{0,224},{32,0},{64,32},{96,64},{128,96},{160,128},{192,160},{224,1... | collective-permute-start | bytes 491528 | tf_op jit(solution)/shard_map/ppermute | solution.py:313
  64.5 24.9 %collective-permute-start.8 = (bf16[4,32,640]{2,1,0:T(8,128)(2,1)S(1)}, bf16[4,32,640]{2,1,0:T(8,128)(2,1)S(1)}, u32[]{:S(2)}, u32[]{:S(2)}) collective-permute-start(bf16[4,32,640]{2,1,0:T(8,128)(2,1)S(1)} %get-tuple-element.24), channel_id=1, source_target_pairs={{0,128},{32,160},{64,192},{96,224},{128,0},{160,32},{192,64},{224,... | collective-permute-start | bytes 491528 | tf_op jit(solution)/shard_map/ppermute | solution.py:313
  75.0 14.4 %collective-permute-start.10 = (bf16[4,32,640]{2,1,0:T(8,128)(2,1)S(1)}, bf16[4,32,640]{2,1,0:T(8,128)(2,1)S(1)}, u32[]{:S(2)}, u32[]{:S(2)}) collective-permute-start(bf16[4,32,640]{2,1,0:T(8,128)(2,1)S(1)} %slice.9), channel_id=1, source_target_pairs={{0,224},{32,0},{64,32},{96,64},{128,96},{160,128},{192,160},{224,1... | collective-permute-start | bytes 491528 | tf_op jit(solution)/shard_map/ppermute | solution.py:313
  81.3 10.2 %collective-permute-start.9 = (bf16[4,32,640]{2,1,0:T(8,128)(2,1)S(1)}, bf16[4,32,640]{2,1,0:T(8,128)(2,1)S(1)}, u32[]{:S(2)}, u32[]{:S(2)}) collective-permute-start(bf16[4,32,640]{2,1,0:T(8,128)(2,1)S(1)} %slice.8), channel_id=1, source_target_pairs={{0,32},{32,64},{64,96},{96,128},{128,160},{160,192},{192,224},{224... | collective-permute-start | bytes 491528 | tf_op jit(solution)/shard_map/ppermute | solution.py:313

commit v3 on v2

--- a/solution.py
+++ b/solution.py
@@ -10,6 +10,8 @@
 BF16 = jnp.bfloat16
 ITERS = 12
 ROOT_COST = 2 * 10**9
+INNER = (1, 2)
+OUTER = (0, 3)
 PATCHES = 4
 SIDES = 5
 K = 256
@@ -50,13 +52,15 @@
 
 
 def weighted_grams(ens_ref, flipped_ref, rows, innov):
-    flipped_ref[...] = ens_ref[0, 0].T
-    driven = jnp.concatenate([row * innov for row in rows] + [jnp.zeros((8 - len(rows), SLOTS), F32)], axis=0)
-    scaled = [(flipped_ref[...].astype(F32) * row).astype(BF16) for row in rows]
-    both = dot(jnp.concatenate(scaled + list(split(driven)), axis=0), ens_ref[0, 0])
-    n = len(rows) * K
-    drives = both[n : n + 8] + both[n + 8 : n + 16]
-    return [(both[i * K : (i + 1) * K], drives[i : i + 1]) for i in range(len(rows))]
+    flipped_ref[0:K] = ens_ref[0, 0].T
+    flipped_ref[K:] = jnp.broadcast_to(innov, (16, SLOTS)).astype(BF16)
+    flipped = flipped_ref[...]
+    pairs = []
+    for row in rows:
+        scaled = (flipped[0:K].astype(F32) * row).astype(BF16)
+        both = lax.dot_general(flipped, scaled, (((1,), (1,)), ((), ())), preferred_element_type=F32)
+        pairs.append((both[0:K], both[K : K + 1]))
+    return pairs
 
 
 def sent_kernel(count_ref, ens_ref, innov_ref, prec_ref, taper_ref, near_ref, far_ref, next_ref, prev_ref, flipped_ref):
@@ -132,7 +136,7 @@
         in_specs=gram_specs(),
         out_specs=[pl.BlockSpec((1, EXT, K), lambda p: (p, 0, 0))] * 2 + [pl.BlockSpec((1, EXT, K), lambda p: (0, 0, 0))] * 2,
         out_shape=[full, full, one, one],
-        scratch_shapes=[pltpu.VMEM((K, SLOTS), BF16)],
+        scratch_shapes=[pltpu.VMEM((K + 16, SLOTS), BF16)],
         compiler_params=PARAMS,
         cost_estimate=COST,
         name="sent_grams",
@@ -146,7 +150,7 @@
         in_specs=gram_specs(),
         out_specs=pl.BlockSpec((PATCHES, EXT, K), lambda p: (0, 0, 0)),
         out_shape=jax.ShapeDtypeStruct((PATCHES, EXT, K), F32),
-        scratch_shapes=[pltpu.VMEM((K, SLOTS), BF16)],
+        scratch_shapes=[pltpu.VMEM((K + 16, SLOTS), BF16)],
         compiler_params=PARAMS,
         cost_estimate=COST,
         name="kept_grams",
@@ -157,28 +161,39 @@
     refs[0][p], refs[1][p] = split(x)
 
 
-def root_kernel(patches, *refs):
-    edges = len(patches) > 0 and patches[0] == 0
-    count = 5 if edges else 3
-    sources, out_ref, held, rest = refs[:count], refs[count], refs[count + 1 : 2 * count + 1], refs[2 * count + 1 :]
-    sems, yh, yl, zh, zl, sh, sl, diag_ref, scale_ref = rest
+def root_kernel(edges, *refs):
+    n = 2
+    if edges:
+        sums, following, previous, out_ref, *rest = refs
+        pairs = [[(sums, 0, 0, 0), (following, 0, 1, 0)], [(sums, 1, 0, 1), (previous, 0, 1, 1)]]
+    else:
+        *parts, out_ref, sums_ref, rest_s, rest_sems = refs[:5] + refs[-2:]
+        rest = refs[5:-2]
+        pairs = [[(ref, p, w, i) for w, ref in enumerate(parts)] for i, p in enumerate(INNER)]
+    held, sems, yh, yl, zh, zl, sh, sl, diag_ref, scale_ref = rest
     y, z, s = (yh, yl), (zh, zl), (sh, sl)
-    n = len(patches)
-    copies = []
+    copies = [
+        [pltpu.make_async_copy(ref.at[at], held.at[w, i], sems.at[p, j]) for j, (ref, at, w, i) in enumerate(pairs[p])]
+        for p in range(n)
+    ]
     for p in range(n):
-        which = [0, 1, 2] + ([3 if p == 0 else 4] if edges else [])
-        at = [patches[p]] * 3 + [0]
-        copies.append(
-            [pltpu.make_async_copy(sources[w].at[i], held[w].at[p if w < 3 else 0], sems.at[p, j]) for j, (w, i) in enumerate(zip(which, at))]
-        )
         start_all(copies[p])
+    if not edges:
+        others = [
+            pltpu.make_async_copy(ref.at[p], rest_s.at[w, i], rest_sems.at[w, i])
+            for w, ref in enumerate(parts)
+            for i, p in enumerate(OUTER)
+        ]
+        start_all(others)
     row = lax.broadcasted_iota(jnp.int32, (K, K), 0)
     col = lax.broadcasted_iota(jnp.int32, (K, K), 1)
     diag_ref[...] = jnp.where(row == col, 1.5, 0.0).astype(F32)
 
     def total(p, part):
-        value = held[0][p, part, :] + held[1][p, part, :] + held[2][p, part, :]
-        return value + held[3 + p][0, part, :] if edges else value
+        value = held[0, p, part, :]
+        for w in range(1, held.shape[0]):
+            value = value + held[w, p, part, :]
+        return value
 
     def product(a, b, p):
         ah, al, bh, bl = a[0][p], a[1][p], b[0][p], b[1][p]
@@ -191,7 +206,7 @@
         for copy in copies[p]:
             copy.wait()
         system = total(p, slice(0, K)) + jnp.where(row == col, float(K - 1), 0.0)
-        bound = jnp.max(jnp.sum(jnp.abs(system), axis=1, keepdims=True), axis=0, keepdims=True)
+        bound = jnp.max(jnp.sum(jnp.abs(system), axis=0, keepdims=True), axis=1, keepdims=True)
         scale_ref[p] = jnp.broadcast_to(1.0 / jnp.sqrt(bound), (8, K))
         root = system / bound
         split_to(y, p, root)
@@ -207,101 +222,122 @@
             split_to(z, p, product(s, z, p))
         return carry
 
-    lax.fori_loop(0, ITERS - 2, sweep, 0, unroll=2)
+    lax.fori_loop(0, ITERS - 2, sweep, 0, unroll=True)
     for p in range(n):
         residual(p)
     for p in range(n):
-        half = product(s, z, p) * scale_ref[p, 0:1, :]
-        flipped = half.T
+        flipped = product(s, z, p) * scale_ref[p, 0:1, :]
+        half = flipped.T
         inner = jnp.sum(half * total(p, slice(K, K + 1)), axis=1, keepdims=True)
         mean_weight = jnp.sum(flipped * inner, axis=0, keepdims=True)
         out_ref[p] = (jnp.sqrt(float(K - 1)) * flipped + mean_weight).astype(BF16)
-
-
-def root_weights(patches, *args):
-    n = len(patches)
+    if not edges:
+        for copy in others:
+            copy.wait()
+        for i in range(n):
+            sums_ref[i] = rest_s[0, i] + rest_s[1, i] + rest_s[2, i]
+
+
+def root_weights(edges, *args):
+    n = 2
     piece = pltpu.VMEM((n, K, K), BF16)
-    full, one = pltpu.VMEM((n, EXT, K), F32), pltpu.VMEM((1, EXT, K), F32)
+    parts = 2 if edges else 3
+    held, sems = pltpu.VMEM((parts, n, EXT, K), F32), pltpu.SemaphoreType.DMA((parts, max(n, parts)))
+    shapes = [jax.ShapeDtypeStruct((n, K, K), BF16)] + ([] if edges else [jax.ShapeDtypeStruct((n, EXT, K), F32)])
     return pl.pallas_call(
-        functools.partial(root_kernel, patches),
+        functools.partial(root_kernel, edges),
         in_specs=[ANY] * len(args),
-        out_specs=VMEM,
-        out_shape=jax.ShapeDtypeStruct((n, K, K), BF16),
-        scratch_shapes=([full] * 3 + [one] * 2)[: len(args)]
-        + [pltpu.SemaphoreType.DMA((n, 4))]
+        out_specs=[VMEM] * len(shapes),
+        out_shape=shapes,
+        scratch_shapes=[held, sems]
         + [piece] * 6
-        + [pltpu.VMEM((K, K), F32), pltpu.VMEM((n, 8, K), F32)],
+        + [pltpu.VMEM((K, K), F32), pltpu.VMEM((n, 8, K), F32)]
+        + ([] if edges else [held, sems]),
         compiler_params=PARAMS,
         cost_estimate=pl.CostEstimate(flops=ROOT_COST, bytes_accessed=1000, transcendentals=0),
         name="root_weights",
     )(*args)
 
 
-def apply_kernel(inner_ref, outer_ref, states, c0, c2, c6, c1, c7, c4, states_s, result_s, sems):
+def analysed(states, flipped):
+    states = states.astype(F32)
+    mean = jnp.sum(states, axis=0, keepdims=True) * (1.0 / K)
+    return (mean + dot(flipped, (states - mean).astype(BF16))).astype(BF16)
+
+
+def apply_kernel(patches, flipped_ref, states, *refs):
+    *out_refs, states_s, sems = refs
     rows = states_s.shape[3]
+    copies = [pltpu.make_async_copy(states.at[:, p], states_s.at[:, i], sems.at[i]) for i, p in enumerate(patches)]
+    start_all(copies)
+    whole = out_refs[-1]
+    for i in range(len(patches)):
+        copies[i].wait()
+        whole[:, i] = analysed(states_s[:, i].reshape(K, rows), flipped_ref[i]).reshape(PEERS, K // PEERS, rows)
+    if len(out_refs) == 1:
+        return
+    c0, c2, c6, c1, c7, c4 = out_refs[:6]
     me = lax.axis_index("mem")
-    copies = [pltpu.make_async_copy(states.at[:, p], states_s.at[:, p], sems.at[p]) for p in range(PATCHES)]
-    start_all(copies)
-    flipped = (outer_ref[0], inner_ref[0], inner_ref[1], outer_ref[1])
-    for p in range(PATCHES):
-        copies[p].wait()
-        value = states_s[:, p].reshape(K, rows).astype(F32)
-        mean = jnp.sum(value, axis=0, keepdims=True) * (1.0 / K)
-        result = mean + dot(flipped[p], (value - mean).astype(BF16))
-        result_s[:, p] = result.astype(BF16).reshape(PEERS, K // PEERS, rows)
 
     def away(places):
-        return result_s[lax.rem(me + places, PEERS)]
-
+        return whole[lax.rem(me + places, PEERS)]
+
+    n = len(patches)
     c0[...] = away(0)
-    c2[0:PATCHES] = away(2)
-    c2[PATCHES:] = away(3)
-    c6[0:PATCHES] = away(6)
-    c6[PATCHES:] = away(5)
+    c2[0:n] = away(2)
+    c2[n:] = away(3)
+    c6[0:n] = away(6)
+    c6[n:] = away(5)
     c1[...] = away(1)
     c7[...] = away(7)
     c4[...] = away(4)
 
 
-def apply_weights(inner, outer, states):
-    block = states.shape[1:]
-    twice = (2 * PATCHES,) + block[1:]
+def apply_weights(patches, flipped, states, turned):
+    n = len(patches)
+    block = (n,) + states.shape[2:]
+    twice = (2 * n,) + states.shape[2:]
+    whole = pltpu.VMEM((PEERS,) + block, BF16)
+    shapes = (block, twice, twice, block, block, block) if turned else ((PEERS,) + block,)
     return pl.pallas_call(
-        apply_kernel,
-        in_specs=[VMEM, VMEM, ANY],
-        out_specs=[VMEM] * 6,
-        out_shape=[jax.ShapeDtypeStruct(shape, BF16) for shape in (block, twice, twice, block, block, block)],
-        scratch_shapes=[pltpu.VMEM(states.shape, BF16)] * 2 + [pltpu.SemaphoreType.DMA((PATCHES,))],
+        functools.partial(apply_kernel, patches),
+        in_specs=[VMEM, ANY],
+        out_specs=[VMEM] * len(shapes),
+        out_shape=[jax.ShapeDtypeStruct(shape, BF16) for shape in shapes],
+        scratch_shapes=[whole] * (2 if turned else 1) + [pltpu.SemaphoreType.DMA((n,))],
         compiler_params=SMALL,
         cost_estimate=COST,
         name="apply_weights",
-    )(inner, outer, states)
-
-
-def gather_kernel(c0, c2, c6, c1, c7, c4, c3, c5, out, sems):
+    )(flipped, states)
+
+
+def gather_kernel(first, c0, c2, c6, c1, c7, c4, c3, c5, out, sems):
     me = lax.axis_index("mem")
     parts = ((c0, 0), (c1, 1), (c2, 2), (c3, 3), (c4, 4), (c5, 5), (c6, 6), (c7, 7))
     copies = []
+    for j in range(PEERS):
+        copies.append(pltpu.make_async_copy(first.at[j], out.at[j, pl.ds(1, 2)], sems.at[j]))
     for ref, places in parts:
         source = lax.rem(me + PEERS - places, PEERS)
-        copies.append(pltpu.make_async_copy(ref.at[pl.ds(0, PATCHES)], out.at[source], sems.at[places]))
+        for i, p in enumerate(OUTER):
+            copies.append(pltpu.make_async_copy(ref.at[i], out.at[source, p], sems.at[PEERS + 2 * places + i]))
     start_all(copies)
     for copy in copies:
         copy.wait()
 
 
-def gather(*parts):
-    shape = (PEERS,) + parts[0].shape
+def gather(first, *parts):
+    shape = (PEERS, PATCHES) + first.shape[2:]
     return pl.pallas_call(
         gather_kernel,
-        in_specs=[VMEM] * PEERS,
+        in_specs=[VMEM] * (PEERS + 1),
         out_specs=ANY,
         out_shape=jax.ShapeDtypeStruct(shape, BF16),
-        scratch_shapes=[pltpu.SemaphoreType.DMA((PEERS,))],
+        scratch_shapes=[pltpu.SemaphoreType.DMA((3 * PEERS,))],
         compiler_params=SMALL,
         cost_estimate=COST,
         name="gather",
-    )(*parts)
+    )(first, *parts)
 
 
 def swap(value):
@@ -320,14 +356,15 @@
 
 
 def spread(c0, c2, c6, c1, c7, c4):
+    n = c0.shape[0]
     c2 = shift(c2, "mem", 2)
     c6 = shift(c6, "mem", -2)
     c1 = shift(c1, "mem", 1)
     c7 = shift(c7, "mem", -1)
     c4 = shift(c4, "mem", 4)
-    c3 = shift(c2[PATCHES:], "mem", 1)
-    c5 = shift(c6[PATCHES:], "mem", -1)
-    return gather(c0, c2, c6, c1, c7, c4, c3, c5)
+    c3 = shift(c2[n:], "mem", 1)
+    c5 = shift(c6[n:], "mem", -1)
+    return c0, c2, c6, c1, c7, c4, c3, c5
 
 
 def body(background, obs_ensemble, innovation, obs_precision, taper_weight, obs_count):
@@ -341,9 +378,12 @@
     following = shift(following, "mem", 1)
     previous = shift(previous, "mem", -1)
     own = kept_grams(*obs)
-    inner = root_weights((1, 2), own, near, far)
-    outer = root_weights((0, 3), own, near, far, following, previous)
-    analysis = spread(*apply_weights(inner, outer, states))
+    flipped, sums = root_weights(False, own, near, far)
+    (first,) = apply_weights(INNER, flipped, states, False)
+    first, following, previous = lax.optimization_barrier((first, following, previous))
+    first = swap(first)
+    (flipped,) = root_weights(True, sums, following, previous)
+    analysis = gather(first, *spread(*apply_weights(OUTER, flipped, states, True)))
     return analysis.reshape(1, PEERS * PATCHES, K // PEERS, rows)
 
 

time: 94.5 us -> 87.2 us (0.923)
  waiting for transfers between devices: 29.4 us -> 18.5 us
  starting transfers between devices: 27.5 us -> 32.1 us
    ppermute x9, waiting for transfers between devices: 23.5 us -> 9.96 us  [shift(): lax.ppermute(value, axis, [(i, (i + by) % peers) for i in range(peers)])]
    all_to_all x1 -> x2, starting transfers between devices: 8.61 us -> 13.3 us  [swap(): return lax.all_to_all(value, 'mem', split_axis=0, concat_axis=0, tiled=True)]
    all_to_all x1 -> x2, waiting for transfers between devices: 0.01 us -> 2.85 us  [swap(): return lax.all_to_all(value, 'mem', split_axis=0, concat_axis=0, tiled=True)]
    pallas_call x4 -> x5, Pallas kernels: 23.7 us -> 22.4 us  [the longest x2 18.7 us: root_weights(): pl.pallas_call(functools.partial(root_kernel, edges), in_specs=[ANY] * le...]
  transfers between devices with their start and end apart: 12 -> 13, of which waited for: 7 -> 7; matrix products, arithmetic and copies ran while one was open for 0% -> 0% of each run, Pallas kernels for 33% -> 37%
where the time goes in v3:
time: 87.2 us; the launch traced here: 85.7 us
  Pallas kernels  32.5 us (37%)
  starting transfers between devices  32.1 us (37%)
  waiting for transfers between devices  18.5 us (21%)
  local copies, waits for them, and re-layouts  2.21 us (3%)
    pallas_call x2, Pallas kernels, root_weights(): pl.pallas_call(functools.partial(root_kernel, edges), in_specs=[ANY] * le...  18.7 us
    ppermute x9, starting transfers between devices, shift(): lax.ppermute(value, axis, [(i, (i + by) % peers) for i in range(peers)])  18.1 us
    all_to_all x2, starting transfers between devices, swap(): return lax.all_to_all(value, 'mem', split_axis=0, concat_axis=0, tiled=True)  13.3 us
    ppermute x9, waiting for transfers between devices, shift(): lax.ppermute(value, axis, [(i, (i + by) % peers) for i in range(peers)])  9.96 us
    ppermute x2, waiting for transfers between devices, pair(): return lax.ppermute(value, axis, pairs + [(j, i) for i, j in pairs])  5.71 us
    pallas_call x1, Pallas kernels, sent_grams(): pl.pallas_call(sent_kernel, grid=(PATCHES,), in_specs=gram_specs(), out_s...  5.13 us
    pallas_call x1, Pallas kernels, kept_grams(): pl.pallas_call(kept_kernel, grid=(PATCHES,), in_specs=gram_specs(), out_s...  5.06 us
    all_to_all x2, waiting for transfers between devices, swap(): return lax.all_to_all(value, 'mem', split_axis=0, concat_axis=0, tiled=True)  2.85 us
  transfers between devices with their start and end apart: 13, of which 7 were waited for; matrix products, arithmetic and copies ran while one was open for 0% of the time, Pallas kernels for 37%

profile of v3, /device:TPU:26, one launch (start us, length us, event | category | flops | bytes accessed | tf_op | source)
XLA Modules:
  0.0 85.7 jit_solution(15278718065688718423)
XLA Ops:
  0.0 8.6 %all-to-all-start = ((bf16[8,4,32,640]{3,2,1,0:T(8,128)(2,1)}), bf16[8,4,32,640]{3,2,1,0:T(8,128)(2,1)S(1)}, u32[]{:S(2)}, u32[]{:S(2)}) async-start(bf16[8,4,32,640]{3,2,1,0:T(8,128)(2,1)} %bitcast.8), calls=%async_computation | async-start | bytes 2621440 | tf_op jit(solution)/shard_map/all_to_all | solution.py:344
  8.7 0.0 copy-start
  8.7 2.2 %copy-done = bf16[1,4,2048,256]{3,2,1,0:T(8,128)(2,1)S(1)} copy-done((bf16[1,4,2048,256]{3,2,1,0:T(8,128)(2,1)S(1)}, bf16[1,4,2048,256]{3,2,1,0:T(8,128)(2,1)}, u32[]{:S(2)}) %copy-start) | copy-done | bytes 4194328
  10.9 5.1 %sent_grams.1 = (f32[4,264,256]{2,1,0:T(8,128)S(1)}, f32[4,264,256]{2,1,0:T(8,128)S(1)}, f32[1,264,256]{2,1,0:T(8,128)S(1)}, f32[1,264,256]{2,1,0:T(8,128)S(1)}) custom-call(s32[4]{0:T(128)S(1)} %bitcast.6, bf16[1,4,2048,256]{3,2,1,0:T(8,128)(2,1)S(1)} %copy-done, bf16[1,4,2048]{2,1,0:T(4,128)(2,1)S(1)} %copy-done.2, bf16[1,4,2048]{2,1,0:T(4,128)(2,1)S(1)} %copy-done.3, ...), custom_call_target="tpu_custom_call" | custom-call | flops 1000 | bytes 1000 | tf_op jit(solution)/shard_map/sent_grams/pallas_call | solution.py:133
  16.0 0.1 collective-permute-start
  16.1 0.6 collective-permute-start.1
  16.7 2.0 %collective-permute-start.2 = (f32[1,264,256]{2,1,0:T(8,128)S(1)}, f32[1,264,256]{2,1,0:T(8,128)S(1)}, u32[]{:S(2)}, u32[]{:S(2)}) collective-permute-start(f32[1,264,256]{2,1,0:T(8,128)S(1)} %get-tuple-element.23), channel_id=1, source_target_pairs={{0,32},{32,64},{64,96},{96,128},{128,160},{160,192},{192,224},{224... | collective-permute-start | bytes 811016 | tf_op jit(solution)/shard_map/ppermute | solution.py:349
  18.8 1.2 %collective-permute-start.3 = (f32[1,264,256]{2,1,0:T(8,128)S(1)}, f32[1,264,256]{2,1,0:T(8,128)S(1)}, u32[]{:S(2)}, u32[]{:S(2)}) collective-permute-start(f32[1,264,256]{2,1,0:T(8,128)S(1)} %get-tuple-element.24), channel_id=1, source_target_pairs={{0,224},{32,0},{64,32},{96,64},{128,96},{160,128},{192,160},{224,1... | collective-permute-start | bytes 811016 | tf_op jit(solution)/shard_map/ppermute | solution.py:349
  20.0 5.1 %kept_grams.1.refs_0_ = f32[4,264,256]{2,1,0:T(8,128)S(1)} custom-call(s32[4]{0:T(128)S(1)} %bitcast.7, bf16[1,4,2048,256]{3,2,1,0:T(8,128)(2,1)S(1)} %copy-done, bf16[1,4,2048]{2,1,0:T(4,128)(2,1)S(1)} %copy-done.2, bf16[1,4,2048]{2,1,0:T(4,128)(2,1)S(1)} %copy-done.3, bf16[1,5,4,2048]{3,2,1,0:T(4,128)(2,1)S(1)} %bitcast.5), custom_call_target="tpu_custom_call" | custom-call | flops 1000 | bytes 1000 | tf_op jit(solution)/shard_map/kept_grams/pallas_call | solution.py:147
  25.0 0.0 collective-permute-done.refs_1_
  25.0 5.7 %collective-permute-done.1.refs_2_ = f32[4,264,256]{2,1,0:T(8,128)S(1)} collective-permute-done((f32[4,264,256]{2,1,0:T(8,128)S(1)}, f32[4,264,256]{2,1,0:T(8,128)S(1)}, u32[]{:S(2)}, u32[]{:S(2)}) %collective-permute-start.1) | collective-permute-done | bytes 1081376 | tf_op jit(solution)/shard_map/ppermute | solution.py:355
  30.8 9.6 %root_weights.2 = (bf16[2,256,256]{2,1,0:T(8,128)(2,1)S(1)}, f32[2,264,256]{2,1,0:T(8,128)S(1)}) custom-call(f32[4,264,256]{2,1,0:T(8,128)S(1)} %kept_grams.1.refs_0_, f32[4,264,256]{2,1,0:T(8,128)S(1)} %collective-permute-done.refs_1_, f32[4,264,256]{2,1,0:T(8,128)S(1)} %collective-permute-done.1.refs_2_), custom_call_target="tpu_custom_call" | custom-call | flops 2000000000 | bytes 1000 | tf_op jit(solution)/shard_map/root_weights/pallas_call | solution.py:247
  40.3 2.9 %all-to-all-done.states = bf16[8,4,32,640]{3,2,1,0:T(8,128)(2,1)S(1)} async-done(((bf16[8,4,32,640]{3,2,1,0:T(8,128)(2,1)}), bf16[8,4,32,640]{3,2,1,0:T(8,128)(2,1)S(1)}, u32[]{:S(2)}, u32[]{:S(2)}) %all-to-all-start) | async-done | bytes 1310752 | tf_op jit(solution)/shard_map/all_to_all | solution.py:344
  43.2 1.6 %apply_weights.2 = bf16[8,2,32,640]{3,2,1,0:T(8,128)(2,1)} custom-call(bf16[2,256,256]{2,1,0:T(8,128)(2,1)S(1)} %get-tuple-element.22.flipped_ref, bf16[8,4,32,640]{3,2,1,0:T(8,128)(2,1)S(1)} %all-to-all-done.states), custom_call_target="tpu_custom_call" | custom-call | flops 1000 | bytes 1000 | tf_op jit(solution)/shard_map/apply_weights/pallas_call | solution.py:302
  44.8 1.3 %collective-permute-done.2.refs_1_ = f32[1,264,256]{2,1,0:T(8,128)S(1)} collective-permute-done((f32[1,264,256]{2,1,0:T(8,128)S(1)}, f32[1,264,256]{2,1,0:T(8,128)S(1)}, u32[]{:S(2)}, u32[]{:S(2)}) %collective-permute-start.2) | collective-permute-done | bytes 270368 | tf_op jit(solution)/shard_map/ppermute | solution.py:349
  46.1 4.7 %all-to-all-start.1 = ((bf16[8,2,32,640]{3,2,1,0:T(8,128)(2,1)}), bf16[8,2,32,640]{3,2,1,0:T(8,128)(2,1)S(1)}, u32[]{:S(2)}, u32[]{:S(2)}) async-start(bf16[8,2,32,640]{3,2,1,0:T(8,128)(2,1)} %apply_weights.2), calls=%async_computation.1 | async-start | bytes 1310720 | tf_op jit(solution)/shard_map/all_to_all | solution.py:344
  50.7 9.1 %root_weights.3.flipped_ref = bf16[2,256,256]{2,1,0:T(8,128)(2,1)S(1)} custom-call(f32[2,264,256]{2,1,0:T(8,128)S(1)} %get-tuple-element.26.refs_0_, f32[1,264,256]{2,1,0:T(8,128)S(1)} %collective-permute-done.2.refs_1_, f32[1,264,256]{2,1,0:T(8,128)S(1)} %collective-permute-done.3.refs_2_), custom_call_target="tpu_custom_call" | custom-call | flops 2000000000 | bytes 1000 | tf_op jit(solution)/shard_map/root_weights/pallas_call | solution.py:247
  59.9 0.8 apply_weights.3
  60.7 4.2 %collective-permute-start.5 = (bf16[4,32,640]{2,1,0:T(8,128)(2,1)S(1)}, bf16[4,32,640]{2,1,0:T(8,128)(2,1)S(1)}, u32[]{:S(2)}, u32[]{:S(2)}) collective-permute-start(bf16[4,32,640]{2,1,0:T(8,128)(2,1)S(1)} %get-tuple-element.31), channel_id=1, source_target_pairs={{0,192},{32,224},{64,0},{96,32},{128,64},{160,96},{192,128},{224,1... | collective-permute-start | bytes 491528 | tf_op jit(solution)/shard_map/ppermute | solution.py:349
  64.9 0.8 collective-permute-start.6
  65.7 2.4 %collective-permute-start.7 = (bf16[2,32,640]{2,1,0:T(8,128)(2,1)S(1)}, bf16[2,32,640]{2,1,0:T(8,128)(2,1)S(1)}, u32[]{:S(2)}, u32[]{:S(2)}) collective-permute-start(bf16[2,32,640]{2,1,0:T(8,128)(2,1)S(1)} %get-tuple-element.33), channel_id=1, source_target_pairs={{0,224},{32,0},{64,32},{96,64},{128,96},{160,128},{192,160},{224,1... | collective-permute-start | bytes 245768 | tf_op jit(solution)/shard_map/ppermute | solution.py:349
  68.1 4.7 %collective-permute-start.8 = (bf16[2,32,640]{2,1,0:T(8,128)(2,1)S(1)}, bf16[2,32,640]{2,1,0:T(8,128)(2,1)S(1)}, u32[]{:S(2)}, u32[]{:S(2)}) collective-permute-start(bf16[2,32,640]{2,1,0:T(8,128)(2,1)S(1)} %get-tuple-element.34), channel_id=1, source_target_pairs={{0,128},{32,160},{64,192},{96,224},{128,0},{160,32},{192,64},{224,... | collective-permute-start | bytes 245768 | tf_op jit(solution)/shard_map/ppermute | solution.py:349
  72.9 3.0 %collective-permute-done.5.c6 = bf16[4,32,640]{2,1,0:T(8,128)(2,1)S(1)} collective-permute-done((bf16[4,32,640]{2,1,0:T(8,128)(2,1)S(1)}, bf16[4,32,640]{2,1,0:T(8,128)(2,1)S(1)}, u32[]{:S(2)}, u32[]{:S(2)}) %collective-permute-start.5) | collective-permute-done | bytes 163872 | tf_op jit(solution)/shard_map/ppermute | solution.py:349
  75.9 2.4 %collective-permute-start.10 = (bf16[2,32,640]{2,1,0:T(8,128)(2,1)S(1)}, bf16[2,32,640]{2,1,0:T(8,128)(2,1)S(1)}, u32[]{:S(2)}, u32[]{:S(2)}) collective-permute-start(bf16[2,32,640]{2,1,0:T(8,128)(2,1)S(1)} %slice.9), channel_id=1, source_target_pairs={{0,224},{32,0},{64,32},{96,64},{128,96},{160,128},{192,160},{224,1... | collective-permute-start | bytes 245768 | tf_op jit(solution)/shard_map/ppermute | solution.py:349
  78.3 0.3 collective-permute-start.9
  78.6 0.4 collective-permute-done.6.c1
  79.0 0.0 collective-permute-done.7.c7
  79.0 4.9 %collective-permute-done.8.c4 = bf16[2,32,640]{2,1,0:T(8,128)(2,1)S(1)} collective-permute-done((bf16[2,32,640]{2,1,0:T(8,128)(2,1)S(1)}, bf16[2,32,640]{2,1,0:T(8,128)(2,1)S(1)}, u32[]{:S(2)}, u32[]{:S(2)}) %collective-permute-start.8) | collective-permute-done | bytes 81952 | tf_op jit(solution)/shard_map/ppermute | solution.py:349
  83.9 0.0 collective-permute-done.10.c5
  83.9 0.3 collective-permute-done.9.c3
  84.2 0.0 all-to-all-done.1.first
  84.3 1.2 %gather.1 = bf16[8,4,32,640]{3,2,1,0:T(8,128)(2,1)} custom-call(bf16[8,2,32,640]{3,2,1,0:T(8,128)(2,1)S(1)} %all-to-all-done.1.first, bf16[2,32,640]{2,1,0:T(8,128)(2,1)S(1)} %get-tuple-element.29.c0, bf16[4,32,640]{2,1,0:T(8,128)(2,1)S(1)} %collective-permute-done.4.c2, bf16[4,32,640]{2,1,0:T(8,128)(2,1)S(1)} %collective-permute-done.5.c6, ...), custom_call_target="tpu_custom_call" | custom-call | flops 1000 | bytes 1000 | tf_op jit(solution)/shard_map/gather/pallas_call | solution.py:331
  (13 shorter events, 0.0 us)
Async XLA Ops:
  0.0 8.6 %copy-start.1 = (bf16[1,4,5,2048]{3,1,2,0:T(4,128)(2,1)S(1)}, bf16[1,4,5,2048]{3,1,2,0:T(4,128)(2,1)}, u32[]{:S(2)}) copy-start(bf16[1,4,5,2048]{3,1,2,0:T(4,128)(2,1)} %param.10) | copy-start | bytes 245764
  0.0 8.6 %copy-start.2 = (bf16[1,4,2048]{2,1,0:T(4,128)(2,1)S(1)}, bf16[1,4,2048]{2,1,0:T(4,128)(2,1)}, u32[]{:S(2)}) copy-start(bf16[1,4,2048]{2,1,0:T(4,128)(2,1)} %innov_ref.3) | copy-start | bytes 49156
  0.0 8.6 %copy-start.3 = (bf16[1,4,2048]{2,1,0:T(4,128)(2,1)S(1)}, bf16[1,4,2048]{2,1,0:T(4,128)(2,1)}, u32[]{:S(2)}) copy-start(bf16[1,4,2048]{2,1,0:T(4,128)(2,1)} %prec_ref.3) | copy-start | bytes 49156
  0.0 8.6 %copy-start.4 = (s32[1,4]{1,0:T(1,128)S(1)}, s32[1,4]{1,0:T(1,128)}, u32[]{:S(2)}) copy-start(s32[1,4]{1,0:T(1,128)} %param.11) | copy-start | bytes 52
  0.0 43.2 %all-to-all-start = ((bf16[8,4,32,640]{3,2,1,0:T(8,128)(2,1)}), bf16[8,4,32,640]{3,2,1,0:T(8,128)(2,1)S(1)}, u32[]{:S(2)}, u32[]{:S(2)}) async-start(bf16[8,4,32,640]{3,2,1,0:T(8,128)(2,1)} %bitcast.8), calls=%async_computation | async-start | bytes 2621440 | tf_op jit(solution)/shard_map/all_to_all | solution.py:344
  8.7 2.2 %copy-start = (bf16[1,4,2048,256]{3,2,1,0:T(8,128)(2,1)S(1)}, bf16[1,4,2048,256]{3,2,1,0:T(8,128)(2,1)}, u32[]{:S(2)}) copy-start(bf16[1,4,2048,256]{3,2,1,0:T(8,128)(2,1)} %ens_ref.3) | copy-start | bytes 12582916
  16.0 9.0 %collective-permute-start = (f32[4,264,256]{2,1,0:T(8,128)S(1)}, f32[4,264,256]{2,1,0:T(8,128)S(1)}, u32[]{:S(2)}, u32[]{:S(2)}) collective-permute-start(f32[4,264,256]{2,1,0:T(8,128)S(1)} %get-tuple-element.20), channel_id=1, source_target_pairs={{0,1},{2,3},{4,5},{6,7},{8,9},{10,11},{12,13},{14,15},{16,17},{18,... | collective-permute-start | bytes 3244040 | tf_op jit(solution)/shard_map/ppermute | solution.py:355
  16.1 14.7 %collective-permute-start.1 = (f32[4,264,256]{2,1,0:T(8,128)S(1)}, f32[4,264,256]{2,1,0:T(8,128)S(1)}, u32[]{:S(2)}, u32[]{:S(2)}) collective-permute-start(f32[4,264,256]{2,1,0:T(8,128)S(1)} %get-tuple-element.21), channel_id=1, source_target_pairs={{1,2},{3,4},{5,6},{7,8},{9,10},{11,12},{13,14},{15,16},{17,18},{19... | collective-permute-start | bytes 3244040 | tf_op jit(solution)/shard_map/ppermute | solution.py:355
  16.7 29.3 %collective-permute-start.2 = (f32[1,264,256]{2,1,0:T(8,128)S(1)}, f32[1,264,256]{2,1,0:T(8,128)S(1)}, u32[]{:S(2)}, u32[]{:S(2)}) collective-permute-start(f32[1,264,256]{2,1,0:T(8,128)S(1)} %get-tuple-element.23), channel_id=1, source_target_pairs={{0,32},{32,64},{64,96},{96,128},{128,160},{160,192},{192,224},{224... | collective-permute-start | bytes 811016 | tf_op jit(solution)/shard_map/ppermute | solution.py:349
  18.8 27.3 %collective-permute-start.3 = (f32[1,264,256]{2,1,0:T(8,128)S(1)}, f32[1,264,256]{2,1,0:T(8,128)S(1)}, u32[]{:S(2)}, u32[]{:S(2)}) collective-permute-start(f32[1,264,256]{2,1,0:T(8,128)S(1)} %get-tuple-element.24), channel_id=1, source_target_pairs={{0,224},{32,0},{64,32},{96,64},{128,96},{160,128},{192,160},{224,1... | collective-permute-start | bytes 811016 | tf_op jit(solution)/shard_map/ppermute | solution.py:349
  46.1 38.2 %all-to-all-start.1 = ((bf16[8,2,32,640]{3,2,1,0:T(8,128)(2,1)}), bf16[8,2,32,640]{3,2,1,0:T(8,128)(2,1)S(1)}, u32[]{:S(2)}, u32[]{:S(2)}) async-start(bf16[8,2,32,640]{3,2,1,0:T(8,128)(2,1)} %apply_weights.2), calls=%async_computation.1 | async-start | bytes 1310720 | tf_op jit(solution)/shard_map/all_to_all | solution.py:344
  60.7 15.2 %collective-permute-start.5 = (bf16[4,32,640]{2,1,0:T(8,128)(2,1)S(1)}, bf16[4,32,640]{2,1,0:T(8,128)(2,1)S(1)}, u32[]{:S(2)}, u32[]{:S(2)}) collective-permute-start(bf16[4,32,640]{2,1,0:T(8,128)(2,1)S(1)} %get-tuple-element.31), channel_id=1, source_target_pairs={{0,192},{32,224},{64,0},{96,32},{128,64},{160,96},{192,128},{224,1... | collective-permute-start | bytes 491528 | tf_op jit(solution)/shard_map/ppermute | solution.py:349
  64.9 13.4 %collective-permute-start.4 = (bf16[4,32,640]{2,1,0:T(8,128)(2,1)S(1)}, bf16[4,32,640]{2,1,0:T(8,128)(2,1)S(1)}, u32[]{:S(2)}, u32[]{:S(2)}) collective-permute-start(bf16[4,32,640]{2,1,0:T(8,128)(2,1)S(1)} %get-tuple-element.30), channel_id=1, source_target_pairs={{0,64},{32,96},{64,128},{96,160},{128,192},{160,224},{192,0},{224,... | collective-permute-start | bytes 491528 | tf_op jit(solution)/shard_map/ppermute | solution.py:349
  64.9 14.1 %collective-permute-start.6 = (bf16[2,32,640]{2,1,0:T(8,128)(2,1)S(1)}, bf16[2,32,640]{2,1,0:T(8,128)(2,1)S(1)}, u32[]{:S(2)}, u32[]{:S(2)}) collective-permute-start(bf16[2,32,640]{2,1,0:T(8,128)(2,1)S(1)} %get-tuple-element.32), channel_id=1, source_target_pairs={{0,32},{32,64},{64,96},{96,128},{128,160},{160,192},{192,224},{224... | collective-permute-start | bytes 245768 | tf_op jit(solution)/shard_map/ppermute | solution.py:349
  65.7 13.3 %collective-permute-start.7 = (bf16[2,32,640]{2,1,0:T(8,128)(2,1)S(1)}, bf16[2,32,640]{2,1,0:T(8,128)(2,1)S(1)}, u32[]{:S(2)}, u32[]{:S(2)}) collective-permute-start(bf16[2,32,640]{2,1,0:T(8,128)(2,1)S(1)} %get-tuple-element.33), channel_id=1, source_target_pairs={{0,224},{32,0},{64,32},{96,64},{128,96},{160,128},{192,160},{224,1... | collective-permute-start | bytes 245768 | tf_op jit(solution)/shard_map/ppermute | solution.py:349
  68.1 15.8 %collective-permute-start.8 = (bf16[2,32,640]{2,1,0:T(8,128)(2,1)S(1)}, bf16[2,32,640]{2,1,0:T(8,128)(2,1)S(1)}, u32[]{:S(2)}, u32[]{:S(2)}) collective-permute-start(bf16[2,32,640]{2,1,0:T(8,128)(2,1)S(1)} %get-tuple-element.34), channel_id=1, source_target_pairs={{0,128},{32,160},{64,192},{96,224},{128,0},{160,32},{192,64},{224,... | collective-permute-start | bytes 245768 | tf_op jit(solution)/shard_map/ppermute | solution.py:349
  75.9 8.1 %collective-permute-start.10 = (bf16[2,32,640]{2,1,0:T(8,128)(2,1)S(1)}, bf16[2,32,640]{2,1,0:T(8,128)(2,1)S(1)}, u32[]{:S(2)}, u32[]{:S(2)}) collective-permute-start(bf16[2,32,640]{2,1,0:T(8,128)(2,1)S(1)} %slice.9), channel_id=1, source_target_pairs={{0,224},{32,0},{64,32},{96,64},{128,96},{160,128},{192,160},{224,1... | collective-permute-start | bytes 245768 | tf_op jit(solution)/shard_map/ppermute | solution.py:349
  78.3 6.0 %collective-permute-start.9 = (bf16[2,32,640]{2,1,0:T(8,128)(2,1)S(1)}, bf16[2,32,640]{2,1,0:T(8,128)(2,1)S(1)}, u32[]{:S(2)}, u32[]{:S(2)}) collective-permute-start(bf16[2,32,640]{2,1,0:T(8,128)(2,1)S(1)} %slice.8), channel_id=1, source_target_pairs={{0,32},{32,64},{64,96},{96,128},{128,160},{160,192},{192,224},{224... | collective-permute-start | bytes 245768 | tf_op jit(solution)/shard_map/ppermute | solution.py:349

commit v4 on v3

--- a/solution.py
+++ b/solution.py
@@ -18,6 +18,8 @@
 SLOTS = 2048
 PEERS = 8
 EXT = K + 8
+HALF = K // 2
+EDGE = HALF + 8
 VMEM = pl.BlockSpec(memory_space=pltpu.VMEM)
 SMEM = pl.BlockSpec(memory_space=pltpu.SMEM)
 ANY = pl.BlockSpec(memory_space=pl.ANY)
@@ -63,29 +65,55 @@
     return pairs
 
 
+def upper_lower(n):
+    row = lax.broadcasted_iota(jnp.int32, (n, n), 0)
+    col = lax.broadcasted_iota(jnp.int32, (n, n), 1)
+    return row <= col, row == col
+
+
+def diagonal(gram):
+    return jnp.sum(jnp.where(upper_lower(K)[1], gram, 0.0), axis=0, keepdims=True)
+
+
+def unpacked(packed, diag):
+    upper, same = upper_lower(packed.shape[0])
+    flipped = packed.T
+    return jnp.where(upper, packed, flipped), jnp.where(same, diag, jnp.where(upper, flipped, packed))
+
+
+def unfolded(ref):
+    ahead, behind = unpacked(ref[0:HALF, 0:HALF], ref[HALF + 1 : HALF + 2, HALF:])
+    across = ref[0:HALF, HALF:]
+    return jnp.concatenate(
+        [jnp.concatenate([ahead, across], axis=1), jnp.concatenate([across.T, behind], axis=1)], axis=0
+    )
+
+
 def sent_kernel(count_ref, ens_ref, innov_ref, prec_ref, taper_ref, near_ref, far_ref, next_ref, prev_ref, flipped_ref):
-    p = pl.program_id(0)
     even = lax.rem(lax.axis_index("reg"), 2) == 0
-    weights = slot_weights(p, count_ref, prec_ref, taper_ref)
-    sided = [jnp.where(even, weights[1], weights[2]), jnp.where(even, weights[2], weights[1])]
-    innov = pick_row(innov_ref[0], p)
-
-    def store(rows, refs):
-        for (gram, drive), ref in zip(weighted_grams(ens_ref, flipped_ref, rows, innov), refs):
-            ref[0, 0:K, :] = gram
-            ref[0, K:EXT, :] = jnp.broadcast_to(drive, (EXT - K, K))
-
-    @pl.when(p == 0)
-    def _():
-        store(sided + [weights[4]], (near_ref, far_ref, prev_ref))
-
-    @pl.when((p > 0) & (p < PATCHES - 1))
-    def _():
-        store(sided, (near_ref, far_ref))
-
-    @pl.when(p == PATCHES - 1)
-    def _():
-        store(sided + [weights[3]], (near_ref, far_ref, next_ref))
+    for p in range(PATCHES):
+
+        @pl.when(pl.program_id(0) == p)
+        def _():
+            weights = slot_weights(p, count_ref, prec_ref, taper_ref)
+            rows = [jnp.where(even, weights[1], weights[2]), jnp.where(even, weights[2], weights[1])]
+            rows += {0: [weights[4]], PATCHES - 1: [weights[3]]}.get(p, [])
+            (near, near_drive), (far, far_drive), *edge = weighted_grams(ens_ref, flipped_ref, rows, pick_row(innov_ref[0], p))
+            near_ref[0, 0:K, :] = near
+            near_ref[0, K:EXT, :] = jnp.broadcast_to(near_drive, (EXT - K, K))
+            if p < 2:
+                far_ref[p, 0:K, :] = far
+                far_ref[p, K:EXT, :] = jnp.broadcast_to(far_drive, (EXT - K, K))
+            else:
+                at = PATCHES - 1 - p
+                far_ref[at, 0:K, :] = jnp.where(upper_lower(K)[0], far_ref[at, 0:K, :], far)
+                far_ref[at, K + 1 : K + 2, :] = far_drive
+                far_ref[at, K + 2 : K + 3, :] = diagonal(far)
+            for (gram, drive), ref in zip(edge, (next_ref if p else prev_ref,)):
+                ref[0, 0:HALF, 0:HALF] = jnp.where(upper_lower(HALF)[0], gram[0:HALF, 0:HALF], gram[HALF:, HALF:])
+                ref[0, 0:HALF, HALF:] = gram[0:HALF, HALF:]
+                ref[0, HALF:, :] = jnp.broadcast_to(drive, (EDGE - HALF, K))
+                ref[0, HALF + 1 : HALF + 2, :] = diagonal(gram)
 
 
 def kept_kernel(count_ref, ens_ref, innov_ref, prec_ref, taper_ref, own_ref, flipped_ref):
@@ -129,13 +157,15 @@
 
 def sent_grams(*args):
     full = jax.ShapeDtypeStruct((PATCHES, EXT, K), F32)
-    one = jax.ShapeDtypeStruct((1, EXT, K), F32)
+    two = jax.ShapeDtypeStruct((2, EXT, K), F32)
+    one = jax.ShapeDtypeStruct((1, EDGE, K), F32)
     return pl.pallas_call(
         sent_kernel,
         grid=(PATCHES,),
         in_specs=gram_specs(),
-        out_specs=[pl.BlockSpec((1, EXT, K), lambda p: (p, 0, 0))] * 2 + [pl.BlockSpec((1, EXT, K), lambda p: (0, 0, 0))] * 2,
-        out_shape=[full, full, one, one],
+        out_specs=[pl.BlockSpec((1, EXT, K), lambda p: (p, 0, 0)), pl.BlockSpec((2, EXT, K), lambda p: (0, 0, 0))]
+        + [pl.BlockSpec((1, EDGE, K), lambda p: (0, 0, 0))] * 2,
+        out_shape=[full, two, one, one],
         scratch_shapes=[pltpu.VMEM((K + 16, SLOTS), BF16)],
         compiler_params=PARAMS,
         cost_estimate=COST,
@@ -164,36 +194,24 @@
 def root_kernel(edges, *refs):
     n = 2
     if edges:
-        sums, following, previous, out_ref, *rest = refs
-        pairs = [[(sums, 0, 0, 0), (following, 0, 1, 0)], [(sums, 1, 0, 1), (previous, 0, 1, 1)]]
+        sums, following, previous, out_ref, total_s, edge_s, *rest = refs
+        sources = [(sums, total_s), (following, edge_s.at[pl.ds(0, 1)]), (previous, edge_s.at[pl.ds(1, 1)])]
     else:
-        *parts, out_ref, sums_ref, rest_s, rest_sems = refs[:5] + refs[-2:]
-        rest = refs[5:-2]
-        pairs = [[(ref, p, w, i) for w, ref in enumerate(parts)] for i, p in enumerate(INNER)]
-    held, sems, yh, yl, zh, zl, sh, sl, diag_ref, scale_ref = rest
+        own, near, far, out_ref, sums_ref, total_s, own_s, near_s, far_s, *rest = refs
+        sources = [(own, own_s), (near, near_s), (far, far_s)]
+    sems, yh, yl, zh, zl, sh, sl, diag_ref, scale_ref = rest
     y, z, s = (yh, yl), (zh, zl), (sh, sl)
-    copies = [
-        [pltpu.make_async_copy(ref.at[at], held.at[w, i], sems.at[p, j]) for j, (ref, at, w, i) in enumerate(pairs[p])]
-        for p in range(n)
-    ]
-    for p in range(n):
-        start_all(copies[p])
-    if not edges:
-        others = [
-            pltpu.make_async_copy(ref.at[p], rest_s.at[w, i], rest_sems.at[w, i])
-            for w, ref in enumerate(parts)
-            for i, p in enumerate(OUTER)
-        ]
-        start_all(others)
+    copies = [pltpu.make_async_copy(a, b, sems.at[i]) for i, (a, b) in enumerate(sources)]
+    start_all(copies)
     row = lax.broadcasted_iota(jnp.int32, (K, K), 0)
     col = lax.broadcasted_iota(jnp.int32, (K, K), 1)
     diag_ref[...] = jnp.where(row == col, 1.5, 0.0).astype(F32)
 
-    def total(p, part):
-        value = held[0, p, part, :]
-        for w in range(1, held.shape[0]):
-            value = value + held[w, p, part, :]
-        return value
+    def add_up(ref, patches, pair):
+        packed = far_s[pair, 0:K, :]
+        for i, (p, gram) in enumerate(zip(patches, unpacked(packed, far_s[pair, K + 2 : K + 3, :]))):
+            ref[i, 0:K, :] = own_s[p, 0:K, :] + near_s[p, 0:K, :] + gram
+            ref[i, K : K + 1, :] = own_s[p, K : K + 1, :] + near_s[p, K : K + 1, :] + far_s[pair, K + i : K + i + 1, :]
 
     def product(a, b, p):
         ah, al, bh, bl = a[0][p], a[1][p], b[0][p], b[1][p]
@@ -202,10 +220,15 @@
     def residual(p):
         split_to(s, p, diag_ref[...] - 0.5 * product(z, y, p))
 
+    for copy in copies:
+        copy.wait()
+    if not edges:
+        add_up(total_s, INNER, 1)
     for p in range(n):
-        for copy in copies[p]:
-            copy.wait()
-        system = total(p, slice(0, K)) + jnp.where(row == col, float(K - 1), 0.0)
+        if edges:
+            total_s[p, 0:K, :] += unfolded(edge_s.at[p])
+            total_s[p, K : K + 1, :] += edge_s[p, HALF : HALF + 1, :]
+        system = total_s[p, 0:K, :] + jnp.where(row == col, float(K - 1), 0.0)
         bound = jnp.max(jnp.sum(jnp.abs(system), axis=0, keepdims=True), axis=1, keepdims=True)
         scale_ref[p] = jnp.broadcast_to(1.0 / jnp.sqrt(bound), (8, K))
         root = system / bound
@@ -228,31 +251,27 @@
     for p in range(n):
         flipped = product(s, z, p) * scale_ref[p, 0:1, :]
         half = flipped.T
-        inner = jnp.sum(half * total(p, slice(K, K + 1)), axis=1, keepdims=True)
+        inner = jnp.sum(half * total_s[p, K : K + 1, :], axis=1, keepdims=True)
         mean_weight = jnp.sum(flipped * inner, axis=0, keepdims=True)
         out_ref[p] = (jnp.sqrt(float(K - 1)) * flipped + mean_weight).astype(BF16)
     if not edges:
-        for copy in others:
-            copy.wait()
-        for i in range(n):
-            sums_ref[i] = rest_s[0, i] + rest_s[1, i] + rest_s[2, i]
+        add_up(sums_ref, OUTER, 0)
 
 
 def root_weights(edges, *args):
     n = 2
     piece = pltpu.VMEM((n, K, K), BF16)
-    parts = 2 if edges else 3
-    held, sems = pltpu.VMEM((parts, n, EXT, K), F32), pltpu.SemaphoreType.DMA((parts, max(n, parts)))
+    two, full, edge = (pltpu.VMEM(shape, F32) for shape in ((n, EXT, K), (PATCHES, EXT, K), (2, EDGE, K)))
     shapes = [jax.ShapeDtypeStruct((n, K, K), BF16)] + ([] if edges else [jax.ShapeDtypeStruct((n, EXT, K), F32)])
     return pl.pallas_call(
         functools.partial(root_kernel, edges),
         in_specs=[ANY] * len(args),
         out_specs=[VMEM] * len(shapes),
         out_shape=shapes,
-        scratch_shapes=[held, sems]
+        scratch_shapes=([two, edge] if edges else [two, full, full, two])
+        + [pltpu.SemaphoreType.DMA((3,))]
         + [piece] * 6
-        + [pltpu.VMEM((K, K), F32), pltpu.VMEM((n, 8, K), F32)]
-        + ([] if edges else [held, sems]),
+        + [pltpu.VMEM((K, K), F32), pltpu.VMEM((n, 8, K), F32)],
         compiler_params=PARAMS,
         cost_estimate=pl.CostEstimate(flops=ROOT_COST, bytes_accessed=1000, transcendentals=0),
         name="root_weights",

time: 87.2 us -> 83.6 us (0.959); the launches traced: 85.7 us -> 83.4 us
  waiting for transfers between devices: 18.5 us -> 17.4 us
    all_to_all x2, waiting for transfers between devices: 2.85 us -> 9.23 us  [swap(): return lax.all_to_all(value, 'mem', split_axis=0, concat_axis=0, tiled=True)]
    ppermute x2, waiting for transfers between devices: 5.71 us -> 0.01 us  [pair(): return lax.ppermute(value, axis, pairs + [(j, i) for i, j in pairs])]
    ppermute x9, waiting for transfers between devices: 9.96 us -> 8.14 us  [shift(): lax.ppermute(value, axis, [(i, (i + by) % peers) for i in range(peers)])]
    all_to_all x2, starting transfers between devices: 13.3 us -> 12.4 us  [swap(): return lax.all_to_all(value, 'mem', split_axis=0, concat_axis=0, tiled=True)]
  transfers between devices with their start and end apart: 13 -> 13, of which waited for: 7 -> 4; matrix products, arithmetic and copies ran while one was open for 0% -> 0% of each run, Pallas kernels for 37% -> 37%
where the time goes in v4:
time: 83.6 us; the launch traced here: 83.4 us
  Pallas kernels  32.2 us (39%)
  starting transfers between devices  31.3 us (37%)
  waiting for transfers between devices  17.4 us (21%)
  local copies, waits for them, and re-layouts  2.21 us (3%)
    pallas_call x2, Pallas kernels, root_weights(): pl.pallas_call(functools.partial(root_kernel, edges), in_specs=[ANY] * le...  18.7 us
    ppermute x9, starting transfers between devices, shift(): lax.ppermute(value, axis, [(i, (i + by) % peers) for i in range(peers)])  18.2 us
    all_to_all x2, starting transfers between devices, swap(): return lax.all_to_all(value, 'mem', split_axis=0, concat_axis=0, tiled=True)  12.4 us
    all_to_all x2, waiting for transfers between devices, swap(): return lax.all_to_all(value, 'mem', split_axis=0, concat_axis=0, tiled=True)  9.23 us
    ppermute x9, waiting for transfers between devices, shift(): lax.ppermute(value, axis, [(i, (i + by) % peers) for i in range(peers)])  8.14 us
    pallas_call x1, Pallas kernels, kept_grams(): pl.pallas_call(kept_kernel, grid=(PATCHES,), in_specs=gram_specs(), out_s...  5.06 us
    pallas_call x1, Pallas kernels, sent_grams(): pl.pallas_call(sent_kernel, grid=(PATCHES,), in_specs=gram_specs(), out_s...  4.72 us
    pallas_call x2, Pallas kernels, apply_weights(): pl.pallas_call(functools.partial(apply_kernel, patches), in_specs=[VMEM,...  2.41 us
  transfers between devices with their start and end apart: 13, of which 4 were waited for; matrix products, arithmetic and copies ran while one was open for 0% of the time, Pallas kernels for 37%

profile of v4, /device:TPU:26, one launch (start us, length us, event | category | flops | bytes accessed | tf_op | source)
XLA Modules:
  0.0 83.4 jit_solution(288058715586336177)
XLA Ops:
  0.0 8.6 %all-to-all-start = ((bf16[8,4,32,640]{3,2,1,0:T(8,128)(2,1)}), bf16[8,4,32,640]{3,2,1,0:T(8,128)(2,1)S(1)}, u32[]{:S(2)}, u32[]{:S(2)}) async-start(bf16[8,4,32,640]{3,2,1,0:T(8,128)(2,1)} %bitcast.8), calls=%async_computation | async-start | bytes 2621440 | tf_op jit(solution)/shard_map/all_to_all | solution.py:363
  8.7 0.0 copy-start
  8.7 2.2 %copy-done = bf16[1,4,2048,256]{3,2,1,0:T(8,128)(2,1)S(1)} copy-done((bf16[1,4,2048,256]{3,2,1,0:T(8,128)(2,1)S(1)}, bf16[1,4,2048,256]{3,2,1,0:T(8,128)(2,1)}, u32[]{:S(2)}) %copy-start) | copy-done | bytes 4194328
  10.9 4.7 %sent_grams.1 = (f32[4,264,256]{2,1,0:T(8,128)S(1)}, f32[2,264,256]{2,1,0:T(8,128)S(1)}, f32[1,136,256]{2,1,0:T(8,128)S(1)}, f32[1,136,256]{2,1,0:T(8,128)S(1)}) custom-call(s32[4]{0:T(128)S(1)} %bitcast.6, bf16[1,4,2048,256]{3,2,1,0:T(8,128)(2,1)S(1)} %copy-done, bf16[1,4,2048]{2,1,0:T(4,128)(2,1)S(1)} %copy-done.2, bf16[1,4,2048]{2,1,0:T(4,128)(2,1)S(1)} %copy-done.3, ...), custom_call_target="tpu_custom_call" | custom-call | flops 1000 | bytes 1000 | tf_op jit(solution)/shard_map/sent_grams/pallas_call | solution.py:162
  15.6 0.1 collective-permute-start
  15.7 0.6 collective-permute-start.1
  16.3 2.0 %collective-permute-start.2 = (f32[1,136,256]{2,1,0:T(8,128)S(1)}, f32[1,136,256]{2,1,0:T(8,128)S(1)}, u32[]{:S(2)}, u32[]{:S(2)}) collective-permute-start(f32[1,136,256]{2,1,0:T(8,128)S(1)} %get-tuple-element.23), channel_id=1, source_target_pairs={{0,32},{32,64},{64,96},{96,128},{128,160},{160,192},{192,224},{224... | collective-permute-start | bytes 417800 | tf_op jit(solution)/shard_map/ppermute | solution.py:368
  18.3 1.2 %collective-permute-start.3 = (f32[1,136,256]{2,1,0:T(8,128)S(1)}, f32[1,136,256]{2,1,0:T(8,128)S(1)}, u32[]{:S(2)}, u32[]{:S(2)}) collective-permute-start(f32[1,136,256]{2,1,0:T(8,128)S(1)} %get-tuple-element.24), channel_id=1, source_target_pairs={{0,224},{32,0},{64,32},{96,64},{128,96},{160,128},{192,160},{224,1... | collective-permute-start | bytes 417800 | tf_op jit(solution)/shard_map/ppermute | solution.py:368
  19.6 5.1 %kept_grams.1.refs_0_ = f32[4,264,256]{2,1,0:T(8,128)S(1)} custom-call(s32[4]{0:T(128)S(1)} %bitcast.7, bf16[1,4,2048,256]{3,2,1,0:T(8,128)(2,1)S(1)} %copy-done, bf16[1,4,2048]{2,1,0:T(4,128)(2,1)S(1)} %copy-done.2, bf16[1,4,2048]{2,1,0:T(4,128)(2,1)S(1)} %copy-done.3, bf16[1,5,4,2048]{3,2,1,0:T(4,128)(2,1)S(1)} %bitcast.5), custom_call_target="tpu_custom_call" | custom-call | flops 1000 | bytes 1000 | tf_op jit(solution)/shard_map/kept_grams/pallas_call | solution.py:177
  24.6 0.0 collective-permute-done.1.refs_2_
  24.6 9.3 %root_weights.2 = (bf16[2,256,256]{2,1,0:T(8,128)(2,1)S(1)}, f32[2,264,256]{2,1,0:T(8,128)S(1)}) custom-call(f32[4,264,256]{2,1,0:T(8,128)S(1)} %kept_grams.1.refs_0_, f32[4,264,256]{2,1,0:T(8,128)S(1)} %collective-permute-done.refs_1_, f32[2,264,256]{2,1,0:T(8,128)S(1)} %collective-permute-done.1.refs_2_), custom_call_target="tpu_custom_call" | custom-call | flops 2000000000 | bytes 1000 | tf_op jit(solution)/shard_map/root_weights/pallas_call | solution.py:266
  34.0 9.2 %all-to-all-done.states = bf16[8,4,32,640]{3,2,1,0:T(8,128)(2,1)S(1)} async-done(((bf16[8,4,32,640]{3,2,1,0:T(8,128)(2,1)}), bf16[8,4,32,640]{3,2,1,0:T(8,128)(2,1)S(1)}, u32[]{:S(2)}, u32[]{:S(2)}) %all-to-all-start) | async-done | bytes 1310752 | tf_op jit(solution)/shard_map/all_to_all | solution.py:363
  43.2 1.6 %apply_weights.2 = bf16[8,2,32,640]{3,2,1,0:T(8,128)(2,1)} custom-call(bf16[2,256,256]{2,1,0:T(8,128)(2,1)S(1)} %get-tuple-element.22.flipped_ref, bf16[8,4,32,640]{3,2,1,0:T(8,128)(2,1)S(1)} %all-to-all-done.states), custom_call_target="tpu_custom_call" | custom-call | flops 1000 | bytes 1000 | tf_op jit(solution)/shard_map/apply_weights/pallas_call | solution.py:321
  44.8 0.0 collective-permute-done.2.refs_1_
  44.8 0.0 collective-permute-done.3.refs_2_
  44.8 3.8 %all-to-all-start.1 = ((bf16[8,2,32,640]{3,2,1,0:T(8,128)(2,1)}), bf16[8,2,32,640]{3,2,1,0:T(8,128)(2,1)S(1)}, u32[]{:S(2)}, u32[]{:S(2)}) async-start(bf16[8,2,32,640]{3,2,1,0:T(8,128)(2,1)} %apply_weights.2), calls=%async_computation.1 | async-start | bytes 1310720 | tf_op jit(solution)/shard_map/all_to_all | solution.py:363
  48.6 9.4 %root_weights.3.flipped_ref = bf16[2,256,256]{2,1,0:T(8,128)(2,1)S(1)} custom-call(f32[2,264,256]{2,1,0:T(8,128)S(1)} %get-tuple-element.26.refs_0_, f32[1,136,256]{2,1,0:T(8,128)S(1)} %collective-permute-done.2.refs_1_, f32[1,136,256]{2,1,0:T(8,128)S(1)} %collective-permute-done.3.refs_2_), custom_call_target="tpu_custom_call" | custom-call | flops 2000000000 | bytes 1000 | tf_op jit(solution)/shard_map/root_weights/pallas_call | solution.py:266
  58.0 0.8 apply_weights.3
  58.8 3.9 %collective-permute-start.5 = (bf16[4,32,640]{2,1,0:T(8,128)(2,1)S(1)}, bf16[4,32,640]{2,1,0:T(8,128)(2,1)S(1)}, u32[]{:S(2)}, u32[]{:S(2)}) collective-permute-start(bf16[4,32,640]{2,1,0:T(8,128)(2,1)S(1)} %get-tuple-element.31), channel_id=1, source_target_pairs={{0,192},{32,224},{64,0},{96,32},{128,64},{160,96},{192,128},{224,1... | collective-permute-start | bytes 491528 | tf_op jit(solution)/shard_map/ppermute | solution.py:368
  62.8 0.9 %collective-permute-start.6 = (bf16[2,32,640]{2,1,0:T(8,128)(2,1)S(1)}, bf16[2,32,640]{2,1,0:T(8,128)(2,1)S(1)}, u32[]{:S(2)}, u32[]{:S(2)}) collective-permute-start(bf16[2,32,640]{2,1,0:T(8,128)(2,1)S(1)} %get-tuple-element.32), channel_id=1, source_target_pairs={{0,32},{32,64},{64,96},{96,128},{128,160},{160,192},{192,224},{224... | collective-permute-start | bytes 245768 | tf_op jit(solution)/shard_map/ppermute | solution.py:368
  63.6 2.4 %collective-permute-start.7 = (bf16[2,32,640]{2,1,0:T(8,128)(2,1)S(1)}, bf16[2,32,640]{2,1,0:T(8,128)(2,1)S(1)}, u32[]{:S(2)}, u32[]{:S(2)}) collective-permute-start(bf16[2,32,640]{2,1,0:T(8,128)(2,1)S(1)} %get-tuple-element.33), channel_id=1, source_target_pairs={{0,224},{32,0},{64,32},{96,64},{128,96},{160,128},{192,160},{224,1... | collective-permute-start | bytes 245768 | tf_op jit(solution)/shard_map/ppermute | solution.py:368
  66.0 4.7 %collective-permute-start.8 = (bf16[2,32,640]{2,1,0:T(8,128)(2,1)S(1)}, bf16[2,32,640]{2,1,0:T(8,128)(2,1)S(1)}, u32[]{:S(2)}, u32[]{:S(2)}) collective-permute-start(bf16[2,32,640]{2,1,0:T(8,128)(2,1)S(1)} %get-tuple-element.34), channel_id=1, source_target_pairs={{0,128},{32,160},{64,192},{96,224},{128,0},{160,32},{192,64},{224,... | collective-permute-start | bytes 245768 | tf_op jit(solution)/shard_map/ppermute | solution.py:368
  70.7 2.6 %collective-permute-done.5.c6 = bf16[4,32,640]{2,1,0:T(8,128)(2,1)S(1)} collective-permute-done((bf16[4,32,640]{2,1,0:T(8,128)(2,1)S(1)}, bf16[4,32,640]{2,1,0:T(8,128)(2,1)S(1)}, u32[]{:S(2)}, u32[]{:S(2)}) %collective-permute-start.5) | collective-permute-done | bytes 163872 | tf_op jit(solution)/shard_map/ppermute | solution.py:368
  73.3 2.6 %collective-permute-start.10 = (bf16[2,32,640]{2,1,0:T(8,128)(2,1)S(1)}, bf16[2,32,640]{2,1,0:T(8,128)(2,1)S(1)}, u32[]{:S(2)}, u32[]{:S(2)}) collective-permute-start(bf16[2,32,640]{2,1,0:T(8,128)(2,1)S(1)} %slice.9), channel_id=1, source_target_pairs={{0,224},{32,0},{64,32},{96,64},{128,96},{160,128},{192,160},{224,1... | collective-permute-start | bytes 245768 | tf_op jit(solution)/shard_map/ppermute | solution.py:368
  75.9 0.5 collective-permute-start.9
  76.4 0.5 collective-permute-done.6.c1
  76.9 0.0 collective-permute-done.7.c7
  76.9 5.0 %collective-permute-done.8.c4 = bf16[2,32,640]{2,1,0:T(8,128)(2,1)S(1)} collective-permute-done((bf16[2,32,640]{2,1,0:T(8,128)(2,1)S(1)}, bf16[2,32,640]{2,1,0:T(8,128)(2,1)S(1)}, u32[]{:S(2)}, u32[]{:S(2)}) %collective-permute-start.8) | collective-permute-done | bytes 81952 | tf_op jit(solution)/shard_map/ppermute | solution.py:368
  81.9 0.0 collective-permute-done.10.c5
  81.9 0.0 collective-permute-done.9.c3
  81.9 0.0 all-to-all-done.1.first
  81.9 1.2 %gather.1 = bf16[8,4,32,640]{3,2,1,0:T(8,128)(2,1)} custom-call(bf16[8,2,32,640]{3,2,1,0:T(8,128)(2,1)S(1)} %all-to-all-done.1.first, bf16[2,32,640]{2,1,0:T(8,128)(2,1)S(1)} %get-tuple-element.29.c0, bf16[4,32,640]{2,1,0:T(8,128)(2,1)S(1)} %collective-permute-done.4.c2, bf16[4,32,640]{2,1,0:T(8,128)(2,1)S(1)} %collective-permute-done.5.c6, ...), custom_call_target="tpu_custom_call" | custom-call | flops 1000 | bytes 1000 | tf_op jit(solution)/shard_map/gather/pallas_call | solution.py:350
  (13 shorter events, 0.0 us)
Async XLA Ops:
  0.0 8.6 %copy-start.1 = (bf16[1,4,5,2048]{3,1,2,0:T(4,128)(2,1)S(1)}, bf16[1,4,5,2048]{3,1,2,0:T(4,128)(2,1)}, u32[]{:S(2)}) copy-start(bf16[1,4,5,2048]{3,1,2,0:T(4,128)(2,1)} %param.10) | copy-start | bytes 245764
  0.0 8.6 %copy-start.2 = (bf16[1,4,2048]{2,1,0:T(4,128)(2,1)S(1)}, bf16[1,4,2048]{2,1,0:T(4,128)(2,1)}, u32[]{:S(2)}) copy-start(bf16[1,4,2048]{2,1,0:T(4,128)(2,1)} %innov_ref.3) | copy-start | bytes 49156
  0.0 8.6 %copy-start.3 = (bf16[1,4,2048]{2,1,0:T(4,128)(2,1)S(1)}, bf16[1,4,2048]{2,1,0:T(4,128)(2,1)}, u32[]{:S(2)}) copy-start(bf16[1,4,2048]{2,1,0:T(4,128)(2,1)} %prec_ref.3) | copy-start | bytes 49156
  0.0 8.6 %copy-start.4 = (s32[1,4]{1,0:T(1,128)S(1)}, s32[1,4]{1,0:T(1,128)}, u32[]{:S(2)}) copy-start(s32[1,4]{1,0:T(1,128)} %param.11) | copy-start | bytes 52
  0.0 43.2 %all-to-all-start = ((bf16[8,4,32,640]{3,2,1,0:T(8,128)(2,1)}), bf16[8,4,32,640]{3,2,1,0:T(8,128)(2,1)S(1)}, u32[]{:S(2)}, u32[]{:S(2)}) async-start(bf16[8,4,32,640]{3,2,1,0:T(8,128)(2,1)} %bitcast.8), calls=%async_computation | async-start | bytes 2621440 | tf_op jit(solution)/shard_map/all_to_all | solution.py:363
  8.7 2.2 %copy-start = (bf16[1,4,2048,256]{3,2,1,0:T(8,128)(2,1)S(1)}, bf16[1,4,2048,256]{3,2,1,0:T(8,128)(2,1)}, u32[]{:S(2)}) copy-start(bf16[1,4,2048,256]{3,2,1,0:T(8,128)(2,1)} %ens_ref.3) | copy-start | bytes 12582916
  15.6 9.1 %collective-permute-start = (f32[4,264,256]{2,1,0:T(8,128)S(1)}, f32[4,264,256]{2,1,0:T(8,128)S(1)}, u32[]{:S(2)}, u32[]{:S(2)}) collective-permute-start(f32[4,264,256]{2,1,0:T(8,128)S(1)} %get-tuple-element.20), channel_id=1, source_target_pairs={{0,1},{2,3},{4,5},{6,7},{8,9},{10,11},{12,13},{14,15},{16,17},{18,... | collective-permute-start | bytes 3244040 | tf_op jit(solution)/shard_map/ppermute | solution.py:374
  15.7 8.9 %collective-permute-start.1 = (f32[2,264,256]{2,1,0:T(8,128)S(1)}, f32[2,264,256]{2,1,0:T(8,128)S(1)}, u32[]{:S(2)}, u32[]{:S(2)}) collective-permute-start(f32[2,264,256]{2,1,0:T(8,128)S(1)} %get-tuple-element.21), channel_id=1, source_target_pairs={{1,2},{3,4},{5,6},{7,8},{9,10},{11,12},{13,14},{15,16},{17,18},{19... | collective-permute-start | bytes 1622024 | tf_op jit(solution)/shard_map/ppermute | solution.py:374
  16.3 28.5 %collective-permute-start.2 = (f32[1,136,256]{2,1,0:T(8,128)S(1)}, f32[1,136,256]{2,1,0:T(8,128)S(1)}, u32[]{:S(2)}, u32[]{:S(2)}) collective-permute-start(f32[1,136,256]{2,1,0:T(8,128)S(1)} %get-tuple-element.23), channel_id=1, source_target_pairs={{0,32},{32,64},{64,96},{96,128},{128,160},{160,192},{192,224},{224... | collective-permute-start | bytes 417800 | tf_op jit(solution)/shard_map/ppermute | solution.py:368
  18.3 26.5 %collective-permute-start.3 = (f32[1,136,256]{2,1,0:T(8,128)S(1)}, f32[1,136,256]{2,1,0:T(8,128)S(1)}, u32[]{:S(2)}, u32[]{:S(2)}) collective-permute-start(f32[1,136,256]{2,1,0:T(8,128)S(1)} %get-tuple-element.24), channel_id=1, source_target_pairs={{0,224},{32,0},{64,32},{96,64},{128,96},{160,128},{192,160},{224,1... | collective-permute-start | bytes 417800 | tf_op jit(solution)/shard_map/ppermute | solution.py:368
  44.8 37.1 %all-to-all-start.1 = ((bf16[8,2,32,640]{3,2,1,0:T(8,128)(2,1)}), bf16[8,2,32,640]{3,2,1,0:T(8,128)(2,1)S(1)}, u32[]{:S(2)}, u32[]{:S(2)}) async-start(bf16[8,2,32,640]{3,2,1,0:T(8,128)(2,1)} %apply_weights.2), calls=%async_computation.1 | async-start | bytes 1310720 | tf_op jit(solution)/shard_map/all_to_all | solution.py:363
  58.8 14.4 %collective-permute-start.5 = (bf16[4,32,640]{2,1,0:T(8,128)(2,1)S(1)}, bf16[4,32,640]{2,1,0:T(8,128)(2,1)S(1)}, u32[]{:S(2)}, u32[]{:S(2)}) collective-permute-start(bf16[4,32,640]{2,1,0:T(8,128)(2,1)S(1)} %get-tuple-element.31), channel_id=1, source_target_pairs={{0,192},{32,224},{64,0},{96,32},{128,64},{160,96},{192,128},{224,1... | collective-permute-start | bytes 491528 | tf_op jit(solution)/shard_map/ppermute | solution.py:368
  62.7 13.1 %collective-permute-start.4 = (bf16[4,32,640]{2,1,0:T(8,128)(2,1)S(1)}, bf16[4,32,640]{2,1,0:T(8,128)(2,1)S(1)}, u32[]{:S(2)}, u32[]{:S(2)}) collective-permute-start(bf16[4,32,640]{2,1,0:T(8,128)(2,1)S(1)} %get-tuple-element.30), channel_id=1, source_target_pairs={{0,64},{32,96},{64,128},{96,160},{128,192},{160,224},{192,0},{224,... | collective-permute-start | bytes 491528 | tf_op jit(solution)/shard_map/ppermute | solution.py:368
  62.8 14.2 %collective-permute-start.6 = (bf16[2,32,640]{2,1,0:T(8,128)(2,1)S(1)}, bf16[2,32,640]{2,1,0:T(8,128)(2,1)S(1)}, u32[]{:S(2)}, u32[]{:S(2)}) collective-permute-start(bf16[2,32,640]{2,1,0:T(8,128)(2,1)S(1)} %get-tuple-element.32), channel_id=1, source_target_pairs={{0,32},{32,64},{64,96},{96,128},{128,160},{160,192},{192,224},{224... | collective-permute-start | bytes 245768 | tf_op jit(solution)/shard_map/ppermute | solution.py:368
  63.6 13.3 %collective-permute-start.7 = (bf16[2,32,640]{2,1,0:T(8,128)(2,1)S(1)}, bf16[2,32,640]{2,1,0:T(8,128)(2,1)S(1)}, u32[]{:S(2)}, u32[]{:S(2)}) collective-permute-start(bf16[2,32,640]{2,1,0:T(8,128)(2,1)S(1)} %get-tuple-element.33), channel_id=1, source_target_pairs={{0,224},{32,0},{64,32},{96,64},{128,96},{160,128},{192,160},{224,1... | collective-permute-start | bytes 245768 | tf_op jit(solution)/shard_map/ppermute | solution.py:368
  66.0 15.9 %collective-permute-start.8 = (bf16[2,32,640]{2,1,0:T(8,128)(2,1)S(1)}, bf16[2,32,640]{2,1,0:T(8,128)(2,1)S(1)}, u32[]{:S(2)}, u32[]{:S(2)}) collective-permute-start(bf16[2,32,640]{2,1,0:T(8,128)(2,1)S(1)} %get-tuple-element.34), channel_id=1, source_target_pairs={{0,128},{32,160},{64,192},{96,224},{128,0},{160,32},{192,64},{224,... | collective-permute-start | bytes 245768 | tf_op jit(solution)/shard_map/ppermute | solution.py:368
  73.3 8.7 %collective-permute-start.10 = (bf16[2,32,640]{2,1,0:T(8,128)(2,1)S(1)}, bf16[2,32,640]{2,1,0:T(8,128)(2,1)S(1)}, u32[]{:S(2)}, u32[]{:S(2)}) collective-permute-start(bf16[2,32,640]{2,1,0:T(8,128)(2,1)S(1)} %slice.9), channel_id=1, source_target_pairs={{0,224},{32,0},{64,32},{96,64},{128,96},{160,128},{192,160},{224,1... | collective-permute-start | bytes 245768 | tf_op jit(solution)/shard_map/ppermute | solution.py:368
  75.9 6.1 %collective-permute-start.9 = (bf16[2,32,640]{2,1,0:T(8,128)(2,1)S(1)}, bf16[2,32,640]{2,1,0:T(8,128)(2,1)S(1)}, u32[]{:S(2)}, u32[]{:S(2)}) collective-permute-start(bf16[2,32,640]{2,1,0:T(8,128)(2,1)S(1)} %slice.8), channel_id=1, source_target_pairs={{0,32},{32,64},{64,96},{96,128},{128,160},{160,192},{192,224},{224... | collective-permute-start | bytes 245768 | tf_op jit(solution)/shard_map/ppermute | solution.py:368

commit v5 on v4

--- a/solution.py
+++ b/solution.py
@@ -99,6 +99,7 @@
             rows = [jnp.where(even, weights[1], weights[2]), jnp.where(even, weights[2], weights[1])]
             rows += {0: [weights[4]], PATCHES - 1: [weights[3]]}.get(p, [])
             (near, near_drive), (far, far_drive), *edge = weighted_grams(ens_ref, flipped_ref, rows, pick_row(innov_ref[0], p))
+            far = 0.5 * (far + far.T)
             near_ref[0, 0:K, :] = near
             near_ref[0, K:EXT, :] = jnp.broadcast_to(near_drive, (EXT - K, K))
             if p < 2:
@@ -110,6 +111,7 @@
                 far_ref[at, K + 1 : K + 2, :] = far_drive
                 far_ref[at, K + 2 : K + 3, :] = diagonal(far)
             for (gram, drive), ref in zip(edge, (next_ref if p else prev_ref,)):
+                gram = 0.5 * (gram + gram.T)
                 ref[0, 0:HALF, 0:HALF] = jnp.where(upper_lower(HALF)[0], gram[0:HALF, 0:HALF], gram[HALF:, HALF:])
                 ref[0, 0:HALF, HALF:] = gram[0:HALF, HALF:]
                 ref[0, HALF:, :] = jnp.broadcast_to(drive, (EDGE - HALF, K))
@@ -191,10 +193,26 @@
     refs[0][p], refs[1][p] = split(x)
 
 
+def analysed(states, flipped):
+    states = states.astype(F32)
+    mean = jnp.sum(states, axis=0, keepdims=True) * (1.0 / K)
+    return (mean + dot(flipped, (states - mean).astype(BF16))).astype(BF16)
+
+
+def cut_for_peers(whole, refs):
+    me = lax.axis_index("mem")
+    n = whole.shape[1]
+    for ref, places in zip(refs, ((0,), (2, 3), (6, 5), (1,), (7,), (4,))):
+        for i, away in enumerate(places):
+            ref[i * n : (i + 1) * n] = whole[lax.rem(me + away, PEERS)]
+
+
 def root_kernel(edges, *refs):
     n = 2
     if edges:
-        sums, following, previous, out_ref, total_s, edge_s, *rest = refs
+        sums, following, previous, states, *refs = refs
+        out_refs, (whole, states_s, state_sem, total_s, edge_s, *rest) = refs[:6], refs[6:]
+        fetch = pltpu.make_async_copy(states, states_s, state_sem.at[0])
         sources = [(sums, total_s), (following, edge_s.at[pl.ds(0, 1)]), (previous, edge_s.at[pl.ds(1, 1)])]
     else:
         own, near, far, out_ref, sums_ref, total_s, own_s, near_s, far_s, *rest = refs
@@ -203,6 +221,8 @@
     y, z, s = (yh, yl), (zh, zl), (sh, sl)
     copies = [pltpu.make_async_copy(a, b, sems.at[i]) for i, (a, b) in enumerate(sources)]
     start_all(copies)
+    if edges:
+        fetch.start()
     row = lax.broadcasted_iota(jnp.int32, (K, K), 0)
     col = lax.broadcasted_iota(jnp.int32, (K, K), 1)
     diag_ref[...] = jnp.where(row == col, 1.5, 0.0).astype(F32)
@@ -248,13 +268,23 @@
     lax.fori_loop(0, ITERS - 2, sweep, 0, unroll=True)
     for p in range(n):
         residual(p)
+    if edges:
+        fetch.wait()
     for p in range(n):
         flipped = product(s, z, p) * scale_ref[p, 0:1, :]
         half = flipped.T
         inner = jnp.sum(half * total_s[p, K : K + 1, :], axis=1, keepdims=True)
         mean_weight = jnp.sum(flipped * inner, axis=0, keepdims=True)
-        out_ref[p] = (jnp.sqrt(float(K - 1)) * flipped + mean_weight).astype(BF16)
-    if not edges:
+        transform = (jnp.sqrt(float(K - 1)) * flipped + mean_weight).astype(BF16)
+        if edges:
+            rows = states_s.shape[3]
+            result = analysed(states_s[:, OUTER[p]].reshape(K, rows), transform)
+            whole[:, p] = result.reshape(PEERS, K // PEERS, rows)
+        else:
+            out_ref[p] = transform
+    if edges:
+        cut_for_peers(whole, out_refs)
+    else:
         add_up(sums_ref, OUTER, 0)
 
 
@@ -262,13 +292,21 @@
     n = 2
     piece = pltpu.VMEM((n, K, K), BF16)
     two, full, edge = (pltpu.VMEM(shape, F32) for shape in ((n, EXT, K), (PATCHES, EXT, K), (2, EDGE, K)))
-    shapes = [jax.ShapeDtypeStruct((n, K, K), BF16)] + ([] if edges else [jax.ShapeDtypeStruct((n, EXT, K), F32)])
+    if edges:
+        states = args[-1].shape
+        block, twice = (n,) + states[2:], (2 * n,) + states[2:]
+        shapes = [jax.ShapeDtypeStruct(shape, BF16) for shape in (block, twice, twice, block, block, block)]
+        more = [pltpu.VMEM((PEERS,) + block, BF16), pltpu.VMEM(states, BF16), pltpu.SemaphoreType.DMA((1,))]
+    else:
+        shapes = [jax.ShapeDtypeStruct((n, K, K), BF16), jax.ShapeDtypeStruct((n, EXT, K), F32)]
+        more = []
     return pl.pallas_call(
         functools.partial(root_kernel, edges),
         in_specs=[ANY] * len(args),
         out_specs=[VMEM] * len(shapes),
         out_shape=shapes,
-        scratch_shapes=([two, edge] if edges else [two, full, full, two])
+        scratch_shapes=more
+        + ([two, edge] if edges else [two, full, full, two])
         + [pltpu.SemaphoreType.DMA((3,))]
         + [piece] * 6
         + [pltpu.VMEM((K, K), F32), pltpu.VMEM((n, 8, K), F32)],
@@ -278,85 +316,79 @@
     )(*args)
 
 
-def analysed(states, flipped):
-    states = states.astype(F32)
-    mean = jnp.sum(states, axis=0, keepdims=True) * (1.0 / K)
-    return (mean + dot(flipped, (states - mean).astype(BF16))).astype(BF16)
-
-
-def apply_kernel(patches, flipped_ref, states, *refs):
-    *out_refs, states_s, sems = refs
+def apply_kernel(flipped_ref, states, out_ref, states_s, sems):
     rows = states_s.shape[3]
-    copies = [pltpu.make_async_copy(states.at[:, p], states_s.at[:, i], sems.at[i]) for i, p in enumerate(patches)]
+    copies = [pltpu.make_async_copy(states.at[:, p], states_s.at[:, i], sems.at[i]) for i, p in enumerate(INNER)]
     start_all(copies)
-    whole = out_refs[-1]
-    for i in range(len(patches)):
-        copies[i].wait()
-        whole[:, i] = analysed(states_s[:, i].reshape(K, rows), flipped_ref[i]).reshape(PEERS, K // PEERS, rows)
-    if len(out_refs) == 1:
-        return
-    c0, c2, c6, c1, c7, c4 = out_refs[:6]
-    me = lax.axis_index("mem")
-
-    def away(places):
-        return whole[lax.rem(me + places, PEERS)]
-
-    n = len(patches)
-    c0[...] = away(0)
-    c2[0:n] = away(2)
-    c2[n:] = away(3)
-    c6[0:n] = away(6)
-    c6[n:] = away(5)
-    c1[...] = away(1)
-    c7[...] = away(7)
-    c4[...] = away(4)
-
-
-def apply_weights(patches, flipped, states, turned):
-    n = len(patches)
-    block = (n,) + states.shape[2:]
-    twice = (2 * n,) + states.shape[2:]
-    whole = pltpu.VMEM((PEERS,) + block, BF16)
-    shapes = (block, twice, twice, block, block, block) if turned else ((PEERS,) + block,)
+    for i, copy in enumerate(copies):
+        copy.wait()
+        result = analysed(states_s[:, i].reshape(K, rows), flipped_ref[i])
+        out_ref[:, i] = result.reshape(PEERS, K // PEERS, rows)
+
+
+def apply_weights(flipped, states):
+    shape = (PEERS, len(INNER)) + states.shape[2:]
     return pl.pallas_call(
-        functools.partial(apply_kernel, patches),
+        apply_kernel,
         in_specs=[VMEM, ANY],
-        out_specs=[VMEM] * len(shapes),
-        out_shape=[jax.ShapeDtypeStruct(shape, BF16) for shape in shapes],
-        scratch_shapes=[whole] * (2 if turned else 1) + [pltpu.SemaphoreType.DMA((n,))],
+        out_specs=VMEM,
+        out_shape=jax.ShapeDtypeStruct(shape, BF16),
+        scratch_shapes=[pltpu.VMEM(shape, BF16), pltpu.SemaphoreType.DMA((PEERS,))],
         compiler_params=SMALL,
         cost_estimate=COST,
         name="apply_weights",
     )(flipped, states)
 
 
-def gather_kernel(first, c0, c2, c6, c1, c7, c4, c3, c5, out, sems):
+def place(parts, out, sems):
     me = lax.axis_index("mem")
-    parts = ((c0, 0), (c1, 1), (c2, 2), (c3, 3), (c4, 4), (c5, 5), (c6, 6), (c7, 7))
     copies = []
-    for j in range(PEERS):
-        copies.append(pltpu.make_async_copy(first.at[j], out.at[j, pl.ds(1, 2)], sems.at[j]))
     for ref, places in parts:
         source = lax.rem(me + PEERS - places, PEERS)
         for i, p in enumerate(OUTER):
-            copies.append(pltpu.make_async_copy(ref.at[i], out.at[source, p], sems.at[PEERS + 2 * places + i]))
+            copies.append(pltpu.make_async_copy(ref.at[i], out.at[source, p], sems.at[len(copies)]))
+    return copies
+
+
+def gather_kernel(first, c0, c2, c6, c1, c7, out, sems):
+    copies = place(((c0, 0), (c1, 1), (c2, 2), (c6, 6), (c7, 7)), out, sems)
+    for j in range(PEERS):
+        copies.append(pltpu.make_async_copy(first.at[j], out.at[j, pl.ds(1, 2)], sems.at[len(copies)]))
     start_all(copies)
     for copy in copies:
         copy.wait()
 
 
-def gather(first, *parts):
-    shape = (PEERS, PATCHES) + first.shape[2:]
-    return pl.pallas_call(
+def gather_rest_kernel(so_far, c4, c3, c5, out, sems):
+    copies = place(((c4, 4), (c3, 3), (c5, 5)), out, sems)
+    start_all(copies)
+    for copy in copies:
+        copy.wait()
+
+
+def gather(first, c0, c2, c6, c1, c7, c4, c3, c5):
+    shape = jax.ShapeDtypeStruct((PEERS, PATCHES) + first.shape[2:], BF16)
+    some = pl.pallas_call(
         gather_kernel,
-        in_specs=[VMEM] * (PEERS + 1),
+        in_specs=[VMEM] * 6,
         out_specs=ANY,
-        out_shape=jax.ShapeDtypeStruct(shape, BF16),
-        scratch_shapes=[pltpu.SemaphoreType.DMA((3 * PEERS,))],
+        out_shape=shape,
+        scratch_shapes=[pltpu.SemaphoreType.DMA((18,))],
         compiler_params=SMALL,
         cost_estimate=COST,
         name="gather",
-    )(first, *parts)
+    )(first, c0, c2, c6, c1, c7)
+    return pl.pallas_call(
+        gather_rest_kernel,
+        in_specs=[ANY] + [VMEM] * 3,
+        out_specs=ANY,
+        out_shape=shape,
+        input_output_aliases={0: 0},
+        scratch_shapes=[pltpu.SemaphoreType.DMA((6,))],
+        compiler_params=SMALL,
+        cost_estimate=COST,
+        name="gather_rest",
+    )(some, c4, c3, c5)
 
 
 def swap(value):
@@ -398,11 +430,11 @@
     previous = shift(previous, "mem", -1)
     own = kept_grams(*obs)
     flipped, sums = root_weights(False, own, near, far)
-    (first,) = apply_weights(INNER, flipped, states, False)
+    first = apply_weights(flipped, states)
     first, following, previous = lax.optimization_barrier((first, following, previous))
     first = swap(first)
-    (flipped,) = root_weights(True, sums, following, previous)
-    analysis = gather(first, *spread(*apply_weights(OUTER, flipped, states, True)))
+    blocks = root_weights(True, sums, following, previous, states)
+    analysis = gather(first, *spread(*blocks))
     return analysis.reshape(1, PEERS * PATCHES, K // PEERS, rows)
 
 

time: 83.6 us -> 83.1 us (level)
  waiting for transfers between devices: 17.4 us -> 15.9 us
  Pallas kernels: 32.2 us -> 33.1 us
    ppermute x9, waiting for transfers between devices: 8.14 us -> 7 us  [shift(): lax.ppermute(value, axis, [(i, (i + by) % peers) for i in range(peers)])]
  transfers between devices with their start and end apart: 13 -> 13, of which waited for: 4 -> 4; matrix products, arithmetic and copies ran while one was open for 0% -> 0% of each run, Pallas kernels for 37% -> 39%
where the time goes in v5:
time: 83.1 us; the launch traced here: 82.8 us
  Pallas kernels  33.1 us (40%)
  starting transfers between devices  31.3 us (38%)
  waiting for transfers between devices  15.9 us (19%)
  local copies, waits for them, and re-layouts  2.21 us (3%)
    pallas_call x2, Pallas kernels, root_weights(): pl.pallas_call(functools.partial(root_kernel, edges), in_specs=[ANY] * le...  19.4 us
    ppermute x9, starting transfers between devices, shift(): lax.ppermute(value, axis, [(i, (i + by) % peers) for i in range(peers)])  18.2 us
    all_to_all x2, starting transfers between devices, swap(): return lax.all_to_all(value, 'mem', split_axis=0, concat_axis=0, tiled=True)  12.4 us
    all_to_all x2, waiting for transfers between devices, swap(): return lax.all_to_all(value, 'mem', split_axis=0, concat_axis=0, tiled=True)  8.86 us
    ppermute x9, waiting for transfers between devices, shift(): lax.ppermute(value, axis, [(i, (i + by) % peers) for i in range(peers)])  7 us
    pallas_call x1, Pallas kernels, sent_grams(): pl.pallas_call(sent_kernel, grid=(PATCHES,), in_specs=gram_specs(), out_s...  5.08 us
    pallas_call x1, Pallas kernels, kept_grams(): pl.pallas_call(kept_kernel, grid=(PATCHES,), in_specs=gram_specs(), out_s...  5.06 us
    unnamed x10, local copies, waits for them, and re-layouts  2.2 us
  transfers between devices with their start and end apart: 13, of which 4 were waited for; matrix products, arithmetic and copies ran while one was open for 0% of the time, Pallas kernels for 39%

profile of v5, /device:TPU:26, one launch (start us, length us, event | category | flops | bytes accessed | tf_op | source)
XLA Modules:
  0.0 82.8 jit_solution(13904515985960240491)
XLA Ops:
  0.0 8.6 %all-to-all-start = ((bf16[8,4,32,640]{3,2,1,0:T(8,128)(2,1)}), bf16[8,4,32,640]{3,2,1,0:T(8,128)(2,1)S(1)}, u32[]{:S(2)}, u32[]{:S(2)}) async-start(bf16[8,4,32,640]{3,2,1,0:T(8,128)(2,1)} %bitcast.8), calls=%async_computation | async-start | bytes 2621440 | tf_op jit(solution)/shard_map/all_to_all | solution.py:395
  8.7 0.0 copy-start
  8.7 2.2 %copy-done = bf16[1,4,2048,256]{3,2,1,0:T(8,128)(2,1)S(1)} copy-done((bf16[1,4,2048,256]{3,2,1,0:T(8,128)(2,1)S(1)}, bf16[1,4,2048,256]{3,2,1,0:T(8,128)(2,1)}, u32[]{:S(2)}) %copy-start) | copy-done | bytes 4194328
  10.9 5.1 %sent_grams.1 = (f32[4,264,256]{2,1,0:T(8,128)S(1)}, f32[2,264,256]{2,1,0:T(8,128)S(1)}, f32[1,136,256]{2,1,0:T(8,128)S(1)}, f32[1,136,256]{2,1,0:T(8,128)S(1)}) custom-call(s32[4]{0:T(128)S(1)} %bitcast.6, bf16[1,4,2048,256]{3,2,1,0:T(8,128)(2,1)S(1)} %copy-done, bf16[1,4,2048]{2,1,0:T(4,128)(2,1)S(1)} %copy-done.2, bf16[1,4,2048]{2,1,0:T(4,128)(2,1)S(1)} %copy-done.3, ...), custom_call_target="tpu_custom_call" | custom-call | flops 1000 | bytes 1000 | tf_op jit(solution)/shard_map/sent_grams/pallas_call | solution.py:164
  15.9 0.1 collective-permute-start
  16.0 0.6 collective-permute-start.1
  16.7 2.0 %collective-permute-start.2 = (f32[1,136,256]{2,1,0:T(8,128)S(1)}, f32[1,136,256]{2,1,0:T(8,128)S(1)}, u32[]{:S(2)}, u32[]{:S(2)}) collective-permute-start(f32[1,136,256]{2,1,0:T(8,128)S(1)} %get-tuple-element.23), channel_id=1, source_target_pairs={{0,32},{32,64},{64,96},{96,128},{128,160},{160,192},{192,224},{224... | collective-permute-start | bytes 417800 | tf_op jit(solution)/shard_map/ppermute | solution.py:400
  18.7 1.2 %collective-permute-start.3 = (f32[1,136,256]{2,1,0:T(8,128)S(1)}, f32[1,136,256]{2,1,0:T(8,128)S(1)}, u32[]{:S(2)}, u32[]{:S(2)}) collective-permute-start(f32[1,136,256]{2,1,0:T(8,128)S(1)} %get-tuple-element.24), channel_id=1, source_target_pairs={{0,224},{32,0},{64,32},{96,64},{128,96},{160,128},{192,160},{224,1... | collective-permute-start | bytes 417800 | tf_op jit(solution)/shard_map/ppermute | solution.py:400
  19.9 5.1 %kept_grams.1.refs_0_ = f32[4,264,256]{2,1,0:T(8,128)S(1)} custom-call(s32[4]{0:T(128)S(1)} %bitcast.7, bf16[1,4,2048,256]{3,2,1,0:T(8,128)(2,1)S(1)} %copy-done, bf16[1,4,2048]{2,1,0:T(4,128)(2,1)S(1)} %copy-done.2, bf16[1,4,2048]{2,1,0:T(4,128)(2,1)S(1)} %copy-done.3, bf16[1,5,4,2048]{3,2,1,0:T(4,128)(2,1)S(1)} %bitcast.5), custom_call_target="tpu_custom_call" | custom-call | flops 1000 | bytes 1000 | tf_op jit(solution)/shard_map/kept_grams/pallas_call | solution.py:179
  25.0 0.0 collective-permute-done.1.refs_2_
  25.0 9.3 %root_weights.2 = (bf16[2,256,256]{2,1,0:T(8,128)(2,1)S(1)}, f32[2,264,256]{2,1,0:T(8,128)S(1)}) custom-call(f32[4,264,256]{2,1,0:T(8,128)S(1)} %kept_grams.1.refs_0_, f32[4,264,256]{2,1,0:T(8,128)S(1)} %collective-permute-done.refs_1_, f32[2,264,256]{2,1,0:T(8,128)S(1)} %collective-permute-done.1.refs_2_), custom_call_target="tpu_custom_call" | custom-call | flops 2000000000 | bytes 1000 | tf_op jit(solution)/shard_map/root_weights/pallas_call | solution.py:303
  34.3 8.9 %all-to-all-done.states.refs_3_ = bf16[8,4,32,640]{3,2,1,0:T(8,128)(2,1)S(1)} async-done(((bf16[8,4,32,640]{3,2,1,0:T(8,128)(2,1)}), bf16[8,4,32,640]{3,2,1,0:T(8,128)(2,1)S(1)}, u32[]{:S(2)}, u32[]{:S(2)}) %all-to-all-start) | async-done | bytes 1310752 | tf_op jit(solution)/shard_map/all_to_all | solution.py:395
  43.2 1.6 %apply_weights.1 = bf16[8,2,32,640]{3,2,1,0:T(8,128)(2,1)} custom-call(bf16[2,256,256]{2,1,0:T(8,128)(2,1)S(1)} %get-tuple-element.22.flipped_ref, bf16[8,4,32,640]{3,2,1,0:T(8,128)(2,1)S(1)} %all-to-all-done.states.refs_3_), custom_call_target="tpu_custom_call" | custom-call | flops 1000 | bytes 1000 | tf_op jit(solution)/shard_map/apply_weights/pallas_call | solution.py:331
  44.9 0.0 collective-permute-done.3.refs_2_
  44.9 3.8 %all-to-all-start.1 = ((bf16[8,2,32,640]{3,2,1,0:T(8,128)(2,1)}), bf16[8,2,32,640]{3,2,1,0:T(8,128)(2,1)S(1)}, u32[]{:S(2)}, u32[]{:S(2)}) async-start(bf16[8,2,32,640]{3,2,1,0:T(8,128)(2,1)} %apply_weights.1), calls=%async_computation.1 | async-start | bytes 1310720 | tf_op jit(solution)/shard_map/all_to_all | solution.py:395
  48.7 10.1 %root_weights.3 = (bf16[2,32,640]{2,1,0:T(8,128)(2,1)S(1)}, bf16[4,32,640]{2,1,0:T(8,128)(2,1)S(1)}, bf16[4,32,640]{2,1,0:T(8,128)(2,1)S(1)}, bf16[2,32,640]{2,1...) custom-call(f32[2,264,256]{2,1,0:T(8,128)S(1)} %get-tuple-element.26.refs_0_, ...), custom_call_target="tpu_custom_call" | custom-call | flops 2000000000 | bytes 1000 | tf_op jit(solution)/shard_map/root_weights/pallas_call | solution.py:303
  58.8 3.9 %collective-permute-start.5 = (bf16[4,32,640]{2,1,0:T(8,128)(2,1)S(1)}, bf16[4,32,640]{2,1,0:T(8,128)(2,1)S(1)}, u32[]{:S(2)}, u32[]{:S(2)}) collective-permute-start(bf16[4,32,640]{2,1,0:T(8,128)(2,1)S(1)} %get-tuple-element.31), channel_id=1, source_target_pairs={{0,192},{32,224},{64,0},{96,32},{128,64},{160,96},{192,128},{224,1... | collective-permute-start | bytes 491528 | tf_op jit(solution)/shard_map/ppermute | solution.py:400
  62.7 0.0 collective-permute-start.4
  62.7 0.9 %collective-permute-start.6 = (bf16[2,32,640]{2,1,0:T(8,128)(2,1)S(1)}, bf16[2,32,640]{2,1,0:T(8,128)(2,1)S(1)}, u32[]{:S(2)}, u32[]{:S(2)}) collective-permute-start(bf16[2,32,640]{2,1,0:T(8,128)(2,1)S(1)} %get-tuple-element.32), channel_id=1, source_target_pairs={{0,32},{32,64},{64,96},{96,128},{128,160},{160,192},{192,224},{224... | collective-permute-start | bytes 245768 | tf_op jit(solution)/shard_map/ppermute | solution.py:400
  63.6 2.4 %collective-permute-start.7 = (bf16[2,32,640]{2,1,0:T(8,128)(2,1)S(1)}, bf16[2,32,640]{2,1,0:T(8,128)(2,1)S(1)}, u32[]{:S(2)}, u32[]{:S(2)}) collective-permute-start(bf16[2,32,640]{2,1,0:T(8,128)(2,1)S(1)} %get-tuple-element.33), channel_id=1, source_target_pairs={{0,224},{32,0},{64,32},{96,64},{128,96},{160,128},{192,160},{224,1... | collective-permute-start | bytes 245768 | tf_op jit(solution)/shard_map/ppermute | solution.py:400
  65.9 4.7 %collective-permute-start.8 = (bf16[2,32,640]{2,1,0:T(8,128)(2,1)S(1)}, bf16[2,32,640]{2,1,0:T(8,128)(2,1)S(1)}, u32[]{:S(2)}, u32[]{:S(2)}) collective-permute-start(bf16[2,32,640]{2,1,0:T(8,128)(2,1)S(1)} %get-tuple-element.34), channel_id=1, source_target_pairs={{0,128},{32,160},{64,192},{96,224},{128,0},{160,32},{192,64},{224,... | collective-permute-start | bytes 245768 | tf_op jit(solution)/shard_map/ppermute | solution.py:400
  70.6 2.6 %collective-permute-done.5.c6 = bf16[4,32,640]{2,1,0:T(8,128)(2,1)S(1)} collective-permute-done((bf16[4,32,640]{2,1,0:T(8,128)(2,1)S(1)}, bf16[4,32,640]{2,1,0:T(8,128)(2,1)S(1)}, u32[]{:S(2)}, u32[]{:S(2)}) %collective-permute-start.5) | collective-permute-done | bytes 163872 | tf_op jit(solution)/shard_map/ppermute | solution.py:400
  73.3 2.6 %collective-permute-start.10 = (bf16[2,32,640]{2,1,0:T(8,128)(2,1)S(1)}, bf16[2,32,640]{2,1,0:T(8,128)(2,1)S(1)}, u32[]{:S(2)}, u32[]{:S(2)}) collective-permute-start(bf16[2,32,640]{2,1,0:T(8,128)(2,1)S(1)} %slice.9), channel_id=1, source_target_pairs={{0,224},{32,0},{64,32},{96,64},{128,96},{160,128},{192,160},{224,1... | collective-permute-start | bytes 245768 | tf_op jit(solution)/shard_map/ppermute | solution.py:400
  75.9 0.0 collective-permute-done.4.c2
  75.9 0.4 collective-permute-start.9
  76.4 0.6 collective-permute-done.6.c1
  77.0 0.0 collective-permute-done.7.c7
  77.0 0.0 all-to-all-done.1.first
  77.0 1.1 %gather.1.so_far = bf16[8,4,32,640]{3,2,1,0:T(8,128)(2,1)} custom-call(bf16[8,2,32,640]{3,2,1,0:T(8,128)(2,1)S(1)} %all-to-all-done.1.first, bf16[2,32,640]{2,1,0:T(8,128)(2,1)S(1)} %get-tuple-element.29.c0, bf16[4,32,640]{2,1,0:T(8,128)(2,1)S(1)} %collective-permute-done.4.c2, bf16[4,32,640]{2,1,0:T(8,128)(2,1)S(1)} %collective-permute-done.5.c6, ...), custom_call_target="tpu_custom_call" | custom-call | flops 1000 | bytes 1000 | tf_op jit(solution)/shard_map/gather/pallas_call | solution.py:371
  78.1 3.8 %collective-permute-done.8.c4 = bf16[2,32,640]{2,1,0:T(8,128)(2,1)S(1)} collective-permute-done((bf16[2,32,640]{2,1,0:T(8,128)(2,1)S(1)}, bf16[2,32,640]{2,1,0:T(8,128)(2,1)S(1)}, u32[]{:S(2)}, u32[]{:S(2)}) %collective-permute-start.8) | collective-permute-done | bytes 81952 | tf_op jit(solution)/shard_map/ppermute | solution.py:400
  81.8 0.0 collective-permute-done.9.c3
  81.9 0.7 gather_rest.1
  (13 shorter events, 0.0 us)
Async XLA Ops:
  0.0 8.6 %copy-start.1 = (bf16[1,4,5,2048]{3,1,2,0:T(4,128)(2,1)S(1)}, bf16[1,4,5,2048]{3,1,2,0:T(4,128)(2,1)}, u32[]{:S(2)}) copy-start(bf16[1,4,5,2048]{3,1,2,0:T(4,128)(2,1)} %param.10) | copy-start | bytes 245764
  0.0 8.6 %copy-start.2 = (bf16[1,4,2048]{2,1,0:T(4,128)(2,1)S(1)}, bf16[1,4,2048]{2,1,0:T(4,128)(2,1)}, u32[]{:S(2)}) copy-start(bf16[1,4,2048]{2,1,0:T(4,128)(2,1)} %innov_ref.3) | copy-start | bytes 49156
  0.0 8.6 %copy-start.3 = (bf16[1,4,2048]{2,1,0:T(4,128)(2,1)S(1)}, bf16[1,4,2048]{2,1,0:T(4,128)(2,1)}, u32[]{:S(2)}) copy-start(bf16[1,4,2048]{2,1,0:T(4,128)(2,1)} %prec_ref.3) | copy-start | bytes 49156
  0.0 8.6 %copy-start.4 = (s32[1,4]{1,0:T(1,128)S(1)}, s32[1,4]{1,0:T(1,128)}, u32[]{:S(2)}) copy-start(s32[1,4]{1,0:T(1,128)} %param.11) | copy-start | bytes 52
  0.0 43.2 %all-to-all-start = ((bf16[8,4,32,640]{3,2,1,0:T(8,128)(2,1)}), bf16[8,4,32,640]{3,2,1,0:T(8,128)(2,1)S(1)}, u32[]{:S(2)}, u32[]{:S(2)}) async-start(bf16[8,4,32,640]{3,2,1,0:T(8,128)(2,1)} %bitcast.8), calls=%async_computation | async-start | bytes 2621440 | tf_op jit(solution)/shard_map/all_to_all | solution.py:395
  8.7 2.2 %copy-start = (bf16[1,4,2048,256]{3,2,1,0:T(8,128)(2,1)S(1)}, bf16[1,4,2048,256]{3,2,1,0:T(8,128)(2,1)}, u32[]{:S(2)}) copy-start(bf16[1,4,2048,256]{3,2,1,0:T(8,128)(2,1)} %ens_ref.3) | copy-start | bytes 12582916
  15.9 9.1 %collective-permute-start = (f32[4,264,256]{2,1,0:T(8,128)S(1)}, f32[4,264,256]{2,1,0:T(8,128)S(1)}, u32[]{:S(2)}, u32[]{:S(2)}) collective-permute-start(f32[4,264,256]{2,1,0:T(8,128)S(1)} %get-tuple-element.20), channel_id=1, source_target_pairs={{0,1},{2,3},{4,5},{6,7},{8,9},{10,11},{12,13},{14,15},{16,17},{18,... | collective-permute-start | bytes 3244040 | tf_op jit(solution)/shard_map/ppermute | solution.py:406
  16.0 8.9 %collective-permute-start.1 = (f32[2,264,256]{2,1,0:T(8,128)S(1)}, f32[2,264,256]{2,1,0:T(8,128)S(1)}, u32[]{:S(2)}, u32[]{:S(2)}) collective-permute-start(f32[2,264,256]{2,1,0:T(8,128)S(1)} %get-tuple-element.21), channel_id=1, source_target_pairs={{1,2},{3,4},{5,6},{7,8},{9,10},{11,12},{13,14},{15,16},{17,18},{19... | collective-permute-start | bytes 1622024 | tf_op jit(solution)/shard_map/ppermute | solution.py:406
  16.7 28.2 %collective-permute-start.2 = (f32[1,136,256]{2,1,0:T(8,128)S(1)}, f32[1,136,256]{2,1,0:T(8,128)S(1)}, u32[]{:S(2)}, u32[]{:S(2)}) collective-permute-start(f32[1,136,256]{2,1,0:T(8,128)S(1)} %get-tuple-element.23), channel_id=1, source_target_pairs={{0,32},{32,64},{64,96},{96,128},{128,160},{160,192},{192,224},{224... | collective-permute-start | bytes 417800 | tf_op jit(solution)/shard_map/ppermute | solution.py:400
  18.7 26.2 %collective-permute-start.3 = (f32[1,136,256]{2,1,0:T(8,128)S(1)}, f32[1,136,256]{2,1,0:T(8,128)S(1)}, u32[]{:S(2)}, u32[]{:S(2)}) collective-permute-start(f32[1,136,256]{2,1,0:T(8,128)S(1)} %get-tuple-element.24), channel_id=1, source_target_pairs={{0,224},{32,0},{64,32},{96,64},{128,96},{160,128},{192,160},{224,1... | collective-permute-start | bytes 417800 | tf_op jit(solution)/shard_map/ppermute | solution.py:400
  44.9 32.1 %all-to-all-start.1 = ((bf16[8,2,32,640]{3,2,1,0:T(8,128)(2,1)}), bf16[8,2,32,640]{3,2,1,0:T(8,128)(2,1)S(1)}, u32[]{:S(2)}, u32[]{:S(2)}) async-start(bf16[8,2,32,640]{3,2,1,0:T(8,128)(2,1)} %apply_weights.1), calls=%async_computation.1 | async-start | bytes 1310720 | tf_op jit(solution)/shard_map/all_to_all | solution.py:395
  58.8 14.5 %collective-permute-start.5 = (bf16[4,32,640]{2,1,0:T(8,128)(2,1)S(1)}, bf16[4,32,640]{2,1,0:T(8,128)(2,1)S(1)}, u32[]{:S(2)}, u32[]{:S(2)}) collective-permute-start(bf16[4,32,640]{2,1,0:T(8,128)(2,1)S(1)} %get-tuple-element.31), channel_id=1, source_target_pairs={{0,192},{32,224},{64,0},{96,32},{128,64},{160,96},{192,128},{224,1... | collective-permute-start | bytes 491528 | tf_op jit(solution)/shard_map/ppermute | solution.py:400
  62.7 13.2 %collective-permute-start.4 = (bf16[4,32,640]{2,1,0:T(8,128)(2,1)S(1)}, bf16[4,32,640]{2,1,0:T(8,128)(2,1)S(1)}, u32[]{:S(2)}, u32[]{:S(2)}) collective-permute-start(bf16[4,32,640]{2,1,0:T(8,128)(2,1)S(1)} %get-tuple-element.30), channel_id=1, source_target_pairs={{0,64},{32,96},{64,128},{96,160},{128,192},{160,224},{192,0},{224,... | collective-permute-start | bytes 491528 | tf_op jit(solution)/shard_map/ppermute | solution.py:400
  62.7 14.3 %collective-permute-start.6 = (bf16[2,32,640]{2,1,0:T(8,128)(2,1)S(1)}, bf16[2,32,640]{2,1,0:T(8,128)(2,1)S(1)}, u32[]{:S(2)}, u32[]{:S(2)}) collective-permute-start(bf16[2,32,640]{2,1,0:T(8,128)(2,1)S(1)} %get-tuple-element.32), channel_id=1, source_target_pairs={{0,32},{32,64},{64,96},{96,128},{128,160},{160,192},{192,224},{224... | collective-permute-start | bytes 245768 | tf_op jit(solution)/shard_map/ppermute | solution.py:400
  63.6 13.4 %collective-permute-start.7 = (bf16[2,32,640]{2,1,0:T(8,128)(2,1)S(1)}, bf16[2,32,640]{2,1,0:T(8,128)(2,1)S(1)}, u32[]{:S(2)}, u32[]{:S(2)}) collective-permute-start(bf16[2,32,640]{2,1,0:T(8,128)(2,1)S(1)} %get-tuple-element.33), channel_id=1, source_target_pairs={{0,224},{32,0},{64,32},{96,64},{128,96},{160,128},{192,160},{224,1... | collective-permute-start | bytes 245768 | tf_op jit(solution)/shard_map/ppermute | solution.py:400
  65.9 15.9 %collective-permute-start.8 = (bf16[2,32,640]{2,1,0:T(8,128)(2,1)S(1)}, bf16[2,32,640]{2,1,0:T(8,128)(2,1)S(1)}, u32[]{:S(2)}, u32[]{:S(2)}) collective-permute-start(bf16[2,32,640]{2,1,0:T(8,128)(2,1)S(1)} %get-tuple-element.34), channel_id=1, source_target_pairs={{0,128},{32,160},{64,192},{96,224},{128,0},{160,32},{192,64},{224,... | collective-permute-start | bytes 245768 | tf_op jit(solution)/shard_map/ppermute | solution.py:400
  73.3 8.6 %collective-permute-start.10 = (bf16[2,32,640]{2,1,0:T(8,128)(2,1)S(1)}, bf16[2,32,640]{2,1,0:T(8,128)(2,1)S(1)}, u32[]{:S(2)}, u32[]{:S(2)}) collective-permute-start(bf16[2,32,640]{2,1,0:T(8,128)(2,1)S(1)} %slice.9), channel_id=1, source_target_pairs={{0,224},{32,0},{64,32},{96,64},{128,96},{160,128},{192,160},{224,1... | collective-permute-start | bytes 245768 | tf_op jit(solution)/shard_map/ppermute | solution.py:400
  75.9 5.9 %collective-permute-start.9 = (bf16[2,32,640]{2,1,0:T(8,128)(2,1)S(1)}, bf16[2,32,640]{2,1,0:T(8,128)(2,1)S(1)}, u32[]{:S(2)}, u32[]{:S(2)}) collective-permute-start(bf16[2,32,640]{2,1,0:T(8,128)(2,1)S(1)} %slice.8), channel_id=1, source_target_pairs={{0,32},{32,64},{64,96},{96,128},{128,160},{160,192},{192,224},{224... | collective-permute-start | bytes 245768 | tf_op jit(solution)/shard_map/ppermute | solution.py:400

commit v6 on v5

--- a/solution.py
+++ b/solution.py
@@ -211,7 +211,7 @@
     n = 2
     if edges:
         sums, following, previous, states, *refs = refs
-        out_refs, (whole, states_s, state_sem, total_s, edge_s, *rest) = refs[:6], refs[6:]
+        out_refs, (whole, states_s, pert_s, mean_s, state_sem, total_s, edge_s, *rest) = refs[:6], refs[6:]
         fetch = pltpu.make_async_copy(states, states_s, state_sem.at[0])
         sources = [(sums, total_s), (following, edge_s.at[pl.ds(0, 1)]), (previous, edge_s.at[pl.ds(1, 1)])]
     else:
@@ -265,11 +265,15 @@
             split_to(z, p, product(s, z, p))
         return carry
 
+    if edges:
+        fetch.wait()
+        for i, p in enumerate(OUTER):
+            value = states_s[:, p].reshape(K, states_s.shape[3]).astype(F32)
+            mean_s[i] = jnp.sum(value, axis=0, keepdims=True) * (1.0 / K)
+            pert_s[i] = (value - mean_s[i]).astype(BF16)
     lax.fori_loop(0, ITERS - 2, sweep, 0, unroll=True)
     for p in range(n):
         residual(p)
-    if edges:
-        fetch.wait()
     for p in range(n):
         flipped = product(s, z, p) * scale_ref[p, 0:1, :]
         half = flipped.T
@@ -277,9 +281,8 @@
         mean_weight = jnp.sum(flipped * inner, axis=0, keepdims=True)
         transform = (jnp.sqrt(float(K - 1)) * flipped + mean_weight).astype(BF16)
         if edges:
-            rows = states_s.shape[3]
-            result = analysed(states_s[:, OUTER[p]].reshape(K, rows), transform)
-            whole[:, p] = result.reshape(PEERS, K // PEERS, rows)
+            result = (mean_s[p] + dot(transform, pert_s[p])).astype(BF16)
+            whole[:, p] = result.reshape(PEERS, K // PEERS, states_s.shape[3])
         else:
             out_ref[p] = transform
     if edges:
@@ -296,7 +299,8 @@
         states = args[-1].shape
         block, twice = (n,) + states[2:], (2 * n,) + states[2:]
         shapes = [jax.ShapeDtypeStruct(shape, BF16) for shape in (block, twice, twice, block, block, block)]
-        more = [pltpu.VMEM((PEERS,) + block, BF16), pltpu.VMEM(states, BF16), pltpu.SemaphoreType.DMA((1,))]
+        more = [pltpu.VMEM((PEERS,) + block, BF16), pltpu.VMEM(states, BF16)]
+        more += [pltpu.VMEM((n, K, states[3]), BF16), pltpu.VMEM((n, 1, states[3]), F32), pltpu.SemaphoreType.DMA((1,))]
     else:
         shapes = [jax.ShapeDtypeStruct((n, K, K), BF16), jax.ShapeDtypeStruct((n, EXT, K), F32)]
         more = []

time: 83.1 us -> 83 us (level)
  transfers between devices with their start and end apart: 13 -> 13, of which waited for: 4 -> 5; matrix products, arithmetic and copies ran while one was open for 0% -> 0% of each run, Pallas kernels for 39% -> 39%
where the time goes in v6:
time: 83 us; the launch traced here: 82.7 us
  Pallas kernels  33 us (40%)
  starting transfers between devices  31.2 us (38%)
  waiting for transfers between devices  16 us (19%)
  local copies, waits for them, and re-layouts  2.21 us (3%)
    pallas_call x2, Pallas kernels, root_weights(): pl.pallas_call(functools.partial(root_kernel, edges), in_specs=[ANY] * le...  19.4 us
    ppermute x9, starting transfers between devices, shift(): lax.ppermute(value, axis, [(i, (i + by) % peers) for i in range(peers)])  18.1 us
    all_to_all x2, starting transfers between devices, swap(): return lax.all_to_all(value, 'mem', split_axis=0, concat_axis=0, tiled=True)  12.4 us
    all_to_all x2, waiting for transfers between devices, swap(): return lax.all_to_all(value, 'mem', split_axis=0, concat_axis=0, tiled=True)  8.86 us
    ppermute x9, waiting for transfers between devices, shift(): lax.ppermute(value, axis, [(i, (i + by) % peers) for i in range(peers)])  7.09 us
    pallas_call x1, Pallas kernels, sent_grams(): pl.pallas_call(sent_kernel, grid=(PATCHES,), in_specs=gram_specs(), out_s...  5.08 us
    pallas_call x1, Pallas kernels, kept_grams(): pl.pallas_call(kept_kernel, grid=(PATCHES,), in_specs=gram_specs(), out_s...  5.06 us
    unnamed x10, local copies, waits for them, and re-layouts  2.2 us
  transfers between devices with their start and end apart: 13, of which 5 were waited for; matrix products, arithmetic and copies ran while one was open for 0% of the time, Pallas kernels for 39%

profile of v6, /device:TPU:26, one launch (start us, length us, event | category | flops | bytes accessed | tf_op | source)
XLA Modules:
  0.0 82.7 jit_solution(7502635037581858038)
XLA Ops:
  0.0 8.6 %all-to-all-start = ((bf16[8,4,32,640]{3,2,1,0:T(8,128)(2,1)}), bf16[8,4,32,640]{3,2,1,0:T(8,128)(2,1)S(1)}, u32[]{:S(2)}, u32[]{:S(2)}) async-start(bf16[8,4,32,640]{3,2,1,0:T(8,128)(2,1)} %bitcast.8), calls=%async_computation | async-start | bytes 2621440 | tf_op jit(solution)/shard_map/all_to_all | solution.py:399
  8.7 0.0 copy-start
  8.7 2.2 %copy-done = bf16[1,4,2048,256]{3,2,1,0:T(8,128)(2,1)S(1)} copy-done((bf16[1,4,2048,256]{3,2,1,0:T(8,128)(2,1)S(1)}, bf16[1,4,2048,256]{3,2,1,0:T(8,128)(2,1)}, u32[]{:S(2)}) %copy-start) | copy-done | bytes 4194328
  10.9 5.1 %sent_grams.1 = (f32[4,264,256]{2,1,0:T(8,128)S(1)}, f32[2,264,256]{2,1,0:T(8,128)S(1)}, f32[1,136,256]{2,1,0:T(8,128)S(1)}, f32[1,136,256]{2,1,0:T(8,128)S(1)}) custom-call(s32[4]{0:T(128)S(1)} %bitcast.6, bf16[1,4,2048,256]{3,2,1,0:T(8,128)(2,1)S(1)} %copy-done, bf16[1,4,2048]{2,1,0:T(4,128)(2,1)S(1)} %copy-done.2, bf16[1,4,2048]{2,1,0:T(4,128)(2,1)S(1)} %copy-done.3, ...), custom_call_target="tpu_custom_call" | custom-call | flops 1000 | bytes 1000 | tf_op jit(solution)/shard_map/sent_grams/pallas_call | solution.py:164
  15.9 0.1 collective-permute-start
  16.0 0.6 collective-permute-start.1
  16.7 2.0 %collective-permute-start.2 = (f32[1,136,256]{2,1,0:T(8,128)S(1)}, f32[1,136,256]{2,1,0:T(8,128)S(1)}, u32[]{:S(2)}, u32[]{:S(2)}) collective-permute-start(f32[1,136,256]{2,1,0:T(8,128)S(1)} %get-tuple-element.23), channel_id=1, source_target_pairs={{0,32},{32,64},{64,96},{96,128},{128,160},{160,192},{192,224},{224... | collective-permute-start | bytes 417800 | tf_op jit(solution)/shard_map/ppermute | solution.py:404
  18.7 1.2 %collective-permute-start.3 = (f32[1,136,256]{2,1,0:T(8,128)S(1)}, f32[1,136,256]{2,1,0:T(8,128)S(1)}, u32[]{:S(2)}, u32[]{:S(2)}) collective-permute-start(f32[1,136,256]{2,1,0:T(8,128)S(1)} %get-tuple-element.24), channel_id=1, source_target_pairs={{0,224},{32,0},{64,32},{96,64},{128,96},{160,128},{192,160},{224,1... | collective-permute-start | bytes 417800 | tf_op jit(solution)/shard_map/ppermute | solution.py:404
  19.9 5.1 %kept_grams.1.refs_0_ = f32[4,264,256]{2,1,0:T(8,128)S(1)} custom-call(s32[4]{0:T(128)S(1)} %bitcast.7, bf16[1,4,2048,256]{3,2,1,0:T(8,128)(2,1)S(1)} %copy-done, bf16[1,4,2048]{2,1,0:T(4,128)(2,1)S(1)} %copy-done.2, bf16[1,4,2048]{2,1,0:T(4,128)(2,1)S(1)} %copy-done.3, bf16[1,5,4,2048]{3,2,1,0:T(4,128)(2,1)S(1)} %bitcast.5), custom_call_target="tpu_custom_call" | custom-call | flops 1000 | bytes 1000 | tf_op jit(solution)/shard_map/kept_grams/pallas_call | solution.py:179
  25.0 0.0 collective-permute-done.refs_1_
  25.0 9.3 %root_weights.2 = (bf16[2,256,256]{2,1,0:T(8,128)(2,1)S(1)}, f32[2,264,256]{2,1,0:T(8,128)S(1)}) custom-call(f32[4,264,256]{2,1,0:T(8,128)S(1)} %kept_grams.1.refs_0_, f32[4,264,256]{2,1,0:T(8,128)S(1)} %collective-permute-done.refs_1_, f32[2,264,256]{2,1,0:T(8,128)S(1)} %collective-permute-done.1.refs_2_), custom_call_target="tpu_custom_call" | custom-call | flops 2000000000 | bytes 1000 | tf_op jit(solution)/shard_map/root_weights/pallas_call | solution.py:307
  34.3 8.9 %all-to-all-done.states.refs_3_ = bf16[8,4,32,640]{3,2,1,0:T(8,128)(2,1)S(1)} async-done(((bf16[8,4,32,640]{3,2,1,0:T(8,128)(2,1)}), bf16[8,4,32,640]{3,2,1,0:T(8,128)(2,1)S(1)}, u32[]{:S(2)}, u32[]{:S(2)}) %all-to-all-start) | async-done | bytes 1310752 | tf_op jit(solution)/shard_map/all_to_all | solution.py:399
  43.2 1.6 %apply_weights.1 = bf16[8,2,32,640]{3,2,1,0:T(8,128)(2,1)} custom-call(bf16[2,256,256]{2,1,0:T(8,128)(2,1)S(1)} %get-tuple-element.22.flipped_ref, bf16[8,4,32,640]{3,2,1,0:T(8,128)(2,1)S(1)} %all-to-all-done.states.refs_3_), custom_call_target="tpu_custom_call" | custom-call | flops 1000 | bytes 1000 | tf_op jit(solution)/shard_map/apply_weights/pallas_call | solution.py:335
  44.9 0.0 collective-permute-done.2.refs_1_
  44.9 0.0 collective-permute-done.3.refs_2_
  44.9 3.8 %all-to-all-start.1 = ((bf16[8,2,32,640]{3,2,1,0:T(8,128)(2,1)}), bf16[8,2,32,640]{3,2,1,0:T(8,128)(2,1)S(1)}, u32[]{:S(2)}, u32[]{:S(2)}) async-start(bf16[8,2,32,640]{3,2,1,0:T(8,128)(2,1)} %apply_weights.1), calls=%async_computation.1 | async-start | bytes 1310720 | tf_op jit(solution)/shard_map/all_to_all | solution.py:399
  48.7 10.0 %root_weights.3 = (bf16[2,32,640]{2,1,0:T(8,128)(2,1)S(1)}, bf16[4,32,640]{2,1,0:T(8,128)(2,1)S(1)}, bf16[4,32,640]{2,1,0:T(8,128)(2,1)S(1)}, bf16[2,32,640]{2,1...) custom-call(f32[2,264,256]{2,1,0:T(8,128)S(1)} %get-tuple-element.26.refs_0_, ...), custom_call_target="tpu_custom_call" | custom-call | flops 2000000000 | bytes 1000 | tf_op jit(solution)/shard_map/root_weights/pallas_call | solution.py:307
  58.7 3.9 %collective-permute-start.5 = (bf16[4,32,640]{2,1,0:T(8,128)(2,1)S(1)}, bf16[4,32,640]{2,1,0:T(8,128)(2,1)S(1)}, u32[]{:S(2)}, u32[]{:S(2)}) collective-permute-start(bf16[4,32,640]{2,1,0:T(8,128)(2,1)S(1)} %get-tuple-element.31), channel_id=1, source_target_pairs={{0,192},{32,224},{64,0},{96,32},{128,64},{160,96},{192,128},{224,1... | collective-permute-start | bytes 491528 | tf_op jit(solution)/shard_map/ppermute | solution.py:404
  62.6 0.0 collective-permute-start.4
  62.6 0.9 %collective-permute-start.6 = (bf16[2,32,640]{2,1,0:T(8,128)(2,1)S(1)}, bf16[2,32,640]{2,1,0:T(8,128)(2,1)S(1)}, u32[]{:S(2)}, u32[]{:S(2)}) collective-permute-start(bf16[2,32,640]{2,1,0:T(8,128)(2,1)S(1)} %get-tuple-element.32), channel_id=1, source_target_pairs={{0,32},{32,64},{64,96},{96,128},{128,160},{160,192},{192,224},{224... | collective-permute-start | bytes 245768 | tf_op jit(solution)/shard_map/ppermute | solution.py:404
  63.5 2.4 %collective-permute-start.7 = (bf16[2,32,640]{2,1,0:T(8,128)(2,1)S(1)}, bf16[2,32,640]{2,1,0:T(8,128)(2,1)S(1)}, u32[]{:S(2)}, u32[]{:S(2)}) collective-permute-start(bf16[2,32,640]{2,1,0:T(8,128)(2,1)S(1)} %get-tuple-element.33), channel_id=1, source_target_pairs={{0,224},{32,0},{64,32},{96,64},{128,96},{160,128},{192,160},{224,1... | collective-permute-start | bytes 245768 | tf_op jit(solution)/shard_map/ppermute | solution.py:404
  65.9 4.7 %collective-permute-start.8 = (bf16[2,32,640]{2,1,0:T(8,128)(2,1)S(1)}, bf16[2,32,640]{2,1,0:T(8,128)(2,1)S(1)}, u32[]{:S(2)}, u32[]{:S(2)}) collective-permute-start(bf16[2,32,640]{2,1,0:T(8,128)(2,1)S(1)} %get-tuple-element.34), channel_id=1, source_target_pairs={{0,128},{32,160},{64,192},{96,224},{128,0},{160,32},{192,64},{224,... | collective-permute-start | bytes 245768 | tf_op jit(solution)/shard_map/ppermute | solution.py:404
  70.6 2.8 %collective-permute-done.5.c6 = bf16[4,32,640]{2,1,0:T(8,128)(2,1)S(1)} collective-permute-done((bf16[4,32,640]{2,1,0:T(8,128)(2,1)S(1)}, bf16[4,32,640]{2,1,0:T(8,128)(2,1)S(1)}, u32[]{:S(2)}, u32[]{:S(2)}) %collective-permute-start.5) | collective-permute-done | bytes 163872 | tf_op jit(solution)/shard_map/ppermute | solution.py:404
  73.3 2.6 %collective-permute-start.10 = (bf16[2,32,640]{2,1,0:T(8,128)(2,1)S(1)}, bf16[2,32,640]{2,1,0:T(8,128)(2,1)S(1)}, u32[]{:S(2)}, u32[]{:S(2)}) collective-permute-start(bf16[2,32,640]{2,1,0:T(8,128)(2,1)S(1)} %slice.9), channel_id=1, source_target_pairs={{0,224},{32,0},{64,32},{96,64},{128,96},{160,128},{192,160},{224,1... | collective-permute-start | bytes 245768 | tf_op jit(solution)/shard_map/ppermute | solution.py:404
  75.9 0.4 collective-permute-start.9
  76.3 0.6 collective-permute-done.6.c1
  76.9 0.0 collective-permute-done.7.c7
  76.9 0.0 all-to-all-done.1.first
  76.9 1.1 %gather.1.so_far = bf16[8,4,32,640]{3,2,1,0:T(8,128)(2,1)} custom-call(bf16[8,2,32,640]{3,2,1,0:T(8,128)(2,1)S(1)} %all-to-all-done.1.first, bf16[2,32,640]{2,1,0:T(8,128)(2,1)S(1)} %get-tuple-element.29.c0, bf16[4,32,640]{2,1,0:T(8,128)(2,1)S(1)} %collective-permute-done.4.c2, bf16[4,32,640]{2,1,0:T(8,128)(2,1)S(1)} %collective-permute-done.5.c6, ...), custom_call_target="tpu_custom_call" | custom-call | flops 1000 | bytes 1000 | tf_op jit(solution)/shard_map/gather/pallas_call | solution.py:375
  78.1 3.7 %collective-permute-done.8.c4 = bf16[2,32,640]{2,1,0:T(8,128)(2,1)S(1)} collective-permute-done((bf16[2,32,640]{2,1,0:T(8,128)(2,1)S(1)}, bf16[2,32,640]{2,1,0:T(8,128)(2,1)S(1)}, u32[]{:S(2)}, u32[]{:S(2)}) %collective-permute-start.8) | collective-permute-done | bytes 81952 | tf_op jit(solution)/shard_map/ppermute | solution.py:404
  81.7 0.1 collective-permute-done.9.c3
  81.8 0.7 gather_rest.1
  (13 shorter events, 0.0 us)
Async XLA Ops:
  0.0 8.6 %copy-start.1 = (bf16[1,4,5,2048]{3,1,2,0:T(4,128)(2,1)S(1)}, bf16[1,4,5,2048]{3,1,2,0:T(4,128)(2,1)}, u32[]{:S(2)}) copy-start(bf16[1,4,5,2048]{3,1,2,0:T(4,128)(2,1)} %param.10) | copy-start | bytes 245764
  0.0 8.6 %copy-start.2 = (bf16[1,4,2048]{2,1,0:T(4,128)(2,1)S(1)}, bf16[1,4,2048]{2,1,0:T(4,128)(2,1)}, u32[]{:S(2)}) copy-start(bf16[1,4,2048]{2,1,0:T(4,128)(2,1)} %innov_ref.3) | copy-start | bytes 49156
  0.0 8.6 %copy-start.3 = (bf16[1,4,2048]{2,1,0:T(4,128)(2,1)S(1)}, bf16[1,4,2048]{2,1,0:T(4,128)(2,1)}, u32[]{:S(2)}) copy-start(bf16[1,4,2048]{2,1,0:T(4,128)(2,1)} %prec_ref.3) | copy-start | bytes 49156
  0.0 8.6 %copy-start.4 = (s32[1,4]{1,0:T(1,128)S(1)}, s32[1,4]{1,0:T(1,128)}, u32[]{:S(2)}) copy-start(s32[1,4]{1,0:T(1,128)} %param.11) | copy-start | bytes 52
  0.0 43.2 %all-to-all-start = ((bf16[8,4,32,640]{3,2,1,0:T(8,128)(2,1)}), bf16[8,4,32,640]{3,2,1,0:T(8,128)(2,1)S(1)}, u32[]{:S(2)}, u32[]{:S(2)}) async-start(bf16[8,4,32,640]{3,2,1,0:T(8,128)(2,1)} %bitcast.8), calls=%async_computation | async-start | bytes 2621440 | tf_op jit(solution)/shard_map/all_to_all | solution.py:399
  8.7 2.2 %copy-start = (bf16[1,4,2048,256]{3,2,1,0:T(8,128)(2,1)S(1)}, bf16[1,4,2048,256]{3,2,1,0:T(8,128)(2,1)}, u32[]{:S(2)}) copy-start(bf16[1,4,2048,256]{3,2,1,0:T(8,128)(2,1)} %ens_ref.3) | copy-start | bytes 12582916
  15.9 9.1 %collective-permute-start = (f32[4,264,256]{2,1,0:T(8,128)S(1)}, f32[4,264,256]{2,1,0:T(8,128)S(1)}, u32[]{:S(2)}, u32[]{:S(2)}) collective-permute-start(f32[4,264,256]{2,1,0:T(8,128)S(1)} %get-tuple-element.20), channel_id=1, source_target_pairs={{0,1},{2,3},{4,5},{6,7},{8,9},{10,11},{12,13},{14,15},{16,17},{18,... | collective-permute-start | bytes 3244040 | tf_op jit(solution)/shard_map/ppermute | solution.py:410
  16.0 8.9 %collective-permute-start.1 = (f32[2,264,256]{2,1,0:T(8,128)S(1)}, f32[2,264,256]{2,1,0:T(8,128)S(1)}, u32[]{:S(2)}, u32[]{:S(2)}) collective-permute-start(f32[2,264,256]{2,1,0:T(8,128)S(1)} %get-tuple-element.21), channel_id=1, source_target_pairs={{1,2},{3,4},{5,6},{7,8},{9,10},{11,12},{13,14},{15,16},{17,18},{19... | collective-permute-start | bytes 1622024 | tf_op jit(solution)/shard_map/ppermute | solution.py:410
  16.7 28.2 %collective-permute-start.2 = (f32[1,136,256]{2,1,0:T(8,128)S(1)}, f32[1,136,256]{2,1,0:T(8,128)S(1)}, u32[]{:S(2)}, u32[]{:S(2)}) collective-permute-start(f32[1,136,256]{2,1,0:T(8,128)S(1)} %get-tuple-element.23), channel_id=1, source_target_pairs={{0,32},{32,64},{64,96},{96,128},{128,160},{160,192},{192,224},{224... | collective-permute-start | bytes 417800 | tf_op jit(solution)/shard_map/ppermute | solution.py:404
  18.7 26.2 %collective-permute-start.3 = (f32[1,136,256]{2,1,0:T(8,128)S(1)}, f32[1,136,256]{2,1,0:T(8,128)S(1)}, u32[]{:S(2)}, u32[]{:S(2)}) collective-permute-start(f32[1,136,256]{2,1,0:T(8,128)S(1)} %get-tuple-element.24), channel_id=1, source_target_pairs={{0,224},{32,0},{64,32},{96,64},{128,96},{160,128},{192,160},{224,1... | collective-permute-start | bytes 417800 | tf_op jit(solution)/shard_map/ppermute | solution.py:404
  44.9 32.1 %all-to-all-start.1 = ((bf16[8,2,32,640]{3,2,1,0:T(8,128)(2,1)}), bf16[8,2,32,640]{3,2,1,0:T(8,128)(2,1)S(1)}, u32[]{:S(2)}, u32[]{:S(2)}) async-start(bf16[8,2,32,640]{3,2,1,0:T(8,128)(2,1)} %apply_weights.1), calls=%async_computation.1 | async-start | bytes 1310720 | tf_op jit(solution)/shard_map/all_to_all | solution.py:399
  58.7 14.6 %collective-permute-start.5 = (bf16[4,32,640]{2,1,0:T(8,128)(2,1)S(1)}, bf16[4,32,640]{2,1,0:T(8,128)(2,1)S(1)}, u32[]{:S(2)}, u32[]{:S(2)}) collective-permute-start(bf16[4,32,640]{2,1,0:T(8,128)(2,1)S(1)} %get-tuple-element.31), channel_id=1, source_target_pairs={{0,192},{32,224},{64,0},{96,32},{128,64},{160,96},{192,128},{224,1... | collective-permute-start | bytes 491528 | tf_op jit(solution)/shard_map/ppermute | solution.py:404
  62.6 13.3 %collective-permute-start.4 = (bf16[4,32,640]{2,1,0:T(8,128)(2,1)S(1)}, bf16[4,32,640]{2,1,0:T(8,128)(2,1)S(1)}, u32[]{:S(2)}, u32[]{:S(2)}) collective-permute-start(bf16[4,32,640]{2,1,0:T(8,128)(2,1)S(1)} %get-tuple-element.30), channel_id=1, source_target_pairs={{0,64},{32,96},{64,128},{96,160},{128,192},{160,224},{192,0},{224,... | collective-permute-start | bytes 491528 | tf_op jit(solution)/shard_map/ppermute | solution.py:404
  62.6 14.3 %collective-permute-start.6 = (bf16[2,32,640]{2,1,0:T(8,128)(2,1)S(1)}, bf16[2,32,640]{2,1,0:T(8,128)(2,1)S(1)}, u32[]{:S(2)}, u32[]{:S(2)}) collective-permute-start(bf16[2,32,640]{2,1,0:T(8,128)(2,1)S(1)} %get-tuple-element.32), channel_id=1, source_target_pairs={{0,32},{32,64},{64,96},{96,128},{128,160},{160,192},{192,224},{224... | collective-permute-start | bytes 245768 | tf_op jit(solution)/shard_map/ppermute | solution.py:404
  63.5 13.5 %collective-permute-start.7 = (bf16[2,32,640]{2,1,0:T(8,128)(2,1)S(1)}, bf16[2,32,640]{2,1,0:T(8,128)(2,1)S(1)}, u32[]{:S(2)}, u32[]{:S(2)}) collective-permute-start(bf16[2,32,640]{2,1,0:T(8,128)(2,1)S(1)} %get-tuple-element.33), channel_id=1, source_target_pairs={{0,224},{32,0},{64,32},{96,64},{128,96},{160,128},{192,160},{224,1... | collective-permute-start | bytes 245768 | tf_op jit(solution)/shard_map/ppermute | solution.py:404
  65.9 15.9 %collective-permute-start.8 = (bf16[2,32,640]{2,1,0:T(8,128)(2,1)S(1)}, bf16[2,32,640]{2,1,0:T(8,128)(2,1)S(1)}, u32[]{:S(2)}, u32[]{:S(2)}) collective-permute-start(bf16[2,32,640]{2,1,0:T(8,128)(2,1)S(1)} %get-tuple-element.34), channel_id=1, source_target_pairs={{0,128},{32,160},{64,192},{96,224},{128,0},{160,32},{192,64},{224,... | collective-permute-start | bytes 245768 | tf_op jit(solution)/shard_map/ppermute | solution.py:404
  73.3 8.4 %collective-permute-start.10 = (bf16[2,32,640]{2,1,0:T(8,128)(2,1)S(1)}, bf16[2,32,640]{2,1,0:T(8,128)(2,1)S(1)}, u32[]{:S(2)}, u32[]{:S(2)}) collective-permute-start(bf16[2,32,640]{2,1,0:T(8,128)(2,1)S(1)} %slice.9), channel_id=1, source_target_pairs={{0,224},{32,0},{64,32},{96,64},{128,96},{160,128},{192,160},{224,1... | collective-permute-start | bytes 245768 | tf_op jit(solution)/shard_map/ppermute | solution.py:404
  75.9 5.9 %collective-permute-start.9 = (bf16[2,32,640]{2,1,0:T(8,128)(2,1)S(1)}, bf16[2,32,640]{2,1,0:T(8,128)(2,1)S(1)}, u32[]{:S(2)}, u32[]{:S(2)}) collective-permute-start(bf16[2,32,640]{2,1,0:T(8,128)(2,1)S(1)} %slice.8), channel_id=1, source_target_pairs={{0,32},{32,64},{64,96},{96,128},{128,160},{160,192},{192,224},{224... | collective-permute-start | bytes 245768 | tf_op jit(solution)/shard_map/ppermute | solution.py:404
